TPU v7x, 32 devices: a whole 2x2x4 slice. The times are simulated.
32 devices in a mesh: tile: 8 (over z, x), dp: 4 (over y, core).
Axes of the slice: x: 2, y: 2, z: 4, core: 2. Of those that a mesh axis runs over, the one named last changes fastest.
Arguments:
- features: bfloat16 [512, 256, 128], P('tile'), may hold values from -6 to 6
- target_field: bfloat16 [512, 256], P('tile'), may hold values from -3 to 3
- owner_tile: int32 [128, 1], P(('tile', 'dp')), may hold values from 0 to 7; in each aligned block of 4 rows (0 to 3, 4 to 7, ...) at most 2 rows name the same one
- row_offset: int32 [128], P(('tile', 'dp')), may hold values from 0 to 48
- column_start: int32 [128], P(('tile', 'dp')), may hold values from 0 to 240
- noise_level: int32 [128], P(('tile', 'dp')), may hold values from 0 to 31
- icing_count: int32 [128], P(('tile', 'dp')), may hold values from 1 to 4
- noise_draw: float32 [128, 16, 16], P(('tile', 'dp')), may hold values from -6 to 6
- w_a: bfloat16 [1152, 512], replicated, may hold values from -0.1875 to 0.1875
- w_u: float32 [9, 512], replicated, may hold values from -2 to 2
- b_a: float32 [512], replicated, may hold values from -3 to 3
- e_a: float32 [512], replicated, may hold values from -6 to 6
- w_b: bfloat16 [4608, 128], replicated, may hold values from -0.09375 to 0.09375
- b_b: float32 [128], replicated, may hold values from -3 to 3
- w_o: float32 [128], replicated, may hold values from -0.5 to 0.5
Outputs:
- losses: float32 [128], P(('tile', 'dp'))
- upd_a: float32 [512, 1152], P(('tile', 'dp'))
- upd_b: float32 [512, 1152], P(('tile', 'dp'))
Inputs may be any that keep to these rules, and one draw needn't show every extreme that they name: `owner_tile`: among the 4 patches of one device no tile is named more than 2 times, a bound that some block reaches. `row_offset`: a patch's rows lie inside its tile.
All inputs are finite; a program needn't handle non-finite values.
Results may differ from a plain program's by a relative error of at most 0.0027.
Values may be sent and summed in bfloat16 or wider, within the bound.
No kernel may reach another device: no remote copies, remote signals or barrier semaphores. Data moves between devices by JAX's collectives and lax.ppermute only.
A program may use at most 128 MiB of HBM per device.

v0:
```python
import math

import jax
import jax.numpy as jnp
from jax import lax
from jax.sharding import PartitionSpec as P

C = 128
HID = 512
P_SIZE = 16
LEVELS = 32


SIGMA_LOW = 0.02
SIGMA_HIGH = 80.0
SIGMA_DATA = 0.5
EPSILON = 1e-06


def silu_prime(values):
    sigmoid_val = jax.nn.sigmoid(values)
    return sigmoid_val * (1.0 + values * (1.0 - sigmoid_val))


def tap_window(padded, shift_row, shift_col, side_len):
    window = padded[:, shift_row : shift_row + side_len, shift_col : shift_col + side_len]
    return window.reshape((-1,) + padded.shape[3:])


def patch_terms(
    patch_feats,
    patch_target,
    noise_draw,
    noise_level,
    icing_count,
    w_a,
    w_u,
    b_a,
    e_a,
    w_b,
    b_b,
    w_o,
):
    npatch = patch_feats.shape[0]
    side_len = patch_feats.shape[1]
    channels = patch_feats.shape[3]
    hidden_width = w_a.shape[1]
    pixels = side_len * side_len
    log_step = (math.log(SIGMA_HIGH) - math.log(SIGMA_LOW)) / (LEVELS - 1)
    sigmas = jnp.exp(math.log(SIGMA_LOW) + noise_level.astype(jnp.float32) * log_step)
    variance = sigmas * sigmas + SIGMA_DATA * SIGMA_DATA
    scale_in = 1.0 / jnp.sqrt(variance)
    scale_skip = SIGMA_DATA * SIGMA_DATA / variance
    scale_out = sigmas * SIGMA_DATA * scale_in
    noise_embed = jnp.log(sigmas) / 4.0
    clean_field = patch_target.astype(jnp.float32)
    noisy_field = clean_field + sigmas[:, None, None] * noise_draw
    aim_value = (
        (clean_field - scale_skip[:, None, None] * noisy_field) / scale_out[:, None, None]
    ).reshape(-1)
    scaled_in = jnp.pad(scale_in[:, None, None] * noisy_field, ((0, 0), (1, 1), (1, 1)))
    feat_pad = jnp.pad(patch_feats, ((0, 0), (1, 1), (1, 1), (0, 0)))
    embed_rows = jnp.repeat(noise_embed, pixels)
    pre_a = b_a[None, :] + embed_rows[:, None] * e_a[None, :]
    for tap_index in range(9):
        shift_row, shift_col = (tap_index // 3, tap_index % 3)
        window = tap_window(feat_pad, shift_row, shift_col, side_len)
        pre_a = pre_a + jnp.dot(
            window,
            w_a[tap_index * channels : (tap_index + 1) * channels],
            preferred_element_type=jnp.float32,
        )
        pre_a = (
            pre_a
            + tap_window(scaled_in, shift_row, shift_col, side_len)[:, None]
            * w_u[tap_index][None, :]
        )
    hidden_act = jax.nn.silu(pre_a).astype(jnp.bfloat16)
    act_pad = jnp.pad(
        hidden_act.reshape(npatch, side_len, side_len, hidden_width),
        ((0, 0), (1, 1), (1, 1), (0, 0)),
    )
    pre_b = jnp.zeros((npatch * pixels, channels), jnp.float32) + b_b[None, :]
    for tap_index in range(9):
        shift_row, shift_col = (tap_index // 3, tap_index % 3)
        window = tap_window(act_pad, shift_row, shift_col, side_len)
        pre_b = pre_b + jnp.dot(
            window,
            w_b[tap_index * hidden_width : (tap_index + 1) * hidden_width],
            preferred_element_type=jnp.float32,
        )
    out_act = jax.nn.silu(pre_b)
    output_map = jnp.dot(out_act, w_o, precision=lax.Precision.HIGHEST)
    residual = output_map - aim_value
    weights = jnp.repeat(icing_count.astype(jnp.float32), pixels)
    losses = jnp.mean((weights * residual * residual).reshape(npatch, pixels), axis=1)
    grad_final = 2.0 * weights * residual / pixels
    grad_pre_b = (grad_final[:, None] * w_o[None, :] * silu_prime(pre_b)).astype(jnp.bfloat16)
    grad_hidden = jnp.zeros((npatch, side_len + 2, side_len + 2, hidden_width), jnp.float32)
    parts_b = []
    for tap_index in range(9):
        shift_row, shift_col = (tap_index // 3, tap_index % 3)
        window = tap_window(act_pad, shift_row, shift_col, side_len)
        parts_b.append(
            lax.dot_general(
                window, grad_pre_b, (((0,), (0,)), ((), ())), preferred_element_type=jnp.float32
            )
        )
        back_term = lax.dot_general(
            grad_pre_b,
            w_b[tap_index * hidden_width : (tap_index + 1) * hidden_width],
            (((1,), (1,)), ((), ())),
            preferred_element_type=jnp.float32,
        )
        grad_hidden = grad_hidden.at[
            :, shift_row : shift_row + side_len, shift_col : shift_col + side_len
        ].add(back_term.reshape(npatch, side_len, side_len, hidden_width))
    grad_pre_a = (grad_hidden[:, 1:-1, 1:-1].reshape(-1, hidden_width) * silu_prime(pre_a)).astype(
        jnp.bfloat16
    )
    parts_a = []
    for tap_index in range(9):
        shift_row, shift_col = (tap_index // 3, tap_index % 3)
        window = tap_window(feat_pad, shift_row, shift_col, side_len)
        parts_a.append(
            lax.dot_general(
                grad_pre_a, window, (((0,), (0,)), ((), ())), preferred_element_type=jnp.float32
            )
        )
    return (losses, jnp.concatenate(parts_a, axis=1), jnp.concatenate(parts_b, axis=1))


def local(
    features,
    target_field,
    owner_tile,
    row_offset,
    column_start,
    noise_level,
    icing_count,
    noise_draw,
    w_a,
    w_u,
    b_a,
    e_a,
    w_b,
    b_b,
    w_o,
):
    tile_count = lax.axis_size("tile")
    npatch = owner_tile.shape[0]
    slot_cap = max(2, 2 * npatch // tile_count)
    slot_total = tile_count * slot_cap
    owner_index = owner_tile[:, 0]
    position = jnp.arange(npatch, dtype=jnp.int32)
    same_owner = (owner_index[None, :] == owner_index[:, None]) & (
        position[None, :] < position[:, None]
    )
    slot_rank = jnp.sum(same_owner.astype(jnp.int32), axis=1)
    slot_key = owner_index * slot_cap + slot_rank
    selector = (slot_key[None, :] == jnp.arange(slot_total, dtype=jnp.int32)[:, None]).astype(
        jnp.int32
    )

    def extract(source_row, source_col):
        anchor = jnp.zeros((), jnp.int32)
        feat_block = lax.dynamic_slice(
            features, (source_row, source_col, anchor), (P_SIZE, P_SIZE, C)
        )
        target_block = lax.dynamic_slice(target_field, (source_row, source_col), (P_SIZE, P_SIZE))
        return (feat_block, target_block)

    wanted = jnp.stack([row_offset, column_start], axis=1)
    request_table = jnp.sum(selector[:, :, None] * wanted[None, :, :], axis=1).reshape(
        tile_count, slot_cap, 2
    )
    request = lax.all_to_all(request_table, "tile", split_axis=0, concat_axis=0, tiled=True)
    slot_width = request.shape[1]
    flat_table = request.reshape(-1, 2)
    blocks, fields = jax.vmap(extract)(flat_table[:, 0], flat_table[:, 1])
    blocks = blocks.reshape(tile_count, slot_width, P_SIZE, P_SIZE, C)
    fields = fields.reshape(tile_count, slot_width, P_SIZE, P_SIZE)
    fetched = lax.all_to_all(blocks, "tile", split_axis=0, concat_axis=0, tiled=True)
    fetched_target = lax.all_to_all(fields, "tile", split_axis=0, concat_axis=0, tiled=True)
    patch_feats = fetched.reshape(slot_total, P_SIZE, P_SIZE, C)[slot_key]
    patch_target = fetched_target.reshape(slot_total, P_SIZE, P_SIZE)[slot_key]
    losses, grad_a, grad_b = patch_terms(
        patch_feats,
        patch_target,
        noise_draw,
        noise_level,
        icing_count,
        w_a,
        w_u,
        b_a,
        e_a,
        w_b,
        b_b,
        w_o,
    )
    combined = jnp.concatenate([grad_a, grad_b], axis=1)
    owned_rows = lax.psum_scatter(combined, ("tile", "dp"), scatter_dimension=0, tiled=True)
    tap_width = 9 * C
    shard_a = owned_rows[:, :tap_width]
    shard_b = owned_rows[:, tap_width:]
    squares = lax.psum((jnp.sum(shard_a * shard_a), jnp.sum(shard_b * shard_b)), ("tile", "dp"))
    count_all = HID * tap_width
    upd_a = shard_a / jnp.sqrt(squares[0] / count_all + EPSILON)
    upd_b = shard_b / jnp.sqrt(squares[1] / count_all + EPSILON)
    return (losses, upd_a, upd_b)


def solution(mesh):
    return jax.shard_map(
        local,
        mesh=mesh,
        in_specs=(
            P("tile", None, None),
            P("tile", None),
            P(("tile", "dp"), None),
            P(("tile", "dp")),
            P(("tile", "dp")),
            P(("tile", "dp")),
            P(("tile", "dp")),
            P(("tile", "dp"), None, None),
            P(),
            P(),
            P(),
            P(),
            P(),
            P(),
            P(),
        ),
        out_specs=(P(("tile", "dp")), P(("tile", "dp"), None), P(("tile", "dp"), None)),
        check_vma=False,
    )
```

profile of v0, /device:TPU:0, one launch (start us, length us, event | category | flops | bytes accessed | tf_op | source)
XLA Modules:
  0.0 457.4 jit_solution(10374857467849213329)
XLA Ops:
  10.4 7.3 %all-to-all-start = ((s32[8,2,2]{1,2,0:T(2,128)}), s32[8,2,2]{1,2,0:T(2,128)S(1)}, u32[]{:S(2)}, u32[]{:S(2)}) async-start(s32[8,2,2]{1,2,0:T(2,128)} %copy.29), calls=%async_computation | async-start | bytes 16384 | tf_op jit(solution)/shard_map/all_to_all | solution.py:177
  18.3 5.8 %all-to-all-done = s32[8,2,2]{1,2,0:T(2,128)S(1)} async-done(((s32[8,2,2]{1,2,0:T(2,128)}), s32[8,2,2]{1,2,0:T(2,128)S(1)}, u32[]{:S(2)}, u32[]{:S(2)}) %all-to-all-start) | async-done | bytes 160 | tf_op jit(solution)/shard_map/all_to_all | solution.py:177
  24.2 43.5 %while.12 = (s32[]{:T(128)}, bf16[64,256]{1,0:T(8,128)(2,1)}, s32[16,2]{0,1:T(2,128)S(1)}, bf16[16,16,16]{2,1,0:T(8,128)(2,1)S(1)}, s32[]{:T(128)}) while((s32[]{:T(128)}, bf16[64,256]{1,0:T(8,128)(2,1)}, s32[16,2]{0,1:T(2,128)S(1)}, bf16[16,16,16]{2,1,0:T(8,128)(2,1)S(1)}, s32[]{:T(128)}) %tuple.117), condition=%wide.while_cond.10, body=%wide.while_body.10.sunk | while | flops 2 | bytes 4717 | solution.py:170
  27.6 2.1 bitcast_dynamic-update-slice_fusion.5
  30.3 2.1 bitcast_dynamic-update-slice_fusion.5
  33.0 2.1 bitcast_dynamic-update-slice_fusion.5
  38.5 2.1 bitcast_dynamic-update-slice_fusion.5
  41.2 2.1 bitcast_dynamic-update-slice_fusion.5
  43.9 2.1 bitcast_dynamic-update-slice_fusion.5
  46.6 2.1 bitcast_dynamic-update-slice_fusion.5
  68.5 3.3 all-to-all-start.2
  71.8 55.6 %while.11 = (s32[]{:T(128)}, bf16[64,256,128]{2,1,0:T(8,128)(2,1)}, s32[16,3]{0,1:T(4,128)S(1)}, bf16[16,16,16,128]{3,2,1,0:T(8,128)(2,1)}, s32[]{:T(128)}) while((s32[]{:T(128)}, bf16[64,256,128]{2,1,0:T(8,128)(2,1)}, s32[16,3]{0,1:T(4,128)S(1)}, bf16[16,16,16,128]{3,2,1,0:T(8,128)(2,1)}, s32[]{:T(128)}) %tuple.120), condition=%wide.while_cond.9, body=%wide.while_body.9.sunk | while | flops 2 | bytes 132713 | solution.py:167
  72.5 2.8 bitcast_dynamic-update-slice_fusion.4
  76.0 2.8 bitcast_dynamic-update-slice_fusion.4
  79.5 2.8 bitcast_dynamic-update-slice_fusion.4
  82.9 2.8 bitcast_dynamic-update-slice_fusion.4
  86.4 2.8 bitcast_dynamic-update-slice_fusion.4
  89.9 2.8 bitcast_dynamic-update-slice_fusion.4
  93.4 2.8 bitcast_dynamic-update-slice_fusion.4
  96.8 2.8 bitcast_dynamic-update-slice_fusion.4
  100.3 2.8 bitcast_dynamic-update-slice_fusion.4
  103.8 2.8 bitcast_dynamic-update-slice_fusion.4
  107.2 2.8 bitcast_dynamic-update-slice_fusion.4
  110.7 2.8 bitcast_dynamic-update-slice_fusion.4
  114.2 2.8 bitcast_dynamic-update-slice_fusion.4
  117.7 2.8 bitcast_dynamic-update-slice_fusion.4
  121.1 2.8 bitcast_dynamic-update-slice_fusion.4
  124.6 2.8 bitcast_dynamic-update-slice_fusion.4
  127.4 5.9 %all-to-all-start.1 = ((bf16[8,2,16,16,128]{4,3,2,1,0:T(8,128)(2,1)}), bf16[8,2,16,16,128]{4,3,2,1,0:T(8,128)(2,1)S(1)}, u32[]{:S(2)}, u32[]{:S(2)}) async-start(bf16[8,2,16,16,128]{4,3,2,1,0:T(8,128)(2,1)} %bitcast.3), calls=%async_computation.1 | async-start | bytes 2097152 | tf_op jit(solution)/shard_map/all_to_all | solution.py:183
  137.2 20.4 %all-to-all-done.1 = bf16[8,2,16,16,128]{4,3,2,1,0:T(8,128)(2,1)S(1)} async-done(((bf16[8,2,16,16,128]{4,3,2,1,0:T(8,128)(2,1)}), bf16[8,2,16,16,128]{4,3,2,1,0:T(8,128)(2,1)S(1)}, u32[]{:S(2)}, u32[]{:S(2)}) %all-to-all-start.1) | async-done | bytes 1048608 | tf_op jit(solution)/shard_map/all_to_all | solution.py:183
  162.1 4.6 %multiply_convert_fusion = (bf16[1024,512]{1,0:T(8,128)(2,1)S(1)}, f32[1024,512]{1,0:T(8,128)}) fusion(f32[512]{0:T(512)S(1)} %bitcast.214, f32[1024]{0:T(1024)S(1)} %mul.342, bf16[1024,128]{1,0:T(8,128)(2,1)S(1)} %bitcast.200, bf16[1152,512]{1,0:T(8,128)(2,1)S(1)} %copy-done.42, f32[512]{0:T(512)S(1)} %bitcast.215, f32[1024]{0:T(1024)S(1)} %mul.337, ...), kind=kOutput, calls=%fused_computation.26 | convolution fusion | flops 152043520 | bytes 20379648 | tf_op jit(solution)/shard_map/dot_general | solution.py:68
  166.8 2.7 pad_slice_fusion
  188.3 3.2 dynamic-slice_add_fusion
  191.4 10.5 %scatter-add.31 = f32[4,18,18,512]{3,2,1,0:T(8,128)S(1)} dynamic-update-slice(f32[4,18,18,512]{3,2,1,0:T(8,128)S(1)} %scatter-add.30, f32[4,16,16,512]{3,2,1,0:T(8,128)} %dynamic-slice_add_fusion, s32[]{:T(128)} %constant.298.clone.1, s32[]{:T(128)} %bitcast.39, s32[]{:T(128)} %bitcast.40, s32[]{:T(128)} %constant.298.clone.1) | dynamic-update-slice | bytes 4194308 | tf_op jit(solution)/shard_map/scatter-add | solution.py:117
  202.0 5.6 %add_select_fusion = f32[4,16,16,512]{3,2,1,0:T(8,128)} fusion(f32[4,16,16,512]{3,2,1,0:T(8,128)} %bitcast.181, f32[4,18,18,512]{3,2,1,0:T(8,128)S(1)} %scatter-add.31, s32[]{:T(128)} %bitcast.42, s32[]{:T(128)} %bitcast.43, pred[]{:T(512)} %and_reduce_fusion), kind=kLoop, calls=%fused_computation.6 | loop fusion | flops 1048576 | bytes 6291465 | tf_op jit(solution)/shard_map/select.11
  207.5 10.7 %scatter-add.34 = f32[4,18,18,512]{3,2,1,0:T(8,128)S(1)} dynamic-update-slice(f32[4,18,18,512]{3,2,1,0:T(8,128)S(1)} %scatter-add.31, f32[4,16,16,512]{3,2,1,0:T(8,128)} %add_select_fusion, s32[]{:T(128)} %constant.298.clone.1, s32[]{:T(128)} %bitcast.42, s32[]{:T(128)} %bitcast.43, s32[]{:T(128)} %constant.298.clone.1) | dynamic-update-slice | bytes 4194308 | tf_op jit(solution)/shard_map/scatter-add | solution.py:117
  218.3 2.3 fusion.1
  220.6 2.1 slice_add_fusion.4
  222.7 9.2 %scatter-add.36 = f32[4,18,18,512]{3,2,1,0:T(8,128)S(1)} dynamic-update-slice(f32[4,18,18,512]{3,2,1,0:T(8,128)S(1)} %fusion.1, f32[4,16,16,512]{3,2,1,0:T(8,128)} %slice_add_fusion.4, s32[]{:T(128)} %constant.298.clone.1, s32[]{:T(128)} %constant.311.clone.1, s32[]{:T(128)} %constant.311.clone.1, s32[]{:T(128)} %constant.298.clone.1) | dynamic-update-slice | bytes 4194308 | tf_op jit(solution)/shard_map/scatter-add | solution.py:117
  231.9 3.7 slice_add_fusion.3
  235.6 9.2 %scatter-add.39 = f32[4,18,18,512]{3,2,1,0:T(8,128)S(1)} dynamic-update-slice(f32[4,18,18,512]{3,2,1,0:T(8,128)S(1)} %scatter-add.36, f32[4,16,16,512]{3,2,1,0:T(8,128)} %slice_add_fusion.3, s32[]{:T(128)} %constant.298.clone.1, s32[]{:T(128)} %constant.311.clone.1, s32[]{:T(128)} %constant.297.clone.1, s32[]{:T(128)} %constant.298.clone.1) | dynamic-update-slice | bytes 4194308 | tf_op jit(solution)/shard_map/scatter-add | solution.py:117
  244.8 2.3 fusion
  249.1 9.2 %scatter-add.41 = f32[4,18,18,512]{3,2,1,0:T(8,128)S(1)} dynamic-update-slice(f32[4,18,18,512]{3,2,1,0:T(8,128)S(1)} %fusion, f32[4,16,16,512]{3,2,1,0:T(8,128)} %slice_add_fusion.1, s32[]{:T(128)} %constant.298.clone.1, s32[]{:T(128)} %constant.297.clone.1, s32[]{:T(128)} %constant.311.clone.1, s32[]{:T(128)} %constant.298.clone.1) | dynamic-update-slice | bytes 4194308 | tf_op jit(solution)/shard_map/scatter-add | solution.py:117
  258.3 3.6 slice_add_fusion
  262.0 9.2 %scatter-add.44 = f32[4,18,18,512]{3,2,1,0:T(8,128)S(1)} dynamic-update-slice(f32[4,18,18,512]{3,2,1,0:T(8,128)S(1)} %scatter-add.41, f32[4,16,16,512]{3,2,1,0:T(8,128)} %slice_add_fusion, s32[]{:T(128)} %constant.298.clone.1, s32[]{:T(128)} %constant.297.clone.1, s32[]{:T(128)} %constant.297.clone.1, s32[]{:T(128)} %constant.298.clone.1) | dynamic-update-slice | bytes 4194308 | tf_op jit(solution)/shard_map/scatter-add | solution.py:117
  292.8 6.1 %copy.33 = f32[512,2304]{1,0:T(8,128)} copy(f32[512,2304]{0,1:T(8,128)} %convolution_dynamic-update-slice_fusion) | data formatting | bytes 9437184
  299.6 105.4 %reduce-scatter.4.cloned.1.call-done = f32[16,2304]{1,0:T(8,128)} async-done(((f32[512,2304]{1,0:T(8,128)}), f32[16,2304]{1,0:T(8,128)}) %reduce-scatter.4.cloned.1.call-update) | async-done | bytes 147472
  407.2 40.2 %all-reduce.4 = (f32[]{:T(128)}, f32[]{:T(128)}) all-reduce(f32[]{:T(128)} %get-tuple-element.214, f32[]{:T(128)} %get-tuple-element.213), channel_id=1, replica_groups=mesh['tile'=8,'dp'=4] {'tile','dp'}, use_global_device_ids=true, to_apply=%region_6.7 | all-reduce | flops 2 | bytes 16 | tf_op jit(solution)/shard_map/psum | solution.py:206
  (289 shorter events, 98.9 us)
Async XLA Ops:
  7.2 127.6 %copy-start.46 = (s32[4]{0:T(128)S(1)}, s32[4]{0:T(128)}, u32[]{:S(2)}) copy-start(s32[4]{0:T(128)} %constant.309.clone.1) | copy-start | bytes 52
  7.2 126.4 %copy-start.51 = (s32[4,1]{0,1:T(1,128)S(1)}, s32[4,1]{0,1:T(1,128)}, u32[]{:S(2)}) copy-start(s32[4,1]{0,1:T(1,128)} %param.35) | copy-start | bytes 52
  7.2 126.3 %copy-start.50 = (s32[4]{0:T(128)S(1)}, s32[4]{0:T(128)}, u32[]{:S(2)}) copy-start(s32[4]{0:T(128)} %param.39) | copy-start | bytes 52
  7.2 128.3 %copy-start.44 = (f32[9,512]{1,0:T(8,128)S(1)}, f32[9,512]{1,0:T(8,128)}, u32[]{:S(2)}) copy-start(f32[9,512]{1,0:T(8,128)} %param.42) | copy-start | bytes 55300
  7.2 129.0 %copy-start.43 = (f32[4,16,16]{2,1,0:T(8,128)S(1)}, f32[4,16,16]{2,1,0:T(8,128)}, u32[]{:S(2)}) copy-start(f32[4,16,16]{2,1,0:T(8,128)} %param.40) | copy-start | bytes 12292
  10.4 13.8 %all-to-all-start = ((s32[8,2,2]{1,2,0:T(2,128)}), s32[8,2,2]{1,2,0:T(2,128)S(1)}, u32[]{:S(2)}, u32[]{:S(2)}) async-start(s32[8,2,2]{1,2,0:T(2,128)} %copy.29), calls=%async_computation | async-start | bytes 16384 | tf_op jit(solution)/shard_map/all_to_all | solution.py:177
  68.5 59.0 %all-to-all-start.2 = ((bf16[8,2,256]{2,1,0:T(2,128)(2,1)}), bf16[8,2,256]{2,1,0:T(2,128)(2,1)S(1)}, u32[]{:S(2)}, u32[]{:S(2)}) async-start(bf16[8,2,256]{2,1,0:T(2,128)(2,1)} %reshape.648), calls=%async_computation.2 | async-start | bytes 16384 | tf_op jit(solution)/shard_map/all_to_all | solution.py:184
  127.4 30.2 %all-to-all-start.1 = ((bf16[8,2,16,16,128]{4,3,2,1,0:T(8,128)(2,1)}), bf16[8,2,16,16,128]{4,3,2,1,0:T(8,128)(2,1)S(1)}, u32[]{:S(2)}, u32[]{:S(2)}) async-start(bf16[8,2,16,16,128]{4,3,2,1,0:T(8,128)(2,1)} %bitcast.3), calls=%async_computation.1 | async-start | bytes 2097152 | tf_op jit(solution)/shard_map/all_to_all | solution.py:183
  133.3 25.3 %copy-start.42 = (bf16[1152,512]{1,0:T(8,128)(2,1)S(1)}, bf16[1152,512]{1,0:T(8,128)(2,1)}, u32[]{:S(2)}) copy-start(bf16[1152,512]{1,0:T(8,128)(2,1)} %param.41) | copy-start | bytes 3538948
  133.3 271.6 %reduce-scatter.4.cloned.1.call-start = ((), (), s32[]{:S(2)}) async-start(), calls=%async_computation.4 | async-start | bytes 4866048
  158.2 3.4 copy-start.23
  158.6 1.8 copy-start.37
  158.6 2.2 copy-start.25
  158.6 2.6 copy-start.27
  158.6 3.5 copy-start.40
  166.8 4.6 copy-start.4
  166.8 2.8 copy-start.22
  166.8 2.8 copy-start.45
  169.5 1.4 copy-start.2
  169.5 2.3 copy-start.12
  169.5 2.7 copy-start.14
  169.5 2.7 copy-start.16
  169.5 2.7 copy-start.18
  169.5 2.7 copy-start.10
  169.5 3.2 copy-start.8
  169.5 3.6 copy-start.6
  174.5 11.6 %copy-start = (bf16[1024,128]{1,0:T(8,128)(2,1)}, bf16[1024,128]{1,0:T(8,128)(2,1)S(1)}, u32[]{:S(2)}) copy-start(bf16[1024,128]{1,0:T(8,128)(2,1)S(1)} %multiply_convert_fusion.1) | copy-start | bytes 786436
  218.3 2.3 copy-start.21
  244.8 2.3 copy-start.20
  271.2 1.6 copy-start.39
  272.8 2.0 copy-start.36
  273.7 2.1 copy-start.34
  273.7 3.2 copy-start.32
  274.8 3.2 copy-start.24
  275.9 3.2 copy-start.30
  276.9 3.2 copy-start.28
  278.0 3.2 copy-start.26
  279.0 3.2 copy-start.41
  280.1 3.2 copy-start.1
  280.1 3.2 copy-start.3
  281.2 3.2 copy-start.19
  282.2 3.2 copy-start.17
  283.3 3.2 copy-start.15
  284.4 3.1 copy-start.5
  285.4 3.1 copy-start.13
  286.5 3.2 copy-start.11
  287.5 3.2 copy-start.9
  288.5 3.2 copy-start.7
  (8 other events, 7.7 us)
Sparse Core Ops, SparseCore 0:
  299.1 105.8 reduce-scatter.3
where the time goes:
time: 461 us; the launch traced here: 457 us
  local copies, waits for them, and re-layouts  177 us (38%)
  waiting for transfers between devices  132 us (29%)
  matrix products  44.8 us (10%)
  blocking collectives  40.2 us (9%)
  other arithmetic  31.3 us (7%)
  starting transfers between devices  16.5 us (4%)
  between operations  16.2 us (4%)
    unnamed x2, waiting for transfers between devices  105 us
    gather x96, local copies, waits for them, and re-layouts  99 us
    scatter-add x7, local copies, waits for them, and re-layouts, patch_terms(): grad_hidden = grad_hidden.at[:, shift_row:shift_row + side_len, shift_col...  58.4 us
    psum x1, blocking collectives, local(): lax.psum((jnp.sum(shard_a * shard_a), jnp.sum(shard_b * shard_b)), ('tile...  40.2 us
    all_to_all x1, waiting for transfers between devices, local(): lax.all_to_all(blocks, 'tile', split_axis=0, concat_axis=0, tiled=True)  20.4 us
    add x5, other arithmetic, patch_terms(): grad_hidden = grad_hidden.at[:, shift_row:shift_row + side_len, shift_col...  14.6 us
    dot_general x9, matrix products, patch_terms(): lax.dot_general(grad_pre_b, w_b[tap_index * hidden_width:(tap_index + 1)...  13.4 us
    unnamed x115, local copies, waits for them, and re-layouts  10.8 us
  transfers between devices with their start and end apart: 4, of which 3 were waited for; matrix products, arithmetic and copies ran while one was open for 13% of the time, Pallas kernels for 0%

commit v1 on v0

v1 whole, which is shorter than its diff:
```python
import functools
import math

import jax
import jax.numpy as jnp
from jax import lax
from jax.experimental import pallas as pl
from jax.experimental.pallas import tpu as pltpu
from jax.sharding import PartitionSpec as P

C = 128
HID = 512
P_SIZE = 16
LEVELS = 32
CELLS = P_SIZE * P_SIZE
SPAN = 32
FIELDS = 8
GROUP = 2

SIGMA_LOW = 0.02
SIGMA_HIGH = 80.0
SIGMA_DATA = 0.5
EPSILON = 1e-06
AXES = ("tile", "dp")
BF16 = jnp.bfloat16
F32 = jnp.float32


def sigmoid(values):
    return 0.5 * jnp.tanh(0.5 * values) + 0.5


def from_previous_column(x, col):
    return jnp.where(col == 0, 0.0, pltpu.roll(x, 1, 0))


def from_next_column(x, col):
    return jnp.where(col == P_SIZE - 1, 0.0, pltpu.roll(x, x.shape[0] - 1, 0))


def from_previous_row(x):
    zero = jnp.zeros((P_SIZE, x.shape[1]), x.dtype)
    parts = []
    for at in range(0, x.shape[0], CELLS):
        parts += [zero, x[at : at + CELLS - P_SIZE]]
    return jnp.concatenate(parts, axis=0)


def from_next_row(x):
    zero = jnp.zeros((P_SIZE, x.shape[1]), x.dtype)
    parts = []
    for at in range(0, x.shape[0], CELLS):
        parts += [x[at + P_SIZE : at + CELLS], zero]
    return jnp.concatenate(parts, axis=0)


def store_window(ref, base, tap, rows):
    lanes = pl.ds(tap * C, C)
    shift = tap // 3
    if shift == 0:
        ref[base + P_SIZE : base + CELLS, lanes] = rows[: CELLS - P_SIZE]
    elif shift == 1:
        ref[base : base + CELLS, lanes] = rows
    else:
        ref[base : base + CELLS - P_SIZE, lanes] = rows[P_SIZE:]


def train_kernel(
    dp_count,
    npatch,
    place,
    table_hbm,
    table,
    features,
    target,
    w_a,
    w_u,
    b_a,
    e_a,
    w_b,
    b_b,
    w_o,
    keep_out,
    send_out,
    loss_out,
    ints,
    chosen,
    blocks,
    target32,
    extra32,
    weight_a,
    weight_b,
    win_a,
    act,
    win_g,
    slope,
    aim,
    grad_a,
    grad_b,
    int_sem,
    weight_sems,
    block_sems,
):
    devices = table.shape[0]
    slots = blocks.shape[0]
    taps = 9
    my_tile, my_dp = place[0], place[1]

    copy_ints = pltpu.make_async_copy(table_hbm.at[:, 0, pl.ds(npatch * CELLS, C)], ints, int_sem)
    copy_ints.start()
    copies = [pltpu.make_async_copy(w_a, weight_a.at[pl.ds(0, taps * C)], weight_sems.at[taps])]
    for tap in range(taps):
        copies.append(
            pltpu.make_async_copy(
                w_b.at[pl.ds(tap * HID, HID)],
                weight_b.at[:, pl.ds(tap * C, C)],
                weight_sems.at[tap],
            )
        )
    for copy in copies:
        copy.start()
    copy_ints.wait()

    tile_name = my_tile.astype(F32)

    def choose(device, carry):
        turn, place_at = carry
        for patch in range(npatch):
            owned = ints[device, patch * FIELDS] == tile_name
            mine = jnp.logical_and(owned, turn == my_dp)
            chosen[jnp.where(mine, place_at, slots)] = device * npatch + patch
            place_at = jnp.where(mine, place_at + 1, place_at)
            following = jnp.where(turn == dp_count - 1, 0, turn + 1)
            turn = jnp.where(owned, following, turn)
        return turn, place_at

    _, count = lax.fori_loop(0, devices, choose, (jnp.int32(0), jnp.int32(0)))

    def fields(slot):
        patch = chosen[slot]
        device = lax.div(patch, npatch)
        inner = lax.rem(patch, npatch)
        return device, inner

    def block_copy(slot):
        device, inner = fields(slot)
        row = ints[device, inner * FIELDS + 1].astype(jnp.int32)
        column = ints[device, inner * FIELDS + 2].astype(jnp.int32)
        most = (features.shape[1] - SPAN) // 16
        start = jnp.minimum(lax.shift_right_logical(column, 4), most) * 16
        start = pl.multiple_of(start, 16)
        copy = pltpu.make_async_copy(
            features.at[pl.ds(row, P_SIZE), pl.ds(start, SPAN)],
            blocks.at[slot],
            block_sems.at[slot],
        )
        return copy, row, column, column - start

    def start_block(slot, carry):
        block_copy(slot)[0].start()
        return carry

    lax.fori_loop(0, count, start_block, 0)

    grad_a[...] = jnp.zeros_like(grad_a)
    grad_b[...] = jnp.zeros_like(grad_b)
    loss_out[...] = jnp.zeros_like(loss_out)
    edge = jnp.zeros((P_SIZE, 3 * C), BF16)
    for part in range(GROUP):
        base = part * CELLS
        for ref in (win_a, win_g):
            ref[base : base + P_SIZE, : 3 * C] = edge
            ref[base + CELLS - P_SIZE : base + CELLS, 6 * C : 9 * C] = edge
    target32[...] = target[...].astype(F32)

    def high(value):
        return value.astype(BF16).astype(F32)

    extra32[...] = jnp.zeros_like(extra32)
    w_u_value, b_a_value, e_a_value = w_u[...], b_a[...], e_a[...]
    extra32[0:taps] = high(w_u_value)
    extra32[taps : 2 * taps] = w_u_value - high(w_u_value)
    extra32[2 * taps : 3 * taps] = high(w_u_value)
    extra32[27:28] = high(b_a_value)
    extra32[28:29] = b_a_value - high(b_a_value)
    extra32[29:30] = high(e_a_value)
    extra32[30:31] = e_a_value - high(e_a_value)
    extra32[31:32] = high(e_a_value)
    weight_a[taps * C :] = extra32[...].astype(BF16)
    for copy in copies:
        copy.wait()

    cell_col = lax.broadcasted_iota(jnp.int32, (CELLS, C), 0) & (P_SIZE - 1)
    lane = lax.broadcasted_iota(jnp.int32, (CELLS, C), 1)
    lane_tap = lax.rem(lane, taps)
    lane_row, lane_col = lax.div(lane_tap, 3), lax.rem(lane_tap, 3)
    pick_shape = (P_SIZE, P_SIZE, C)
    pick_row = lax.broadcasted_iota(jnp.int32, pick_shape, 0) & 7
    pick_col = lax.broadcasted_iota(jnp.int32, pick_shape, 1)
    pick_lane = lax.broadcasted_iota(jnp.int32, pick_shape, 2)
    noise_pick = pick_lane == pick_row * P_SIZE + pick_col
    field_shape = (P_SIZE, P_SIZE, target.shape[1])
    field_col = lax.broadcasted_iota(jnp.int32, field_shape, 1)
    field_lane = lax.broadcasted_iota(jnp.int32, field_shape, 2)
    loss_row = lax.broadcasted_iota(jnp.int32, loss_out.shape, 0)
    loss_lane = lax.broadcasted_iota(jnp.int32, loss_out.shape, 1)
    both_col = lax.broadcasted_iota(jnp.int32, (GROUP * CELLS, C), 0) & (P_SIZE - 1)
    log_step = (math.log(SIGMA_HIGH) - math.log(SIGMA_LOW)) / (LEVELS - 1)

    def prepare(part, slot):
        base = part * CELLS
        copy, row, _, offset = block_copy(slot)
        device, inner = fields(slot)
        column = ints[device, inner * FIELDS + 2].astype(jnp.int32)
        level = ints[device, inner * FIELDS + 3]

        span = blocks[slot].astype(F32).reshape(P_SIZE * SPAN, C)
        span = pltpu.roll(span, (P_SIZE * SPAN - offset) & (P_SIZE * SPAN - 1), 0).reshape(P_SIZE, SPAN, C)
        block = span[:, :P_SIZE, :].reshape(CELLS, C)
        for shift, value in enumerate(
            (from_previous_column(block, cell_col), block, from_next_column(block, cell_col))
        ):
            value = value.astype(BF16)
            for shift_row in range(3):
                store_window(win_a, base, 3 * shift_row + shift, value)

        log_sigma = math.log(SIGMA_LOW) + jnp.full((1, 1), level) * log_step
        sigma = jnp.exp(log_sigma)
        variance = sigma * sigma + SIGMA_DATA * SIGMA_DATA
        scale_in = 1.0 / jnp.sqrt(variance)
        embed = jnp.log(sigma) / 4.0

        tile_rows = target.shape[0]
        lines = pltpu.roll(target32[...], lax.rem(tile_rows - row, tile_rows), 0)[:P_SIZE]
        clean = jnp.sum(
            jnp.where(field_lane == column + field_col, lines[:, None, :], 0.0),
            axis=2,
            keepdims=True,
        )
        at = pl.multiple_of(inner * CELLS, C)
        first = table[device, :, pl.ds(at, C)]
        second = table[device, :, pl.ds(pl.multiple_of(at + C, C), C)]
        half = (P_SIZE // 2, P_SIZE, C)
        drawn = jnp.concatenate(
            [jnp.broadcast_to(first[None], half), jnp.broadcast_to(second[None], half)], axis=0
        )
        noise = jnp.sum(jnp.where(noise_pick, drawn, 0.0), axis=2, keepdims=True)
        clean = jnp.broadcast_to(clean, pick_shape).reshape(CELLS, C)
        noise = jnp.broadcast_to(noise, pick_shape).reshape(CELLS, C)
        scaled = scale_in * (clean + sigma * noise)
        aim[base : base + CELLS] = scale_in * (2.0 * sigma * clean - 0.5 * noise)

        rows = jnp.where(
            lane_row == 0,
            from_previous_row(scaled),
            jnp.where(lane_row == 2, from_next_row(scaled), scaled),
        )
        moved = jnp.where(
            lane_col == 0,
            from_previous_column(rows, cell_col),
            jnp.where(lane_col == 2, from_next_column(rows, cell_col), rows),
        )
        moved_high = high(moved)
        value = jnp.where(lane < 2 * taps, moved_high, moved - moved_high)
        embed_high = high(embed)
        rest = jnp.where(
            lane < 29, 1.0, jnp.where(lane < 31, embed_high, embed - embed_high)
        )
        value = jnp.where(lane < 3 * taps, value, jnp.where(lane < 32, rest, 0.0))
        win_a[base : base + CELLS, taps * C :] = value.astype(BF16)

    def work(step, carry):
        slots_at = [step * GROUP + part for part in range(GROUP)]
        real = [slot < count for slot in slots_at]
        used = [jnp.minimum(slot, count - 1) for slot in slots_at]
        for part in range(GROUP):
            @pl.when(real[part])
            def _(part=part):
                block_copy(used[part])[0].wait()

        for part in range(GROUP):
            prepare(part, used[part])
        weights = []
        for part in range(GROUP):
            device, inner = fields(used[part])
            weight = ints[device, inner * FIELDS + 4]
            weights.append(jnp.where(real[part], weight, 0.0))

        for at in range(0, HID, 256):
            lanes = slice(at, at + 256)
            pre_a = jnp.dot(win_a[...], weight_a[:, lanes], preferred_element_type=F32)
            gate = sigmoid(pre_a)
            act[:, lanes] = (pre_a * gate).astype(BF16)
            slope[:, lanes] = gate * (1.0 + pre_a * (1.0 - gate))

        product = jnp.dot(act[...], weight_b[...], preferred_element_type=F32)
        columns = []
        for shift in range(3):
            tap = [product[:, (3 * r + shift) * C : (3 * r + shift + 1) * C] for r in range(3)]
            columns.append(from_previous_row(tap[0]) + tap[1] + from_next_row(tap[2]))
        pre_b = (
            b_b[...]
            + from_previous_column(columns[0], both_col)
            + columns[1]
            + from_next_column(columns[2], both_col)
        )
        gate = sigmoid(pre_b)
        final = jnp.sum(pre_b * gate * w_o[...], axis=1, keepdims=True)
        residual = final - aim[...]
        factors = []
        for part in range(GROUP):
            base = part * CELLS
            mine = residual[base : base + CELLS]
            loss = weights[part] * jnp.sum(mine * mine) * (1.0 / (CELLS * C))
            device, inner = fields(used[part])
            spot = jnp.logical_and(loss_row == device, loss_lane == inner)
            loss_out[...] += jnp.where(spot, loss, 0.0)
            factors.append((2.0 / CELLS) * weights[part] * mine)
        factor = jnp.concatenate(factors, axis=0)
        grad_pre_b = factor * w_o[...] * (gate * (1.0 + pre_b * (1.0 - gate)))
        for shift, value in enumerate(
            (from_next_column(grad_pre_b, both_col), grad_pre_b, from_previous_column(grad_pre_b, both_col))
        ):
            value = value.astype(BF16)
            for part in range(GROUP):
                mine = value[part * CELLS : (part + 1) * CELLS]
                for shift_row in range(3):
                    lanes = pl.ds((3 * shift_row + shift) * C, C)
                    base = part * CELLS
                    if shift_row == 0:
                        win_g[base : base + CELLS - P_SIZE, lanes] = mine[P_SIZE:]
                    elif shift_row == 1:
                        win_g[base : base + CELLS, lanes] = mine
                    else:
                        win_g[base + P_SIZE : base + CELLS, lanes] = mine[: CELLS - P_SIZE]

        over_cells = (((0,), (0,)), ((), ()))
        grad_b[...] += lax.dot_general(
            act[...], win_g[...], over_cells, preferred_element_type=F32
        )
        grad_hidden = lax.dot_general(
            win_g[...], weight_b[...], (((1,), (1,)), ((), ())), preferred_element_type=F32
        )
        grad_pre_a = (grad_hidden * slope[...]).astype(BF16)
        grad_a[...] += lax.dot_general(
            grad_pre_a, win_a[:, : taps * C], over_cells, preferred_element_type=F32
        )
        return carry

    for part in range(GROUP):
        base = part * CELLS
        win_g[base + CELLS - P_SIZE : base + CELLS, : 3 * C] = edge
        win_g[base : base + P_SIZE, 6 * C : 9 * C] = edge
    lax.fori_loop(0, lax.div(count + GROUP - 1, GROUP), work, 0)

    chunk = HID // devices
    my_core = place[2]
    for pair in range(devices // 2):
        for at, grad in ((0, grad_a), (taps * C, grad_b)):
            lanes = pl.ds(at, taps * C)
            even = grad[2 * pair * chunk : (2 * pair + 1) * chunk]
            odd = grad[(2 * pair + 1) * chunk : (2 * pair + 2) * chunk]
            first = my_core == 0
            keep_out[pair, :, lanes] = jnp.where(first, even, odd)
            send_out[pair, :, lanes] = jnp.where(first, odd, even).astype(BF16)


def halve_kernel(fan, count, place, keep, *refs):
    received, outs = refs[:count], refs[count:]
    mine = place[0]
    for peer in range(fan):
        low = jnp.bitwise_xor(mine, peer)
        for high_part in range(keep.shape[0] // fan):
            at = high_part * fan + low
            total = keep[at]
            for other in received:
                total = total + other[at].astype(F32)
            outs[peer][high_part] = total.astype(outs[peer].dtype)


def finish_kernel(npatch, keep, losses, *refs):
    received, (grad, payload) = refs[:-2], refs[-2:]
    total = keep[0]
    for other in received:
        total = total + other[0].astype(F32)
    grad[...] = total
    half = total.shape[1] // 2
    lane = lax.broadcasted_iota(jnp.int32, losses.shape, 1)
    square_a = jnp.sum(total[:, :half] * total[:, :half])
    square_b = jnp.sum(total[:, half:] * total[:, half:])
    value = jnp.where(lane == npatch, square_a, losses[...])
    payload[:, 0, :] = jnp.where(lane == npatch + 1, square_b, value)


def scale_kernel(npatch, entries, grad, payload, losses, upd_a, upd_b):
    total = jnp.sum(payload[:, 0, :], axis=0, keepdims=True)
    lane = lax.broadcasted_iota(jnp.int32, total.shape, 1)
    losses[...] = total
    half = grad.shape[1] // 2
    for part, out in enumerate((upd_a, upd_b)):
        square = jnp.sum(jnp.where(lane == npatch + part, total, 0.0), axis=1, keepdims=True)
        out[...] = grad[:, part * half : (part + 1) * half] / jnp.sqrt(square / entries + EPSILON)


def local(
    features,
    target_field,
    owner_tile,
    row_offset,
    column_start,
    noise_level,
    icing_count,
    noise_draw,
    w_a,
    w_u,
    b_a,
    e_a,
    w_b,
    b_b,
    w_o,
):
    tile_count, dp_count = lax.axis_size("tile"), lax.axis_size("dp")
    devices = tile_count * dp_count
    npatch = owner_tile.shape[0]
    slots = max(2, 2 * npatch // tile_count) * devices // dp_count
    chunk = HID // devices
    width = 2 * 9 * C
    tile, dp = lax.axis_index("tile"), lax.axis_index("dp")
    index = tile * dp_count + dp
    any_space = pl.BlockSpec(memory_space=pl.ANY)
    in_vmem = pl.BlockSpec(memory_space=pltpu.VMEM)
    in_smem = pl.BlockSpec(memory_space=pltpu.SMEM)

    numbers = jnp.stack(
        [owner_tile[:, 0], row_offset, column_start, noise_level, icing_count], axis=1
    ).astype(F32)
    numbers = jnp.pad(numbers, ((0, 0), (0, FIELDS - 5))).reshape(-1)
    numbers = jnp.pad(numbers, (0, C - numbers.shape[0]))
    line = jnp.concatenate([noise_draw.reshape(-1), numbers])
    table = lax.all_to_all(
        jnp.broadcast_to(line[None, None, :], (devices, 1, line.shape[0])),
        AXES,
        split_axis=0,
        concat_axis=0,
        tiled=True,
    )

    place = jnp.stack([tile, dp, lax.rem(index, 2)]).astype(jnp.int32)
    keep, send, losses = pl.pallas_call(
        functools.partial(train_kernel, dp_count, npatch),
        out_shape=(
            jax.ShapeDtypeStruct((devices // 2, chunk, width), F32),
            jax.ShapeDtypeStruct((devices // 2, chunk, width), BF16),
            jax.ShapeDtypeStruct((devices, C), F32),
        ),
        in_specs=[
            in_smem,
            any_space,
            in_vmem,
            any_space,
            in_vmem,
            any_space,
            in_vmem,
            in_vmem,
            in_vmem,
            any_space,
            in_vmem,
            in_vmem,
        ],
        out_specs=(in_vmem, in_vmem, in_vmem),
        scratch_shapes=[
            pltpu.SMEM((devices, C), F32),
            pltpu.SMEM((slots + 1,), jnp.int32),
            pltpu.VMEM((slots, P_SIZE, SPAN, C), BF16),
            pltpu.VMEM(target_field.shape, F32),
            pltpu.VMEM((C, HID), F32),
            pltpu.VMEM((10 * C, HID), BF16),
            pltpu.VMEM((HID, 9 * C), BF16),
            pltpu.VMEM((GROUP * CELLS, 10 * C), BF16),
            pltpu.VMEM((GROUP * CELLS, HID), BF16),
            pltpu.VMEM((GROUP * CELLS, 9 * C), BF16),
            pltpu.VMEM((GROUP * CELLS, HID), F32),
            pltpu.VMEM((GROUP * CELLS, C), F32),
            pltpu.VMEM((HID, 9 * C), F32),
            pltpu.VMEM((HID, 9 * C), F32),
            pltpu.SemaphoreType.DMA,
            pltpu.SemaphoreType.DMA((10,)),
            pltpu.SemaphoreType.DMA((slots,)),
        ],
        compiler_params=pltpu.CompilerParams(vmem_limit_bytes=50 * 1024 * 1024),
        name="train",
    )(
        place,
        table,
        table,
        features,
        target_field,
        w_a,
        w_u,
        b_a.reshape(1, -1),
        e_a.reshape(1, -1),
        w_b,
        b_b.reshape(1, -1),
        w_o.reshape(1, -1),
    )

    def exchange(array, distance):
        return lax.ppermute(array, AXES, [(i, i ^ distance) for i in range(devices)])

    received = [exchange(send, 1)]
    step = 2
    while step < devices:
        fan = min(8, devices // step)
        side = lax.rem(lax.div(index, step), fan).astype(jnp.int32).reshape(1)
        part = (keep.shape[0] // fan, chunk, width)
        outs = pl.pallas_call(
            functools.partial(halve_kernel, fan, len(received)),
            out_shape=(
                jax.ShapeDtypeStruct(part, F32),
                *[jax.ShapeDtypeStruct(part, BF16) for _ in range(fan - 1)],
            ),
            in_specs=[in_smem] + [in_vmem] * (1 + len(received)),
            out_specs=(in_vmem,) * fan,
            compiler_params=pltpu.CompilerParams(vmem_limit_bytes=32 * 1024 * 1024),
            name=f"halve_{step}",
        )(side, keep, *received)
        keep = outs[0]
        received = [exchange(outs[peer], peer * step) for peer in range(1, fan)]
        step *= fan

    grad, payload = pl.pallas_call(
        functools.partial(finish_kernel, npatch),
        out_shape=(
            jax.ShapeDtypeStruct((chunk, width), F32),
            jax.ShapeDtypeStruct((devices, 1, C), F32),
        ),
        in_specs=[in_vmem] * (2 + len(received)),
        out_specs=(in_vmem, in_vmem),
        name="finish",
    )(keep, losses, *received)
    payload = lax.all_to_all(payload, AXES, split_axis=0, concat_axis=0, tiled=True)
    out = jax.ShapeDtypeStruct((chunk, width // 2), F32)
    sums, upd_a, upd_b = pl.pallas_call(
        functools.partial(scale_kernel, npatch, HID * 9 * C),
        out_shape=(jax.ShapeDtypeStruct((1, C), F32), out, out),
        in_specs=[in_vmem, in_vmem],
        out_specs=(in_vmem,) * 3,
        name="scale",
    )(grad, payload)
    return sums[0, :npatch], upd_a, upd_b


def solution(mesh):
    both = P(AXES)
    return jax.shard_map(
        local,
        mesh=mesh,
        in_specs=(
            P("tile", None, None),
            P("tile", None),
            P(AXES, None),
            both,
            both,
            both,
            both,
            P(AXES, None, None),
            P(),
            P(),
            P(),
            P(),
            P(),
            P(),
            P(),
        ),
        out_specs=(both, P(AXES, None), P(AXES, None)),
        check_vma=False,
    )
```

time: 461 us -> 97.4 us (0.21)
  local copies, waits for them, and re-layouts: 177 us -> 13.9 us
  waiting for transfers between devices: 132 us -> 23.9 us
  matrix products: 44.8 us -> 0 us
  other arithmetic: 31.3 us -> 0.09 us
  blocking collectives: 40.2 us -> 10.8 us
  Pallas kernels: 0 us -> 17.6 us
  between operations: 16.2 us -> 0.7 us
  starting transfers between devices: 16.5 us -> 29.7 us
    unnamed x2 -> x0, waiting for transfers between devices: 105 us -> none
    gather x98 -> x0, local copies, waits for them, and re-layouts: 100 us -> none
    scatter-add x7 -> x0, local copies, waits for them, and re-layouts: 58.4 us -> none  [patch_terms(): grad_hidden = grad_hidden.at[:, shift_row:shift_row + side_len, shift_col...]
    dot_general x46 -> x0, matrix products: 44.8 us -> none  [the longest x9 13.4 us: patch_terms(): lax.dot_general(grad_pre_b, w_b[tap_index * hidden_width:(tap_index + 1)...]
    psum x1 -> x0, blocking collectives: 40.2 us -> none  [local(): lax.psum((jnp.sum(shard_a * shard_a), jnp.sum(shard_b * shard_b)), ('tile...]
    ppermute x0 -> x9, starting transfers between devices: none -> 22.4 us  [exchange(): lax.ppermute(array, AXES, [(i, i ^ distance) for i in range(devices)])]
    all_to_all x3 -> x1, waiting for transfers between devices: 26.3 us -> 8.33 us  [local(): lax.all_to_all(jnp.broadcast_to(line[None, None, :], (devices, 1, line.sh...]
    pallas_call x0 -> x5, Pallas kernels: none -> 17.6 us  [the longest x1 13.9 us: local(): pl.pallas_call(functools.partial(train_kernel, dp_count, npatch), out_sha...]
  transfers between devices with their start and end apart: 4 -> 10, of which waited for: 3 -> 9; matrix products, arithmetic and copies ran while one was open for 13% -> 0% of each run, Pallas kernels for 0% -> 0%
where the time goes in v1:
time: 97.4 us; the launch traced here: 96.7 us
  starting transfers between devices  29.7 us (30%)
  waiting for transfers between devices  23.9 us (25%)
  Pallas kernels  17.6 us (18%)
  local copies, waits for them, and re-layouts  13.9 us (14%)
  blocking collectives  10.8 us (11%)
    ppermute x9, starting transfers between devices, exchange(): lax.ppermute(array, AXES, [(i, i ^ distance) for i in range(devices)])  22.4 us
    ppermute x9, waiting for transfers between devices, exchange(): lax.ppermute(array, AXES, [(i, i ^ distance) for i in range(devices)])  15.5 us
    pallas_call x1, Pallas kernels, local(): pl.pallas_call(functools.partial(train_kernel, dp_count, npatch), out_sha...  13.9 us
    all_to_all x1, blocking collectives, local(): lax.all_to_all(payload, AXES, split_axis=0, concat_axis=0, tiled=True)  10.8 us
    unnamed x25, local copies, waits for them, and re-layouts  10.4 us
    all_to_all x1, waiting for transfers between devices, local(): lax.all_to_all(jnp.broadcast_to(line[None, None, :], (devices, 1, line.sh...  8.33 us
    all_to_all x1, starting transfers between devices, local(): lax.all_to_all(jnp.broadcast_to(line[None, None, :], (devices, 1, line.sh...  7.3 us
  transfers between devices with their start and end apart: 10, of which 9 were waited for; matrix products, arithmetic and copies ran while one was open for 0% of the time, Pallas kernels for 0%

profile of v1, /device:TPU:0, one launch (start us, length us, event | category | flops | bytes accessed | tf_op | source)
XLA Modules:
  0.0 96.7 jit_solution(6451468647198198330)
XLA Ops:
  0.6 0.7 stack.35
  1.4 0.1 copy.19
  1.5 0.1 reshape.36
  1.6 0.8 reshape.35
  2.4 0.7 broadcast_in_dim.2
  3.2 7.3 %all-to-all-start = ((f32[32,1,1152]{2,1,0:T(1,128)}), f32[32,1,1152]{2,1,0:T(1,128)S(1)}, u32[]{:S(2)}, u32[]{:S(2)}) async-start(f32[32,1,1152]{2,1,0:T(1,128)} %broadcast_in_dim.2), calls=%async_computation | async-start | bytes 294912 | tf_op jit(solution)/shard_map/all_to_all | solution.py:440
  10.5 0.1 pad_add_fusion.place
  10.5 8.3 %all-to-all-done.table_hbm.table = f32[32,1,1152]{2,1,0:T(1,128)S(1)} async-done(((f32[32,1,1152]{2,1,0:T(1,128)}), f32[32,1,1152]{2,1,0:T(1,128)S(1)}, u32[]{:S(2)}, u32[]{:S(2)}) %all-to-all-start) | async-done | bytes 147488 | tf_op jit(solution)/shard_map/all_to_all | solution.py:440
  18.9 0.0 copy-start.1
  18.9 1.3 %copy-done.1 = bf16[1152,512]{1,0:T(8,128)(2,1)S(1)} copy-done((bf16[1152,512]{1,0:T(8,128)(2,1)S(1)}, bf16[1152,512]{1,0:T(8,128)(2,1)}, u32[]{:S(2)}) %copy-start.1) | copy-done | bytes 1179672
  20.1 1.3 %copy-done.2 = bf16[4608,128]{1,0:T(8,128)(2,1)S(1)} copy-done((bf16[4608,128]{1,0:T(8,128)(2,1)S(1)}, bf16[4608,128]{1,0:T(8,128)(2,1)}, u32[]{:S(2)}) %copy-start.2) | copy-done | bytes 1179672
  21.4 0.8 copy-done.4
  22.2 0.8 copy-done.5
  22.9 0.7 copy-done.7
  23.6 0.7 copy-done.8
  24.3 0.7 copy-done.9
  25.0 0.7 copy-done.10
  25.6 13.9 %train.1 = (f32[16,16,2304]{2,1,0:T(8,128)}, bf16[16,16,2304]{2,1,0:T(8,128)(2,1)S(1)}, f32[32,128]{1,0:T(8,128)S(1)}) custom-call(s32[3]{0:T(128)S(1)} %pad_add_fusion.place, f32[32,1,1152]{2,1,0:T(1,128)S(1)} %all-to-all-done.table_hbm.table, f32[32,1,1152]{2,1,0:T(1,128)S(1)} %all-to-all-done.table_hbm.table, bf16[64,256,128]{2,1,0:T(8,128)(2,1)} %features.1, ...), custom_call_target="tpu_custom_call" | custom-call | tf_op jit(solution)/shard_map/train/pallas_call | solution.py:449
  39.5 0.0 copy-start.6
  39.5 0.6 copy-done.6
  40.1 0.3 collective-permute-start
  40.4 2.5 %collective-permute-done.refs_0_ = bf16[16,16,2304]{2,1,0:T(8,128)(2,1)S(1)} collective-permute-done((bf16[16,16,2304]{2,1,0:T(8,128)(2,1)S(1)}, bf16[16,16,2304]{2,1,0:T(8,128)(2,1)S(1)}, u32[]{:S(2)}, u32[]{:S(2)}) %collective-permute-start) | collective-permute-done | bytes 1179680 | tf_op jit(solution)/shard_map/ppermute | solution.py:508
  42.9 1.7 %copy-done = f32[16,16,2304]{2,1,0:T(8,128)S(1)} copy-done((f32[16,16,2304]{2,1,0:T(8,128)S(1)}, f32[16,16,2304]{2,1,0:T(8,128)}, u32[]{:S(2)}) %copy-start) | copy-done | bytes 2359320
  44.6 0.2 halve_2.1
  44.8 0.6 collective-permute-start.1
  45.4 1.0 %collective-permute-start.2 = (bf16[2,16,2304]{2,1,0:T(8,128)(2,1)S(1)}, bf16[2,16,2304]{2,1,0:T(8,128)(2,1)S(1)}, u32[]{:S(2)}, u32[]{:S(2)}) collective-permute-start(bf16[2,16,2304]{2,1,0:T(8,128)(2,1)S(1)} %get-tuple-element.25), channel_id=1, source_target_pairs={{0,4},{1,5},{2,6},{3,7},{4,0},{5,1},{6,2},{7,3},{8,12},{9,13},{10,... | collective-permute-start | bytes 442376 | tf_op jit(solution)/shard_map/ppermute | solution.py:508
  46.4 2.0 %collective-permute-start.3 = (bf16[2,16,2304]{2,1,0:T(8,128)(2,1)S(1)}, bf16[2,16,2304]{2,1,0:T(8,128)(2,1)S(1)}, u32[]{:S(2)}, u32[]{:S(2)}) collective-permute-start(bf16[2,16,2304]{2,1,0:T(8,128)(2,1)S(1)} %get-tuple-element.26), channel_id=1, source_target_pairs={{0,6},{1,7},{2,4},{3,5},{4,2},{5,3},{6,0},{7,1},{8,14},{9,15},{10,... | collective-permute-start | bytes 442376 | tf_op jit(solution)/shard_map/ppermute | solution.py:508
  48.4 0.7 collective-permute-start.4
  49.1 1.3 %collective-permute-start.5 = (bf16[2,16,2304]{2,1,0:T(8,128)(2,1)S(1)}, bf16[2,16,2304]{2,1,0:T(8,128)(2,1)S(1)}, u32[]{:S(2)}, u32[]{:S(2)}) collective-permute-start(bf16[2,16,2304]{2,1,0:T(8,128)(2,1)S(1)} %get-tuple-element.28), channel_id=1, source_target_pairs={{0,10},{1,11},{2,8},{3,9},{4,14},{5,15},{6,12},{7,13},{8,2},{9,3},... | collective-permute-start | bytes 442376 | tf_op jit(solution)/shard_map/ppermute | solution.py:508
  50.4 0.6 collective-permute-done.1.refs_0_
  50.9 0.7 collective-permute-start.6
  51.6 0.5 collective-permute-done.2.refs_1_
  52.1 2.1 %collective-permute-start.7 = (bf16[2,16,2304]{2,1,0:T(8,128)(2,1)S(1)}, bf16[2,16,2304]{2,1,0:T(8,128)(2,1)S(1)}, u32[]{:S(2)}, u32[]{:S(2)}) collective-permute-start(bf16[2,16,2304]{2,1,0:T(8,128)(2,1)S(1)} %get-tuple-element.30), channel_id=1, source_target_pairs={{0,14},{1,15},{2,12},{3,13},{4,10},{5,11},{6,8},{7,9},{8,6},{9,7},... | collective-permute-start | bytes 442376 | tf_op jit(solution)/shard_map/ppermute | solution.py:508
  54.2 2.5 %collective-permute-done.3.refs_2_ = bf16[2,16,2304]{2,1,0:T(8,128)(2,1)S(1)} collective-permute-done((bf16[2,16,2304]{2,1,0:T(8,128)(2,1)S(1)}, bf16[2,16,2304]{2,1,0:T(8,128)(2,1)S(1)}, u32[]{:S(2)}, u32[]{:S(2)}) %collective-permute-start.3) | collective-permute-done | bytes 147488 | tf_op jit(solution)/shard_map/ppermute | solution.py:508
  56.8 0.0 collective-permute-done.4.refs_3_
  56.8 1.5 %collective-permute-done.5.refs_4_ = bf16[2,16,2304]{2,1,0:T(8,128)(2,1)S(1)} collective-permute-done((bf16[2,16,2304]{2,1,0:T(8,128)(2,1)S(1)}, bf16[2,16,2304]{2,1,0:T(8,128)(2,1)S(1)}, u32[]{:S(2)}, u32[]{:S(2)}) %collective-permute-start.5) | collective-permute-done | bytes 147488 | tf_op jit(solution)/shard_map/ppermute | solution.py:508
  58.3 3.2 %collective-permute-done.6.refs_5_ = bf16[2,16,2304]{2,1,0:T(8,128)(2,1)S(1)} collective-permute-done((bf16[2,16,2304]{2,1,0:T(8,128)(2,1)S(1)}, bf16[2,16,2304]{2,1,0:T(8,128)(2,1)S(1)}, u32[]{:S(2)}, u32[]{:S(2)}) %collective-permute-start.6) | collective-permute-done | bytes 147488 | tf_op jit(solution)/shard_map/ppermute | solution.py:508
  61.5 1.8 %collective-permute-done.7.refs_6_ = bf16[2,16,2304]{2,1,0:T(8,128)(2,1)S(1)} collective-permute-done((bf16[2,16,2304]{2,1,0:T(8,128)(2,1)S(1)}, bf16[2,16,2304]{2,1,0:T(8,128)(2,1)S(1)}, u32[]{:S(2)}, u32[]{:S(2)}) %collective-permute-start.7) | collective-permute-done | bytes 147488 | tf_op jit(solution)/shard_map/ppermute | solution.py:508
  63.3 0.1 halve_16.1
  63.4 0.0 copy-start.3
  63.5 0.6 copy-done.3
  64.1 13.8 %collective-permute-start.8 = (bf16[1,16,2304]{2,1,0:T(8,128)(2,1)S(1)}, bf16[1,16,2304]{2,1,0:T(8,128)(2,1)S(1)}, u32[]{:S(2)}, u32[]{:S(2)}) collective-permute-start(bf16[1,16,2304]{2,1,0:T(8,128)(2,1)S(1)} %get-tuple-element.33), channel_id=1, source_target_pairs={{0,16},{1,17},{2,18},{3,19},{4,20},{5,21},{6,22},{7,23},{8,24},{9,... | collective-permute-start | bytes 221192 | tf_op jit(solution)/shard_map/ppermute | solution.py:508
  77.9 2.8 %collective-permute-done.8.refs_0_ = bf16[1,16,2304]{2,1,0:T(8,128)(2,1)S(1)} collective-permute-done((bf16[1,16,2304]{2,1,0:T(8,128)(2,1)S(1)}, bf16[1,16,2304]{2,1,0:T(8,128)(2,1)S(1)}, u32[]{:S(2)}, u32[]{:S(2)}) %collective-permute-start.8) | collective-permute-done | bytes 73760 | tf_op jit(solution)/shard_map/ppermute | solution.py:508
  80.7 0.6 copy-done.11
  81.4 1.7 %finish.1 = (f32[16,2304]{1,0:T(8,128)}, f32[32,1,128]{2,1,0:T(1,128)}) custom-call(f32[1,16,2304]{2,1,0:T(8,128)} %copy-done.3, f32[32,128]{1,0:T(8,128)} %copy-done.6, bf16[1,16,2304]{2,1,0:T(8,128)(2,1)} %copy-done.11), custom_call_target="tpu_custom_call" | custom-call | tf_op jit(solution)/shard_map/finish/pallas_call | solution.py:531
  83.1 10.8 %all_to_all.10.payload = f32[32,1,128]{2,1,0:T(1,128)} all-to-all(f32[32,1,128]{2,1,0:T(1,128)} %get-tuple-element.35), channel_id=1, replica_groups=mesh['tile'=8,'dp'=4] {'tile','dp'}, dimensions={0} | all-to-all | bytes 32768 | tf_op jit(solution)/shard_map/all_to_all | solution.py:541
  93.9 1.7 %scale.1 = (f32[1,128]{1,0:T(1,128)}, f32[16,1152]{1,0:T(8,128)}, f32[16,1152]{1,0:T(8,128)}) custom-call(f32[16,2304]{1,0:T(8,128)} %get-tuple-element.34.grad, f32[32,1,128]{2,1,0:T(1,128)} %all_to_all.10.payload), custom_call_target="tpu_custom_call" | custom-call | tf_op jit(solution)/shard_map/scale/pallas_call | solution.py:543
  95.6 1.2 %slice_bitcast_fusion = f32[4]{0:T(128)} fusion(f32[1,128]{1,0:T(1,128)} %get-tuple-element.36), kind=kLoop, calls=%fused_computation.3 | loop fusion | bytes 32 | tf_op jit(solution)/shard_map/squeeze | solution.py:550
  (12 shorter events, 0.0 us)
Async XLA Ops:
  3.2 15.7 %all-to-all-start = ((f32[32,1,1152]{2,1,0:T(1,128)}), f32[32,1,1152]{2,1,0:T(1,128)S(1)}, u32[]{:S(2)}, u32[]{:S(2)}) async-start(f32[32,1,1152]{2,1,0:T(1,128)} %broadcast_in_dim.2), calls=%async_computation | async-start | bytes 294912 | tf_op jit(solution)/shard_map/all_to_all | solution.py:440
  18.9 1.3 %copy-start.1 = (bf16[1152,512]{1,0:T(8,128)(2,1)S(1)}, bf16[1152,512]{1,0:T(8,128)(2,1)}, u32[]{:S(2)}) copy-start(bf16[1152,512]{1,0:T(8,128)(2,1)} %w_a.1) | copy-start | bytes 3538948
  20.1 1.3 %copy-start.2 = (bf16[4608,128]{1,0:T(8,128)(2,1)S(1)}, bf16[4608,128]{1,0:T(8,128)(2,1)}, u32[]{:S(2)}) copy-start(bf16[4608,128]{1,0:T(8,128)(2,1)} %w_b.1) | copy-start | bytes 3538948
  21.4 0.8 copy-start.4
  22.2 0.8 copy-start.5
  22.9 0.7 copy-start.7
  23.6 0.7 copy-start.8
  24.3 0.7 copy-start.9
  25.0 0.7 copy-start.10
  39.5 0.6 copy-start.6
  40.1 2.8 %collective-permute-start = (bf16[16,16,2304]{2,1,0:T(8,128)(2,1)S(1)}, bf16[16,16,2304]{2,1,0:T(8,128)(2,1)S(1)}, u32[]{:S(2)}, u32[]{:S(2)}) collective-permute-start(bf16[16,16,2304]{2,1,0:T(8,128)(2,1)S(1)} %get-tuple-element.22), channel_id=1, source_target_pairs={{0,1},{1,0},{2,3},{3,2},{4,5},{5,4},{6,7},{7,6},{8,9},{9,8},{10,11... | collective-permute-start | bytes 3538952 | tf_op jit(solution)/shard_map/ppermute | solution.py:508
  42.9 1.7 %copy-start = (f32[16,16,2304]{2,1,0:T(8,128)S(1)}, f32[16,16,2304]{2,1,0:T(8,128)}, u32[]{:S(2)}) copy-start(f32[16,16,2304]{2,1,0:T(8,128)} %get-tuple-element.21.keep) | copy-start | bytes 7077892
  44.8 6.1 %collective-permute-start.1 = (bf16[2,16,2304]{2,1,0:T(8,128)(2,1)S(1)}, bf16[2,16,2304]{2,1,0:T(8,128)(2,1)S(1)}, u32[]{:S(2)}, u32[]{:S(2)}) collective-permute-start(bf16[2,16,2304]{2,1,0:T(8,128)(2,1)S(1)} %get-tuple-element.24), channel_id=1, source_target_pairs={{0,2},{1,3},{2,0},{3,1},{4,6},{5,7},{6,4},{7,5},{8,10},{9,11},{10,... | collective-permute-start | bytes 442376 | tf_op jit(solution)/shard_map/ppermute | solution.py:508
  45.4 6.7 %collective-permute-start.2 = (bf16[2,16,2304]{2,1,0:T(8,128)(2,1)S(1)}, bf16[2,16,2304]{2,1,0:T(8,128)(2,1)S(1)}, u32[]{:S(2)}, u32[]{:S(2)}) collective-permute-start(bf16[2,16,2304]{2,1,0:T(8,128)(2,1)S(1)} %get-tuple-element.25), channel_id=1, source_target_pairs={{0,4},{1,5},{2,6},{3,7},{4,0},{5,1},{6,2},{7,3},{8,12},{9,13},{10,... | collective-permute-start | bytes 442376 | tf_op jit(solution)/shard_map/ppermute | solution.py:508
  46.4 10.4 %collective-permute-start.3 = (bf16[2,16,2304]{2,1,0:T(8,128)(2,1)S(1)}, bf16[2,16,2304]{2,1,0:T(8,128)(2,1)S(1)}, u32[]{:S(2)}, u32[]{:S(2)}) collective-permute-start(bf16[2,16,2304]{2,1,0:T(8,128)(2,1)S(1)} %get-tuple-element.26), channel_id=1, source_target_pairs={{0,6},{1,7},{2,4},{3,5},{4,2},{5,3},{6,0},{7,1},{8,14},{9,15},{10,... | collective-permute-start | bytes 442376 | tf_op jit(solution)/shard_map/ppermute | solution.py:508
  48.4 8.4 %collective-permute-start.4 = (bf16[2,16,2304]{2,1,0:T(8,128)(2,1)S(1)}, bf16[2,16,2304]{2,1,0:T(8,128)(2,1)S(1)}, u32[]{:S(2)}, u32[]{:S(2)}) collective-permute-start(bf16[2,16,2304]{2,1,0:T(8,128)(2,1)S(1)} %get-tuple-element.27), channel_id=1, source_target_pairs={{0,8},{1,9},{2,10},{3,11},{4,12},{5,13},{6,14},{7,15},{8,0},{9,1},... | collective-permute-start | bytes 442376 | tf_op jit(solution)/shard_map/ppermute | solution.py:508
  49.1 9.2 %collective-permute-start.5 = (bf16[2,16,2304]{2,1,0:T(8,128)(2,1)S(1)}, bf16[2,16,2304]{2,1,0:T(8,128)(2,1)S(1)}, u32[]{:S(2)}, u32[]{:S(2)}) collective-permute-start(bf16[2,16,2304]{2,1,0:T(8,128)(2,1)S(1)} %get-tuple-element.28), channel_id=1, source_target_pairs={{0,10},{1,11},{2,8},{3,9},{4,14},{5,15},{6,12},{7,13},{8,2},{9,3},... | collective-permute-start | bytes 442376 | tf_op jit(solution)/shard_map/ppermute | solution.py:508
  50.9 10.6 %collective-permute-start.6 = (bf16[2,16,2304]{2,1,0:T(8,128)(2,1)S(1)}, bf16[2,16,2304]{2,1,0:T(8,128)(2,1)S(1)}, u32[]{:S(2)}, u32[]{:S(2)}) collective-permute-start(bf16[2,16,2304]{2,1,0:T(8,128)(2,1)S(1)} %get-tuple-element.29), channel_id=1, source_target_pairs={{0,12},{1,13},{2,14},{3,15},{4,8},{5,9},{6,10},{7,11},{8,4},{9,5},... | collective-permute-start | bytes 442376 | tf_op jit(solution)/shard_map/ppermute | solution.py:508
  52.1 11.2 %collective-permute-start.7 = (bf16[2,16,2304]{2,1,0:T(8,128)(2,1)S(1)}, bf16[2,16,2304]{2,1,0:T(8,128)(2,1)S(1)}, u32[]{:S(2)}, u32[]{:S(2)}) collective-permute-start(bf16[2,16,2304]{2,1,0:T(8,128)(2,1)S(1)} %get-tuple-element.30), channel_id=1, source_target_pairs={{0,14},{1,15},{2,12},{3,13},{4,10},{5,11},{6,8},{7,9},{8,6},{9,7},... | collective-permute-start | bytes 442376 | tf_op jit(solution)/shard_map/ppermute | solution.py:508
  63.4 0.7 copy-start.3
  64.1 16.6 %collective-permute-start.8 = (bf16[1,16,2304]{2,1,0:T(8,128)(2,1)S(1)}, bf16[1,16,2304]{2,1,0:T(8,128)(2,1)S(1)}, u32[]{:S(2)}, u32[]{:S(2)}) collective-permute-start(bf16[1,16,2304]{2,1,0:T(8,128)(2,1)S(1)} %get-tuple-element.33), channel_id=1, source_target_pairs={{0,16},{1,17},{2,18},{3,19},{4,20},{5,21},{6,22},{7,23},{8,24},{9,... | collective-permute-start | bytes 221192 | tf_op jit(solution)/shard_map/ppermute | solution.py:508
  80.7 0.6 copy-start.11

commit v2 on v1

--- a/solution.py
+++ b/solution.py
@@ -52,6 +52,10 @@
     for at in range(0, x.shape[0], CELLS):
         parts += [x[at + P_SIZE : at + CELLS], zero]
     return jnp.concatenate(parts, axis=0)
+
+
+def high(value):
+    return value.astype(BF16).astype(F32)
 
 
 def store_window(ref, base, tap, rows):
@@ -65,21 +69,84 @@
         ref[base : base + CELLS - P_SIZE, lanes] = rows[P_SIZE:]
 
 
+def pack_kernel(owner, row, column, level, count, noise, line, drawn, sem):
+    copy = pltpu.make_async_copy(noise, drawn, sem)
+    copy.start()
+    npatch = noise.shape[0]
+    lane = lax.broadcasted_iota(jnp.int32, (1, C), 1)
+    numbers = jnp.zeros((1, C), jnp.int32)
+    for patch in range(npatch):
+        values = (owner[patch], row[patch], column[patch], level[patch], count[patch])
+        for at, value in enumerate(values):
+            numbers = jnp.where(lane == patch * FIELDS + at, value, numbers)
+    shape = (line.shape[0], 1, C)
+    line[:, :, npatch * CELLS :] = jnp.broadcast_to(numbers.astype(F32)[None], shape)
+    copy.wait()
+    rows = C // P_SIZE
+    mine = lax.broadcasted_iota(jnp.int32, (rows, C), 0)
+    here = lax.broadcasted_iota(jnp.int32, (rows, C), 1) // P_SIZE == mine
+    for patch in range(npatch):
+        for at in range(0, P_SIZE, rows):
+            part = drawn[patch, at : at + rows, :]
+            spread = jnp.concatenate([part] * rows, axis=1)
+            flat = jnp.sum(jnp.where(here, spread, 0.0), axis=0, keepdims=True)
+            start = patch * CELLS + at * P_SIZE
+            line[:, :, start : start + C] = jnp.broadcast_to(flat[None], shape)
+
+
+def weights_kernel(
+    w_a, w_u, b_a, e_a, w_b, b_b, w_o, target,
+    weight_a, weight_b, weight_back, ends, target32,
+    small_u, small_b, small_e, extra32, field, sems,
+):
+    taps = 9
+    copies = [
+        pltpu.make_async_copy(w_b.at[pl.ds(tap * HID, HID)], weight_b.at[:, pl.ds(tap * C, C)], sems.at[tap])
+        for tap in range(taps)
+    ]
+    places = (
+        (w_a, weight_a.at[pl.ds(0, taps * C)]),
+        (w_u, small_u),
+        (b_a, small_b),
+        (e_a, small_e),
+        (b_b, ends.at[pl.ds(0, 1)]),
+        (w_o, ends.at[pl.ds(1, 1)]),
+        (target, field),
+    )
+    smalls = [pltpu.make_async_copy(src, dst, sems.at[taps + at]) for at, (src, dst) in enumerate(places)]
+    for copy in smalls + copies:
+        copy.start()
+    for copy in smalls[1:]:
+        copy.wait()
+    target32[...] = field[...].astype(F32)
+    extra32[...] = jnp.zeros_like(extra32)
+    w_u_value, b_a_value, e_a_value = small_u[...], small_b[...], small_e[...]
+    extra32[0:taps] = high(w_u_value)
+    extra32[taps : 2 * taps] = w_u_value - high(w_u_value)
+    extra32[2 * taps : 3 * taps] = high(w_u_value)
+    extra32[27:28] = high(b_a_value)
+    extra32[28:29] = b_a_value - high(b_a_value)
+    extra32[29:30] = high(e_a_value)
+    extra32[30:31] = e_a_value - high(e_a_value)
+    extra32[31:32] = high(e_a_value)
+    weight_a[taps * C :] = extra32[...].astype(BF16)
+    for tap, copy in enumerate(copies):
+        copy.wait()
+        weight_back[tap * C : (tap + 1) * C, :] = weight_b[:, tap * C : (tap + 1) * C].T
+    smalls[0].wait()
+
+
 def train_kernel(
     dp_count,
     npatch,
-    place,
     table_hbm,
     table,
     features,
-    target,
-    w_a,
-    w_u,
-    b_a,
-    e_a,
-    w_b,
-    b_b,
-    w_o,
+    target32_hbm,
+    weight_a_hbm,
+    weight_b_hbm,
+    weight_back_hbm,
+    ends_hbm,
     keep_out,
     send_out,
     loss_out,
@@ -87,9 +154,10 @@
     chosen,
     blocks,
     target32,
-    extra32,
     weight_a,
     weight_b,
+    weight_back,
+    ends,
     win_a,
     act,
     win_g,
@@ -104,21 +172,19 @@
     devices = table.shape[0]
     slots = blocks.shape[0]
     taps = 9
-    my_tile, my_dp = place[0], place[1]
+    my_tile, my_dp = lax.axis_index("tile"), lax.axis_index("dp")
+    my_core = lax.rem(my_tile * dp_count + my_dp, 2)
 
     copy_ints = pltpu.make_async_copy(table_hbm.at[:, 0, pl.ds(npatch * CELLS, C)], ints, int_sem)
     copy_ints.start()
-    copies = [pltpu.make_async_copy(w_a, weight_a.at[pl.ds(0, taps * C)], weight_sems.at[taps])]
-    for tap in range(taps):
-        copies.append(
-            pltpu.make_async_copy(
-                w_b.at[pl.ds(tap * HID, HID)],
-                weight_b.at[:, pl.ds(tap * C, C)],
-                weight_sems.at[tap],
-            )
-        )
-    for copy in copies:
-        copy.start()
+    operands = (
+        (target32_hbm, target32),
+        (ends_hbm, ends),
+        (weight_a_hbm, weight_a),
+        (weight_b_hbm, weight_b),
+        (weight_back_hbm, weight_back),
+    )
+    copies = [pltpu.make_async_copy(src, dst, weight_sems.at[at]) for at, (src, dst) in enumerate(operands)]
     copy_ints.wait()
 
     tile_name = my_tile.astype(F32)
@@ -161,32 +227,23 @@
         return carry
 
     lax.fori_loop(0, count, start_block, 0)
-
-    grad_a[...] = jnp.zeros_like(grad_a)
-    grad_b[...] = jnp.zeros_like(grad_b)
+    for copy in copies:
+        copy.start()
+
+    @pl.when(count == 0)
+    def _():
+        grad_a[...] = jnp.zeros_like(grad_a)
+        grad_b[...] = jnp.zeros_like(grad_b)
+
     loss_out[...] = jnp.zeros_like(loss_out)
     edge = jnp.zeros((P_SIZE, 3 * C), BF16)
     for part in range(GROUP):
-        base = part * CELLS
-        for ref in (win_a, win_g):
-            ref[base : base + P_SIZE, : 3 * C] = edge
-            ref[base + CELLS - P_SIZE : base + CELLS, 6 * C : 9 * C] = edge
-    target32[...] = target[...].astype(F32)
-
-    def high(value):
-        return value.astype(BF16).astype(F32)
-
-    extra32[...] = jnp.zeros_like(extra32)
-    w_u_value, b_a_value, e_a_value = w_u[...], b_a[...], e_a[...]
-    extra32[0:taps] = high(w_u_value)
-    extra32[taps : 2 * taps] = w_u_value - high(w_u_value)
-    extra32[2 * taps : 3 * taps] = high(w_u_value)
-    extra32[27:28] = high(b_a_value)
-    extra32[28:29] = b_a_value - high(b_a_value)
-    extra32[29:30] = high(e_a_value)
-    extra32[30:31] = e_a_value - high(e_a_value)
-    extra32[31:32] = high(e_a_value)
-    weight_a[taps * C :] = extra32[...].astype(BF16)
+        first, last = part * CELLS, (part + 1) * CELLS - P_SIZE
+        win_a[first : first + P_SIZE, : 3 * C] = edge
+        win_a[last : last + P_SIZE, 6 * C : 9 * C] = edge
+        win_g[last : last + P_SIZE, : 3 * C] = edge
+        win_g[first : first + P_SIZE, 6 * C : 9 * C] = edge
+
     for copy in copies:
         copy.wait()
 
@@ -199,7 +256,7 @@
     pick_col = lax.broadcasted_iota(jnp.int32, pick_shape, 1)
     pick_lane = lax.broadcasted_iota(jnp.int32, pick_shape, 2)
     noise_pick = pick_lane == pick_row * P_SIZE + pick_col
-    field_shape = (P_SIZE, P_SIZE, target.shape[1])
+    field_shape = (P_SIZE, P_SIZE, target32.shape[1])
     field_col = lax.broadcasted_iota(jnp.int32, field_shape, 1)
     field_lane = lax.broadcasted_iota(jnp.int32, field_shape, 2)
     loss_row = lax.broadcasted_iota(jnp.int32, loss_out.shape, 0)
@@ -230,7 +287,7 @@
         scale_in = 1.0 / jnp.sqrt(variance)
         embed = jnp.log(sigma) / 4.0
 
-        tile_rows = target.shape[0]
+        tile_rows = target32.shape[0]
         lines = pltpu.roll(target32[...], lax.rem(tile_rows - row, tile_rows), 0)[:P_SIZE]
         clean = jnp.sum(
             jnp.where(field_lane == column + field_col, lines[:, None, :], 0.0),
@@ -299,13 +356,13 @@
             tap = [product[:, (3 * r + shift) * C : (3 * r + shift + 1) * C] for r in range(3)]
             columns.append(from_previous_row(tap[0]) + tap[1] + from_next_row(tap[2]))
         pre_b = (
-            b_b[...]
+            ends[0:1]
             + from_previous_column(columns[0], both_col)
             + columns[1]
             + from_next_column(columns[2], both_col)
         )
         gate = sigmoid(pre_b)
-        final = jnp.sum(pre_b * gate * w_o[...], axis=1, keepdims=True)
+        final = jnp.sum(pre_b * gate * ends[1:2], axis=1, keepdims=True)
         residual = final - aim[...]
         factors = []
         for part in range(GROUP):
@@ -317,7 +374,7 @@
             loss_out[...] += jnp.where(spot, loss, 0.0)
             factors.append((2.0 / CELLS) * weights[part] * mine)
         factor = jnp.concatenate(factors, axis=0)
-        grad_pre_b = factor * w_o[...] * (gate * (1.0 + pre_b * (1.0 - gate)))
+        grad_pre_b = factor * ends[1:2] * (gate * (1.0 + pre_b * (1.0 - gate)))
         for shift, value in enumerate(
             (from_next_column(grad_pre_b, both_col), grad_pre_b, from_previous_column(grad_pre_b, both_col))
         ):
@@ -335,26 +392,20 @@
                         win_g[base + P_SIZE : base + CELLS, lanes] = mine[: CELLS - P_SIZE]
 
         over_cells = (((0,), (0,)), ((), ()))
-        grad_b[...] += lax.dot_general(
+        started = step > 0
+        grad_b[...] = jnp.where(started, grad_b[...], 0.0) + lax.dot_general(
             act[...], win_g[...], over_cells, preferred_element_type=F32
         )
-        grad_hidden = lax.dot_general(
-            win_g[...], weight_b[...], (((1,), (1,)), ((), ())), preferred_element_type=F32
-        )
+        grad_hidden = jnp.dot(win_g[...], weight_back[...], preferred_element_type=F32)
         grad_pre_a = (grad_hidden * slope[...]).astype(BF16)
-        grad_a[...] += lax.dot_general(
+        grad_a[...] = jnp.where(started, grad_a[...], 0.0) + lax.dot_general(
             grad_pre_a, win_a[:, : taps * C], over_cells, preferred_element_type=F32
         )
         return carry
 
-    for part in range(GROUP):
-        base = part * CELLS
-        win_g[base + CELLS - P_SIZE : base + CELLS, : 3 * C] = edge
-        win_g[base : base + P_SIZE, 6 * C : 9 * C] = edge
     lax.fori_loop(0, lax.div(count + GROUP - 1, GROUP), work, 0)
 
     chunk = HID // devices
-    my_core = place[2]
     for pair in range(devices // 2):
         for at, grad in ((0, grad_a), (taps * C, grad_b)):
             lanes = pl.ds(at, taps * C)
@@ -365,9 +416,10 @@
             send_out[pair, :, lanes] = jnp.where(first, odd, even).astype(BF16)
 
 
-def halve_kernel(fan, count, place, keep, *refs):
+def halve_kernel(fan, count, step, keep, *refs):
     received, outs = refs[:count], refs[count:]
-    mine = place[0]
+    index = lax.axis_index("tile") * lax.axis_size("dp") + lax.axis_index("dp")
+    mine = lax.rem(lax.div(index, step), fan)
     for peer in range(fan):
         low = jnp.bitwise_xor(mine, peer)
         for high_part in range(keep.shape[0] // fan):
@@ -395,7 +447,8 @@
 def scale_kernel(npatch, entries, grad, payload, losses, upd_a, upd_b):
     total = jnp.sum(payload[:, 0, :], axis=0, keepdims=True)
     lane = lax.broadcasted_iota(jnp.int32, total.shape, 1)
-    losses[...] = total
+    for patch in range(npatch):
+        losses[patch] = jnp.sum(jnp.where(lane == patch, total, 0.0))
     half = grad.shape[1] // 2
     for part, out in enumerate((upd_a, upd_b)):
         square = jnp.sum(jnp.where(lane == npatch + part, total, 0.0), axis=1, keepdims=True)
@@ -425,57 +478,78 @@
     slots = max(2, 2 * npatch // tile_count) * devices // dp_count
     chunk = HID // devices
     width = 2 * 9 * C
-    tile, dp = lax.axis_index("tile"), lax.axis_index("dp")
-    index = tile * dp_count + dp
-    any_space = pl.BlockSpec(memory_space=pl.ANY)
+    in_hbm = pl.BlockSpec(memory_space=pltpu.HBM)
+    stay = functools.partial(pltpu.with_memory_space_constraint, memory_space=pltpu.HBM)
     in_vmem = pl.BlockSpec(memory_space=pltpu.VMEM)
     in_smem = pl.BlockSpec(memory_space=pltpu.SMEM)
 
-    numbers = jnp.stack(
-        [owner_tile[:, 0], row_offset, column_start, noise_level, icing_count], axis=1
-    ).astype(F32)
-    numbers = jnp.pad(numbers, ((0, 0), (0, FIELDS - 5))).reshape(-1)
-    numbers = jnp.pad(numbers, (0, C - numbers.shape[0]))
-    line = jnp.concatenate([noise_draw.reshape(-1), numbers])
-    table = lax.all_to_all(
-        jnp.broadcast_to(line[None, None, :], (devices, 1, line.shape[0])),
-        AXES,
-        split_axis=0,
-        concat_axis=0,
-        tiled=True,
+    def room(mebibytes):
+        return pltpu.CompilerParams(vmem_limit_bytes=mebibytes * 1024 * 1024)
+
+    line = pl.pallas_call(
+        pack_kernel,
+        out_shape=jax.ShapeDtypeStruct((devices, 1, npatch * CELLS + C), F32),
+        in_specs=[in_smem] * 5 + [in_hbm],
+        out_specs=in_vmem,
+        scratch_shapes=[pltpu.VMEM(noise_draw.shape, F32), pltpu.SemaphoreType.DMA],
+        compiler_params=room(4),
+        name="pack",
+    )(
+        *map(stay, (owner_tile.reshape(-1), row_offset, column_start, noise_level, icing_count, noise_draw))
     )
-
-    place = jnp.stack([tile, dp, lax.rem(index, 2)]).astype(jnp.int32)
+    table = lax.all_to_all(line, AXES, split_axis=0, concat_axis=0, tiled=True)
+
+    weights = pl.pallas_call(
+        weights_kernel,
+        out_shape=(
+            pltpu.HBM((10 * C, HID), BF16),
+            pltpu.HBM((HID, 9 * C), BF16),
+            pltpu.HBM((9 * C, HID), BF16),
+            pltpu.HBM((2, C), F32),
+            pltpu.HBM(target_field.shape, F32),
+        ),
+        in_specs=[in_hbm] * 8,
+        out_specs=(in_vmem,) * 5,
+        scratch_shapes=[
+            pltpu.VMEM((9, HID), F32),
+            pltpu.VMEM((1, HID), F32),
+            pltpu.VMEM((1, HID), F32),
+            pltpu.VMEM((C, HID), F32),
+            pltpu.VMEM(target_field.shape, BF16),
+            pltpu.SemaphoreType.DMA((16,)),
+        ],
+        compiler_params=room(8),
+        name="weights",
+    )(
+        stay(w_a),
+        stay(w_u),
+        stay(b_a.reshape(1, -1)),
+        stay(e_a.reshape(1, -1)),
+        stay(w_b),
+        stay(b_b.reshape(1, -1)),
+        stay(w_o.reshape(1, -1)),
+        stay(target_field),
+    )
+    weight_a, weight_b, weight_back, ends, target32 = weights
+
     keep, send, losses = pl.pallas_call(
         functools.partial(train_kernel, dp_count, npatch),
         out_shape=(
-            jax.ShapeDtypeStruct((devices // 2, chunk, width), F32),
-            jax.ShapeDtypeStruct((devices // 2, chunk, width), BF16),
-            jax.ShapeDtypeStruct((devices, C), F32),
+            pltpu.VMEM((devices // 2, chunk, width), F32),
+            pltpu.VMEM((devices // 2, chunk, width), BF16),
+            pltpu.VMEM((devices, C), F32),
         ),
-        in_specs=[
-            in_smem,
-            any_space,
-            in_vmem,
-            any_space,
-            in_vmem,
-            any_space,
-            in_vmem,
-            in_vmem,
-            in_vmem,
-            any_space,
-            in_vmem,
-            in_vmem,
-        ],
+        in_specs=[in_hbm, in_vmem] + [in_hbm] * 6,
         out_specs=(in_vmem, in_vmem, in_vmem),
         scratch_shapes=[
             pltpu.SMEM((devices, C), F32),
             pltpu.SMEM((slots + 1,), jnp.int32),
             pltpu.VMEM((slots, P_SIZE, SPAN, C), BF16),
             pltpu.VMEM(target_field.shape, F32),
-            pltpu.VMEM((C, HID), F32),
             pltpu.VMEM((10 * C, HID), BF16),
             pltpu.VMEM((HID, 9 * C), BF16),
+            pltpu.VMEM((9 * C, HID), BF16),
+            pltpu.VMEM((2, C), F32),
             pltpu.VMEM((GROUP * CELLS, 10 * C), BF16),
             pltpu.VMEM((GROUP * CELLS, HID), BF16),
             pltpu.VMEM((GROUP * CELLS, 9 * C), BF16),
@@ -484,25 +558,12 @@
             pltpu.VMEM((HID, 9 * C), F32),
             pltpu.VMEM((HID, 9 * C), F32),
             pltpu.SemaphoreType.DMA,
-            pltpu.SemaphoreType.DMA((10,)),
+            pltpu.SemaphoreType.DMA((5,)),
             pltpu.SemaphoreType.DMA((slots,)),
         ],
-        compiler_params=pltpu.CompilerParams(vmem_limit_bytes=50 * 1024 * 1024),
+        compiler_params=room(32),
         name="train",
-    )(
-        place,
-        table,
-        table,
-        features,
-        target_field,
-        w_a,
-        w_u,
-        b_a.reshape(1, -1),
-        e_a.reshape(1, -1),
-        w_b,
-        b_b.reshape(1, -1),
-        w_o.reshape(1, -1),
-    )
+    )(table, table, *map(stay, (features, target32, weight_a, weight_b, weight_back, ends)))
 
     def exchange(array, distance):
         return lax.ppermute(array, AXES, [(i, i ^ distance) for i in range(devices)])
@@ -511,43 +572,45 @@
     step = 2
     while step < devices:
         fan = min(8, devices // step)
-        side = lax.rem(lax.div(index, step), fan).astype(jnp.int32).reshape(1)
         part = (keep.shape[0] // fan, chunk, width)
         outs = pl.pallas_call(
-            functools.partial(halve_kernel, fan, len(received)),
+            functools.partial(halve_kernel, fan, len(received), step),
             out_shape=(
-                jax.ShapeDtypeStruct(part, F32),
-                *[jax.ShapeDtypeStruct(part, BF16) for _ in range(fan - 1)],
+                pltpu.VMEM(part, F32),
+                *[pltpu.VMEM(part, BF16) for _ in range(fan - 1)],
             ),
-            in_specs=[in_smem] + [in_vmem] * (1 + len(received)),
+            in_specs=[in_vmem] * (1 + len(received)),
             out_specs=(in_vmem,) * fan,
-            compiler_params=pltpu.CompilerParams(vmem_limit_bytes=32 * 1024 * 1024),
+            compiler_params=room(8),
             name=f"halve_{step}",
-        )(side, keep, *received)
+        )(keep, *received)
         keep = outs[0]
-        received = [exchange(outs[peer], peer * step) for peer in range(1, fan)]
+        order = sorted(range(1, fan), key=lambda peer: (-peer.bit_count(), -peer))
+        received = [exchange(outs[peer], peer * step) for peer in order]
         step *= fan
 
     grad, payload = pl.pallas_call(
         functools.partial(finish_kernel, npatch),
         out_shape=(
-            jax.ShapeDtypeStruct((chunk, width), F32),
-            jax.ShapeDtypeStruct((devices, 1, C), F32),
+            pltpu.VMEM((chunk, width), F32),
+            pltpu.VMEM((devices, 1, C), F32),
         ),
         in_specs=[in_vmem] * (2 + len(received)),
         out_specs=(in_vmem, in_vmem),
+        compiler_params=room(4),
         name="finish",
     )(keep, losses, *received)
     payload = lax.all_to_all(payload, AXES, split_axis=0, concat_axis=0, tiled=True)
     out = jax.ShapeDtypeStruct((chunk, width // 2), F32)
     sums, upd_a, upd_b = pl.pallas_call(
         functools.partial(scale_kernel, npatch, HID * 9 * C),
-        out_shape=(jax.ShapeDtypeStruct((1, C), F32), out, out),
+        out_shape=(jax.ShapeDtypeStruct((npatch,), F32), out, out),
         in_specs=[in_vmem, in_vmem],
-        out_specs=(in_vmem,) * 3,
+        out_specs=(in_smem, in_vmem, in_vmem),
+        compiler_params=room(4),
         name="scale",
     )(grad, payload)
-    return sums[0, :npatch], upd_a, upd_b
+    return sums, upd_a, upd_b
 
 
 def solution(mesh):

time: 97.4 us -> 82.7 us (0.85)
  local copies, waits for them, and re-layouts: 13.9 us -> 0 us
  Pallas kernels: 17.6 us -> 20.9 us
  waiting for transfers between devices: 23.9 us -> 21.1 us
    unnamed x25 -> x0, local copies, waits for them, and re-layouts: 10.4 us -> none
    pallas_call x3 -> x5, Pallas kernels: 2.1 us -> 6.99 us  [the longest x1 4.17 us: local(): pl.pallas_call(weights_kernel, out_shape=(pltpu.HBM((10 * C, HID), BF16),...]
    all_to_all x1, waiting for transfers between devices: 8.33 us -> 4.24 us  [local(): table = lax.all_to_all(line, AXES, split_axis=0, concat_axis=0, tiled=True)]
    ppermute x9, waiting for transfers between devices: 15.5 us -> 16.8 us  [exchange(): lax.ppermute(array, AXES, [(i, i ^ distance) for i in range(devices)])]
    squeeze x1 -> x0, local copies, waits for them, and re-layouts: 1.17 us -> none  [local(): return (sums[0, :npatch], upd_a, upd_b)]
  transfers between devices with their start and end apart: 10 -> 10, of which waited for: 9 -> 9; matrix products, arithmetic and copies ran while one was open for 0% -> 0% of each run, Pallas kernels for 0% -> 5%
where the time goes in v2:
time: 82.7 us; the launch traced here: 82.4 us
  starting transfers between devices  29 us (35%)
  waiting for transfers between devices  21.1 us (26%)
  Pallas kernels  20.9 us (25%)
  blocking collectives  10.7 us (13%)
    ppermute x9, starting transfers between devices, exchange(): lax.ppermute(array, AXES, [(i, i ^ distance) for i in range(devices)])  21.7 us
    ppermute x9, waiting for transfers between devices, exchange(): lax.ppermute(array, AXES, [(i, i ^ distance) for i in range(devices)])  16.8 us
    pallas_call x1, Pallas kernels, local(): pl.pallas_call(functools.partial(train_kernel, dp_count, npatch), out_sha...  13.1 us
    all_to_all x1, blocking collectives, local(): lax.all_to_all(payload, AXES, split_axis=0, concat_axis=0, tiled=True)  10.7 us
    all_to_all x1, starting transfers between devices, local(): table = lax.all_to_all(line, AXES, split_axis=0, concat_axis=0, tiled=True)  7.3 us
    all_to_all x1, waiting for transfers between devices, local(): table = lax.all_to_all(line, AXES, split_axis=0, concat_axis=0, tiled=True)  4.24 us
    pallas_call x1, Pallas kernels, local(): pl.pallas_call(weights_kernel, out_shape=(pltpu.HBM((10 * C, HID), BF16),...  4.17 us
    pallas_call x1, Pallas kernels, local(): pl.pallas_call(pack_kernel, out_shape=jax.ShapeDtypeStruct((devices, 1, n...  2.3 us
  transfers between devices with their start and end apart: 10, of which 9 were waited for; matrix products, arithmetic and copies ran while one was open for 0% of the time, Pallas kernels for 5%

profile of v2, /device:TPU:0, one launch (start us, length us, event | category | flops | bytes accessed | tf_op | source)
XLA Modules:
  0.0 82.4 jit_solution(8666594920755201436)
XLA Ops:
  0.6 2.3 %pack.1 = f32[32,1,1152]{2,1,0:T(1,128)} custom-call(s32[4]{0:T(128)} %bitcast.7, s32[4]{0:T(128)} %row.1, s32[4]{0:T(128)} %column.1, s32[4]{0:T(128)} %level.1, s32[4]{0:T(128)} %count.1, f32[4,16,16]{2,1,0:T(8,128)} %noise.1), custom_call_target="tpu_custom_call" | custom-call | tf_op jit(solution)/shard_map/pack/pallas_call | solution.py:489
  2.9 7.3 %all-to-all-start = ((f32[32,1,1152]{2,1,0:T(1,128)}), f32[32,1,1152]{2,1,0:T(1,128)S(1)}, u32[]{:S(2)}, u32[]{:S(2)}) async-start(f32[32,1,1152]{2,1,0:T(1,128)} %pack.1), calls=%async_computation | async-start | bytes 294912 | tf_op jit(solution)/shard_map/all_to_all | solution.py:500
  10.2 4.2 %weights.1 = (bf16[1280,512]{1,0:T(8,128)(2,1)}, bf16[512,1152]{1,0:T(8,128)(2,1)}, bf16[1152,512]{1,0:T(8,128)(2,1)}, f32[2,128]{1,0:T(2,128)}, f32[64,256]{1,0:T(8,128)}) custom-call(bf16[1152,512]{1,0:T(8,128)(2,1)} %w_a.1, f32[9,512]{1,0:T(8,128)} %w_u.1, f32[1,512]{1,0:T(1,128)} %bitcast.5, f32[1,512]{1,0:T(1,128)} %bitcast.6, bf16[4608,128]{1,0:T(8,128)(2,1)} %w_b.1, ...), custom_call_target="tpu_custom_call" | custom-call | tf_op jit(solution)/shard_map/weights/pallas_call | solution.py:502
  14.4 4.2 %all-to-all-done.table_hbm.table = f32[32,1,1152]{2,1,0:T(1,128)S(1)} async-done(((f32[32,1,1152]{2,1,0:T(1,128)}), f32[32,1,1152]{2,1,0:T(1,128)S(1)}, u32[]{:S(2)}, u32[]{:S(2)}) %all-to-all-start) | async-done | bytes 147488 | tf_op jit(solution)/shard_map/all_to_all | solution.py:500
  18.7 13.1 %train.1 = (f32[16,16,2304]{2,1,0:T(8,128)S(1)}, bf16[16,16,2304]{2,1,0:T(8,128)(2,1)S(1)}, f32[32,128]{1,0:T(8,128)S(1)}) custom-call(f32[32,1,1152]{2,1,0:T(1,128)S(1)} %all-to-all-done.table_hbm.table, f32[32,1,1152]{2,1,0:T(1,128)S(1)} %all-to-all-done.table_hbm.table, bf16[64,256,128]{2,1,0:T(8,128)(2,1)} %features.1, ...), custom_call_target="tpu_custom_call" | custom-call | tf_op jit(solution)/shard_map/train/pallas_call | solution.py:535
  31.8 0.4 collective-permute-start
  32.1 2.6 %collective-permute-done.refs_0_ = bf16[16,16,2304]{2,1,0:T(8,128)(2,1)S(1)} collective-permute-done((bf16[16,16,2304]{2,1,0:T(8,128)(2,1)S(1)}, bf16[16,16,2304]{2,1,0:T(8,128)(2,1)S(1)}, u32[]{:S(2)}, u32[]{:S(2)}) %collective-permute-start) | collective-permute-done | bytes 1179680 | tf_op jit(solution)/shard_map/ppermute | solution.py:569
  34.7 0.2 halve_2.1
  34.9 1.2 %collective-permute-start.1 = (bf16[2,16,2304]{2,1,0:T(8,128)(2,1)S(1)}, bf16[2,16,2304]{2,1,0:T(8,128)(2,1)S(1)}, u32[]{:S(2)}, u32[]{:S(2)}) collective-permute-start(bf16[2,16,2304]{2,1,0:T(8,128)(2,1)S(1)} %get-tuple-element.31), channel_id=1, source_target_pairs={{0,14},{1,15},{2,12},{3,13},{4,10},{5,11},{6,8},{7,9},{8,6},{9,7},... | collective-permute-start | bytes 442376 | tf_op jit(solution)/shard_map/ppermute | solution.py:569
  36.1 1.8 %collective-permute-start.2 = (bf16[2,16,2304]{2,1,0:T(8,128)(2,1)S(1)}, bf16[2,16,2304]{2,1,0:T(8,128)(2,1)S(1)}, u32[]{:S(2)}, u32[]{:S(2)}) collective-permute-start(bf16[2,16,2304]{2,1,0:T(8,128)(2,1)S(1)} %get-tuple-element.32), channel_id=1, source_target_pairs={{0,12},{1,13},{2,14},{3,15},{4,8},{5,9},{6,10},{7,11},{8,4},{9,5},... | collective-permute-start | bytes 442376 | tf_op jit(solution)/shard_map/ppermute | solution.py:569
  37.8 1.7 %collective-permute-start.3 = (bf16[2,16,2304]{2,1,0:T(8,128)(2,1)S(1)}, bf16[2,16,2304]{2,1,0:T(8,128)(2,1)S(1)}, u32[]{:S(2)}, u32[]{:S(2)}) collective-permute-start(bf16[2,16,2304]{2,1,0:T(8,128)(2,1)S(1)} %get-tuple-element.33), channel_id=1, source_target_pairs={{0,10},{1,11},{2,8},{3,9},{4,14},{5,15},{6,12},{7,13},{8,2},{9,3},... | collective-permute-start | bytes 442376 | tf_op jit(solution)/shard_map/ppermute | solution.py:569
  39.6 0.9 %collective-permute-start.4 = (bf16[2,16,2304]{2,1,0:T(8,128)(2,1)S(1)}, bf16[2,16,2304]{2,1,0:T(8,128)(2,1)S(1)}, u32[]{:S(2)}, u32[]{:S(2)}) collective-permute-start(bf16[2,16,2304]{2,1,0:T(8,128)(2,1)S(1)} %get-tuple-element.34), channel_id=1, source_target_pairs={{0,6},{1,7},{2,4},{3,5},{4,2},{5,3},{6,0},{7,1},{8,14},{9,15},{10,... | collective-permute-start | bytes 442376 | tf_op jit(solution)/shard_map/ppermute | solution.py:569
  40.5 1.3 %collective-permute-start.5 = (bf16[2,16,2304]{2,1,0:T(8,128)(2,1)S(1)}, bf16[2,16,2304]{2,1,0:T(8,128)(2,1)S(1)}, u32[]{:S(2)}, u32[]{:S(2)}) collective-permute-start(bf16[2,16,2304]{2,1,0:T(8,128)(2,1)S(1)} %get-tuple-element.35), channel_id=1, source_target_pairs={{0,8},{1,9},{2,10},{3,11},{4,12},{5,13},{6,14},{7,15},{8,0},{9,1},... | collective-permute-start | bytes 442376 | tf_op jit(solution)/shard_map/ppermute | solution.py:569
  41.8 1.8 %collective-permute-done.1.refs_0_ = bf16[2,16,2304]{2,1,0:T(8,128)(2,1)S(1)} collective-permute-done((bf16[2,16,2304]{2,1,0:T(8,128)(2,1)S(1)}, bf16[2,16,2304]{2,1,0:T(8,128)(2,1)S(1)}, u32[]{:S(2)}, u32[]{:S(2)}) %collective-permute-start.1) | collective-permute-done | bytes 147488 | tf_op jit(solution)/shard_map/ppermute | solution.py:569
  43.6 0.7 collective-permute-start.6
  44.3 1.4 %collective-permute-done.2.refs_1_ = bf16[2,16,2304]{2,1,0:T(8,128)(2,1)S(1)} collective-permute-done((bf16[2,16,2304]{2,1,0:T(8,128)(2,1)S(1)}, bf16[2,16,2304]{2,1,0:T(8,128)(2,1)S(1)}, u32[]{:S(2)}, u32[]{:S(2)}) %collective-permute-start.2) | collective-permute-done | bytes 147488 | tf_op jit(solution)/shard_map/ppermute | solution.py:569
  45.7 1.5 %collective-permute-start.7 = (bf16[2,16,2304]{2,1,0:T(8,128)(2,1)S(1)}, bf16[2,16,2304]{2,1,0:T(8,128)(2,1)S(1)}, u32[]{:S(2)}, u32[]{:S(2)}) collective-permute-start(bf16[2,16,2304]{2,1,0:T(8,128)(2,1)S(1)} %get-tuple-element.37), channel_id=1, source_target_pairs={{0,2},{1,3},{2,0},{3,1},{4,6},{5,7},{6,4},{7,5},{8,10},{9,11},{10,... | collective-permute-start | bytes 442376 | tf_op jit(solution)/shard_map/ppermute | solution.py:569
  47.2 3.3 %collective-permute-done.3.refs_2_ = bf16[2,16,2304]{2,1,0:T(8,128)(2,1)S(1)} collective-permute-done((bf16[2,16,2304]{2,1,0:T(8,128)(2,1)S(1)}, bf16[2,16,2304]{2,1,0:T(8,128)(2,1)S(1)}, u32[]{:S(2)}, u32[]{:S(2)}) %collective-permute-start.3) | collective-permute-done | bytes 147488 | tf_op jit(solution)/shard_map/ppermute | solution.py:569
  50.5 0.7 collective-permute-done.4.refs_3_
  51.3 0.0 collective-permute-done.5.refs_4_
  51.3 1.5 %collective-permute-done.6.refs_5_ = bf16[2,16,2304]{2,1,0:T(8,128)(2,1)S(1)} collective-permute-done((bf16[2,16,2304]{2,1,0:T(8,128)(2,1)S(1)}, bf16[2,16,2304]{2,1,0:T(8,128)(2,1)S(1)}, u32[]{:S(2)}, u32[]{:S(2)}) %collective-permute-start.6) | collective-permute-done | bytes 147488 | tf_op jit(solution)/shard_map/ppermute | solution.py:569
  52.7 1.6 %collective-permute-done.7.refs_6_ = bf16[2,16,2304]{2,1,0:T(8,128)(2,1)S(1)} collective-permute-done((bf16[2,16,2304]{2,1,0:T(8,128)(2,1)S(1)}, bf16[2,16,2304]{2,1,0:T(8,128)(2,1)S(1)}, u32[]{:S(2)}, u32[]{:S(2)}) %collective-permute-start.7) | collective-permute-done | bytes 147488 | tf_op jit(solution)/shard_map/ppermute | solution.py:569
  54.3 0.1 halve_16.1
  54.5 12.2 %collective-permute-start.8 = (bf16[1,16,2304]{2,1,0:T(8,128)(2,1)S(1)}, bf16[1,16,2304]{2,1,0:T(8,128)(2,1)S(1)}, u32[]{:S(2)}, u32[]{:S(2)}) collective-permute-start(bf16[1,16,2304]{2,1,0:T(8,128)(2,1)S(1)} %get-tuple-element.40), channel_id=1, source_target_pairs={{0,16},{1,17},{2,18},{3,19},{4,20},{5,21},{6,22},{7,23},{8,24},{9,... | collective-permute-start | bytes 221192 | tf_op jit(solution)/shard_map/ppermute | solution.py:569
  66.6 4.0 %collective-permute-done.8.refs_0_ = bf16[1,16,2304]{2,1,0:T(8,128)(2,1)S(1)} collective-permute-done((bf16[1,16,2304]{2,1,0:T(8,128)(2,1)S(1)}, bf16[1,16,2304]{2,1,0:T(8,128)(2,1)S(1)}, u32[]{:S(2)}, u32[]{:S(2)}) %collective-permute-start.8) | collective-permute-done | bytes 73760 | tf_op jit(solution)/shard_map/ppermute | solution.py:569
  70.7 0.2 finish.1
  70.8 10.7 %all_to_all.10.payload = f32[32,1,128]{2,1,0:T(1,128)S(1)} all-to-all(f32[32,1,128]{2,1,0:T(1,128)S(1)} %get-tuple-element.42), channel_id=1, replica_groups=mesh['tile'=8,'dp'=4] {'tile','dp'}, dimensions={0} | all-to-all | bytes 32768 | tf_op jit(solution)/shard_map/all_to_all | solution.py:603
  81.6 0.8 scale.1
Async XLA Ops:
  2.9 15.7 %all-to-all-start = ((f32[32,1,1152]{2,1,0:T(1,128)}), f32[32,1,1152]{2,1,0:T(1,128)S(1)}, u32[]{:S(2)}, u32[]{:S(2)}) async-start(f32[32,1,1152]{2,1,0:T(1,128)} %pack.1), calls=%async_computation | async-start | bytes 294912 | tf_op jit(solution)/shard_map/all_to_all | solution.py:500
  31.8 2.9 %collective-permute-start = (bf16[16,16,2304]{2,1,0:T(8,128)(2,1)S(1)}, bf16[16,16,2304]{2,1,0:T(8,128)(2,1)S(1)}, u32[]{:S(2)}, u32[]{:S(2)}) collective-permute-start(bf16[16,16,2304]{2,1,0:T(8,128)(2,1)S(1)} %get-tuple-element.29), channel_id=1, source_target_pairs={{0,1},{1,0},{2,3},{3,2},{4,5},{5,4},{6,7},{7,6},{8,9},{9,8},{10,11... | collective-permute-start | bytes 3538952 | tf_op jit(solution)/shard_map/ppermute | solution.py:569
  34.9 8.6 %collective-permute-start.1 = (bf16[2,16,2304]{2,1,0:T(8,128)(2,1)S(1)}, bf16[2,16,2304]{2,1,0:T(8,128)(2,1)S(1)}, u32[]{:S(2)}, u32[]{:S(2)}) collective-permute-start(bf16[2,16,2304]{2,1,0:T(8,128)(2,1)S(1)} %get-tuple-element.31), channel_id=1, source_target_pairs={{0,14},{1,15},{2,12},{3,13},{4,10},{5,11},{6,8},{7,9},{8,6},{9,7},... | collective-permute-start | bytes 442376 | tf_op jit(solution)/shard_map/ppermute | solution.py:569
  36.1 9.6 %collective-permute-start.2 = (bf16[2,16,2304]{2,1,0:T(8,128)(2,1)S(1)}, bf16[2,16,2304]{2,1,0:T(8,128)(2,1)S(1)}, u32[]{:S(2)}, u32[]{:S(2)}) collective-permute-start(bf16[2,16,2304]{2,1,0:T(8,128)(2,1)S(1)} %get-tuple-element.32), channel_id=1, source_target_pairs={{0,12},{1,13},{2,14},{3,15},{4,8},{5,9},{6,10},{7,11},{8,4},{9,5},... | collective-permute-start | bytes 442376 | tf_op jit(solution)/shard_map/ppermute | solution.py:569
  37.8 12.7 %collective-permute-start.3 = (bf16[2,16,2304]{2,1,0:T(8,128)(2,1)S(1)}, bf16[2,16,2304]{2,1,0:T(8,128)(2,1)S(1)}, u32[]{:S(2)}, u32[]{:S(2)}) collective-permute-start(bf16[2,16,2304]{2,1,0:T(8,128)(2,1)S(1)} %get-tuple-element.33), channel_id=1, source_target_pairs={{0,10},{1,11},{2,8},{3,9},{4,14},{5,15},{6,12},{7,13},{8,2},{9,3},... | collective-permute-start | bytes 442376 | tf_op jit(solution)/shard_map/ppermute | solution.py:569
  39.6 11.7 %collective-permute-start.4 = (bf16[2,16,2304]{2,1,0:T(8,128)(2,1)S(1)}, bf16[2,16,2304]{2,1,0:T(8,128)(2,1)S(1)}, u32[]{:S(2)}, u32[]{:S(2)}) collective-permute-start(bf16[2,16,2304]{2,1,0:T(8,128)(2,1)S(1)} %get-tuple-element.34), channel_id=1, source_target_pairs={{0,6},{1,7},{2,4},{3,5},{4,2},{5,3},{6,0},{7,1},{8,14},{9,15},{10,... | collective-permute-start | bytes 442376 | tf_op jit(solution)/shard_map/ppermute | solution.py:569
  40.5 10.8 %collective-permute-start.5 = (bf16[2,16,2304]{2,1,0:T(8,128)(2,1)S(1)}, bf16[2,16,2304]{2,1,0:T(8,128)(2,1)S(1)}, u32[]{:S(2)}, u32[]{:S(2)}) collective-permute-start(bf16[2,16,2304]{2,1,0:T(8,128)(2,1)S(1)} %get-tuple-element.35), channel_id=1, source_target_pairs={{0,8},{1,9},{2,10},{3,11},{4,12},{5,13},{6,14},{7,15},{8,0},{9,1},... | collective-permute-start | bytes 442376 | tf_op jit(solution)/shard_map/ppermute | solution.py:569
  43.6 9.1 %collective-permute-start.6 = (bf16[2,16,2304]{2,1,0:T(8,128)(2,1)S(1)}, bf16[2,16,2304]{2,1,0:T(8,128)(2,1)S(1)}, u32[]{:S(2)}, u32[]{:S(2)}) collective-permute-start(bf16[2,16,2304]{2,1,0:T(8,128)(2,1)S(1)} %get-tuple-element.36), channel_id=1, source_target_pairs={{0,4},{1,5},{2,6},{3,7},{4,0},{5,1},{6,2},{7,3},{8,12},{9,13},{10,... | collective-permute-start | bytes 442376 | tf_op jit(solution)/shard_map/ppermute | solution.py:569
  45.7 8.6 %collective-permute-start.7 = (bf16[2,16,2304]{2,1,0:T(8,128)(2,1)S(1)}, bf16[2,16,2304]{2,1,0:T(8,128)(2,1)S(1)}, u32[]{:S(2)}, u32[]{:S(2)}) collective-permute-start(bf16[2,16,2304]{2,1,0:T(8,128)(2,1)S(1)} %get-tuple-element.37), channel_id=1, source_target_pairs={{0,2},{1,3},{2,0},{3,1},{4,6},{5,7},{6,4},{7,5},{8,10},{9,11},{10,... | collective-permute-start | bytes 442376 | tf_op jit(solution)/shard_map/ppermute | solution.py:569
  54.5 16.2 %collective-permute-start.8 = (bf16[1,16,2304]{2,1,0:T(8,128)(2,1)S(1)}, bf16[1,16,2304]{2,1,0:T(8,128)(2,1)S(1)}, u32[]{:S(2)}, u32[]{:S(2)}) collective-permute-start(bf16[1,16,2304]{2,1,0:T(8,128)(2,1)S(1)} %get-tuple-element.40), channel_id=1, source_target_pairs={{0,16},{1,17},{2,18},{3,19},{4,20},{5,21},{6,22},{7,23},{8,24},{9,... | collective-permute-start | bytes 221192 | tf_op jit(solution)/shard_map/ppermute | solution.py:569

commit v3 on v2

--- a/solution.py
+++ b/solution.py
@@ -69,19 +69,24 @@
         ref[base : base + CELLS - P_SIZE, lanes] = rows[P_SIZE:]
 
 
-def pack_kernel(owner, row, column, level, count, noise, line, drawn, sem):
-    copy = pltpu.make_async_copy(noise, drawn, sem)
-    copy.start()
-    npatch = noise.shape[0]
+def pack_kernel(*refs):
+    sources, line, scratch, sems = refs[:6], refs[6], refs[7:13], refs[13]
+    copies = [
+        pltpu.make_async_copy(src, dst, sems.at[at]) for at, (src, dst) in enumerate(zip(sources, scratch))
+    ]
+    for copy in copies:
+        copy.start()
+    *integers, drawn = scratch
+    npatch = drawn.shape[0]
     lane = lax.broadcasted_iota(jnp.int32, (1, C), 1)
     numbers = jnp.zeros((1, C), jnp.int32)
+    for copy in copies:
+        copy.wait()
     for patch in range(npatch):
-        values = (owner[patch], row[patch], column[patch], level[patch], count[patch])
-        for at, value in enumerate(values):
-            numbers = jnp.where(lane == patch * FIELDS + at, value, numbers)
+        for at, ref in enumerate(integers):
+            numbers = jnp.where(lane == patch * FIELDS + at, ref[patch], numbers)
     shape = (line.shape[0], 1, C)
     line[:, :, npatch * CELLS :] = jnp.broadcast_to(numbers.astype(F32)[None], shape)
-    copy.wait()
     rows = C // P_SIZE
     mine = lax.broadcasted_iota(jnp.int32, (rows, C), 0)
     here = lax.broadcasted_iota(jnp.int32, (rows, C), 1) // P_SIZE == mine
@@ -185,6 +190,8 @@
         (weight_back_hbm, weight_back),
     )
     copies = [pltpu.make_async_copy(src, dst, weight_sems.at[at]) for at, (src, dst) in enumerate(operands)]
+    for copy in copies:
+        copy.start()
     copy_ints.wait()
 
     tile_name = my_tile.astype(F32)
@@ -227,8 +234,6 @@
         return carry
 
     lax.fori_loop(0, count, start_block, 0)
-    for copy in copies:
-        copy.start()
 
     @pl.when(count == 0)
     def _():
@@ -261,7 +266,6 @@
     field_lane = lax.broadcasted_iota(jnp.int32, field_shape, 2)
     loss_row = lax.broadcasted_iota(jnp.int32, loss_out.shape, 0)
     loss_lane = lax.broadcasted_iota(jnp.int32, loss_out.shape, 1)
-    both_col = lax.broadcasted_iota(jnp.int32, (GROUP * CELLS, C), 0) & (P_SIZE - 1)
     log_step = (math.log(SIGMA_HIGH) - math.log(SIGMA_LOW)) / (LEVELS - 1)
 
     def prepare(part, slot):
@@ -335,69 +339,83 @@
             def _(part=part):
                 block_copy(used[part])[0].wait()
 
-        for part in range(GROUP):
-            prepare(part, used[part])
-        weights = []
-        for part in range(GROUP):
+        rows = [slice(part * CELLS, (part + 1) * CELLS) for part in range(GROUP)]
+
+        def first_layer(part):
+            return jnp.dot(win_a[rows[part]], weight_a[...], preferred_element_type=F32)
+
+        def activate(part, pre_a):
+            gate = sigmoid(pre_a)
+            act[rows[part]] = (pre_a * gate).astype(BF16)
+            slope[rows[part]] = gate * (1.0 + pre_a * (1.0 - gate))
+
+        def second_layer(part):
+            return jnp.dot(act[rows[part]], weight_b[...], preferred_element_type=F32)
+
+        def finish(part, product):
+            columns = []
+            for shift in range(3):
+                tap = [product[:, (3 * r + shift) * C : (3 * r + shift + 1) * C] for r in range(3)]
+                columns.append(from_previous_row(tap[0]) + tap[1] + from_next_row(tap[2]))
+            pre_b = (
+                ends[0:1]
+                + from_previous_column(columns[0], cell_col)
+                + columns[1]
+                + from_next_column(columns[2], cell_col)
+            )
+            gate = sigmoid(pre_b)
+            final = jnp.sum(pre_b * gate * ends[1:2], axis=1, keepdims=True)
+            residual = final - aim[rows[part]]
             device, inner = fields(used[part])
-            weight = ints[device, inner * FIELDS + 4]
-            weights.append(jnp.where(real[part], weight, 0.0))
-
-        for at in range(0, HID, 256):
-            lanes = slice(at, at + 256)
-            pre_a = jnp.dot(win_a[...], weight_a[:, lanes], preferred_element_type=F32)
-            gate = sigmoid(pre_a)
-            act[:, lanes] = (pre_a * gate).astype(BF16)
-            slope[:, lanes] = gate * (1.0 + pre_a * (1.0 - gate))
-
-        product = jnp.dot(act[...], weight_b[...], preferred_element_type=F32)
-        columns = []
-        for shift in range(3):
-            tap = [product[:, (3 * r + shift) * C : (3 * r + shift + 1) * C] for r in range(3)]
-            columns.append(from_previous_row(tap[0]) + tap[1] + from_next_row(tap[2]))
-        pre_b = (
-            ends[0:1]
-            + from_previous_column(columns[0], both_col)
-            + columns[1]
-            + from_next_column(columns[2], both_col)
-        )
-        gate = sigmoid(pre_b)
-        final = jnp.sum(pre_b * gate * ends[1:2], axis=1, keepdims=True)
-        residual = final - aim[...]
-        factors = []
-        for part in range(GROUP):
-            base = part * CELLS
-            mine = residual[base : base + CELLS]
-            loss = weights[part] * jnp.sum(mine * mine) * (1.0 / (CELLS * C))
-            device, inner = fields(used[part])
+            weight = jnp.where(real[part], ints[device, inner * FIELDS + 4], 0.0)
+            loss = weight * jnp.sum(residual * residual) * (1.0 / (CELLS * C))
             spot = jnp.logical_and(loss_row == device, loss_lane == inner)
             loss_out[...] += jnp.where(spot, loss, 0.0)
-            factors.append((2.0 / CELLS) * weights[part] * mine)
-        factor = jnp.concatenate(factors, axis=0)
-        grad_pre_b = factor * ends[1:2] * (gate * (1.0 + pre_b * (1.0 - gate)))
-        for shift, value in enumerate(
-            (from_next_column(grad_pre_b, both_col), grad_pre_b, from_previous_column(grad_pre_b, both_col))
-        ):
-            value = value.astype(BF16)
-            for part in range(GROUP):
-                mine = value[part * CELLS : (part + 1) * CELLS]
+            factor = (2.0 / CELLS) * weight * residual
+            grad_pre_b = factor * ends[1:2] * (gate * (1.0 + pre_b * (1.0 - gate)))
+            base = part * CELLS
+            for shift, value in enumerate(
+                (
+                    from_next_column(grad_pre_b, cell_col),
+                    grad_pre_b,
+                    from_previous_column(grad_pre_b, cell_col),
+                )
+            ):
+                value = value.astype(BF16)
                 for shift_row in range(3):
                     lanes = pl.ds((3 * shift_row + shift) * C, C)
-                    base = part * CELLS
                     if shift_row == 0:
-                        win_g[base : base + CELLS - P_SIZE, lanes] = mine[P_SIZE:]
+                        win_g[base : base + CELLS - P_SIZE, lanes] = value[P_SIZE:]
                     elif shift_row == 1:
-                        win_g[base : base + CELLS, lanes] = mine
+                        win_g[base : base + CELLS, lanes] = value
                     else:
-                        win_g[base + P_SIZE : base + CELLS, lanes] = mine[: CELLS - P_SIZE]
-
+                        win_g[base + P_SIZE : base + CELLS, lanes] = value[: CELLS - P_SIZE]
+
+        def hidden(part):
+            return jnp.dot(win_g[rows[part]], weight_back[...], preferred_element_type=F32)
+
+        def turn_back(part, grad_hidden):
+            return (grad_hidden * slope[rows[part]]).astype(BF16)
+
+        prepare(0, used[0])
+        pre_0 = first_layer(0)
+        prepare(1, used[1])
+        pre_1 = first_layer(1)
+        activate(0, pre_0)
+        product_0 = second_layer(0)
+        activate(1, pre_1)
+        product_1 = second_layer(1)
+        finish(0, product_0)
+        hidden_0 = hidden(0)
+        finish(1, product_1)
+        hidden_1 = hidden(1)
+        back_0 = turn_back(0, hidden_0)
+        started = step > 0
         over_cells = (((0,), (0,)), ((), ()))
-        started = step > 0
         grad_b[...] = jnp.where(started, grad_b[...], 0.0) + lax.dot_general(
             act[...], win_g[...], over_cells, preferred_element_type=F32
         )
-        grad_hidden = jnp.dot(win_g[...], weight_back[...], preferred_element_type=F32)
-        grad_pre_a = (grad_hidden * slope[...]).astype(BF16)
+        grad_pre_a = jnp.concatenate([back_0, turn_back(1, hidden_1)], axis=0)
         grad_a[...] = jnp.where(started, grad_a[...], 0.0) + lax.dot_general(
             grad_pre_a, win_a[:, : taps * C], over_cells, preferred_element_type=F32
         )
@@ -489,9 +507,13 @@
     line = pl.pallas_call(
         pack_kernel,
         out_shape=jax.ShapeDtypeStruct((devices, 1, npatch * CELLS + C), F32),
-        in_specs=[in_smem] * 5 + [in_hbm],
+        in_specs=[in_hbm] * 6,
         out_specs=in_vmem,
-        scratch_shapes=[pltpu.VMEM(noise_draw.shape, F32), pltpu.SemaphoreType.DMA],
+        scratch_shapes=[
+            *[pltpu.SMEM((npatch,), jnp.int32)] * 5,
+            pltpu.VMEM(noise_draw.shape, F32),
+            pltpu.SemaphoreType.DMA((6,)),
+        ],
         compiler_params=room(4),
         name="pack",
     )(
@@ -585,8 +607,7 @@
             name=f"halve_{step}",
         )(keep, *received)
         keep = outs[0]
-        order = sorted(range(1, fan), key=lambda peer: (-peer.bit_count(), -peer))
-        received = [exchange(outs[peer], peer * step) for peer in order]
+        received = [exchange(outs[peer], peer * step) for peer in range(1, fan)]
         step *= fan
 
     grad, payload = pl.pallas_call(

time: 82.7 us -> 79.7 us (0.964)
  blocking collectives: 10.7 us -> 13.9 us
  Pallas kernels: 20.9 us -> 18.2 us
  waiting for transfers between devices: 21.1 us -> 19.4 us
  starting transfers between devices: 29 us -> 27.5 us
    all_to_all x1, blocking collectives: 10.7 us -> 13.9 us  [local(): lax.all_to_all(payload, AXES, split_axis=0, concat_axis=0, tiled=True)]
    pallas_call x1, Pallas kernels: 13.1 us -> 11 us  [local(): pl.pallas_call(functools.partial(train_kernel, dp_count, npatch), out_sha...]
    ppermute x9, waiting for transfers between devices: 16.8 us -> 15.1 us  [exchange(): lax.ppermute(array, AXES, [(i, i ^ distance) for i in range(devices)])]
    ppermute x9, starting transfers between devices: 21.7 us -> 20.2 us  [exchange(): lax.ppermute(array, AXES, [(i, i ^ distance) for i in range(devices)])]
where the time goes in v3:
time: 79.7 us
  starting transfers between devices  27.5 us (35%)
  waiting for transfers between devices  19.4 us (24%)
  Pallas kernels  18.2 us (23%)
  blocking collectives  13.9 us (17%)
    ppermute x9, starting transfers between devices, exchange(): lax.ppermute(array, AXES, [(i, i ^ distance) for i in range(devices)])  20.2 us
    ppermute x9, waiting for transfers between devices, exchange(): lax.ppermute(array, AXES, [(i, i ^ distance) for i in range(devices)])  15.1 us
    all_to_all x1, blocking collectives, local(): lax.all_to_all(payload, AXES, split_axis=0, concat_axis=0, tiled=True)  13.9 us
    pallas_call x1, Pallas kernels, local(): pl.pallas_call(functools.partial(train_kernel, dp_count, npatch), out_sha...  11 us
    all_to_all x1, starting transfers between devices, local(): table = lax.all_to_all(line, AXES, split_axis=0, concat_axis=0, tiled=True)  7.3 us
    all_to_all x1, waiting for transfers between devices, local(): table = lax.all_to_all(line, AXES, split_axis=0, concat_axis=0, tiled=True)  4.24 us
    pallas_call x1, Pallas kernels, local(): pl.pallas_call(weights_kernel, out_shape=(pltpu.HBM((10 * C, HID), BF16),...  4.17 us
    pallas_call x1, Pallas kernels, local(): pl.pallas_call(pack_kernel, out_shape=jax.ShapeDtypeStruct((devices, 1, n...  1.65 us
  transfers between devices with their start and end apart: 10, of which 9 were waited for; matrix products, arithmetic and copies ran while one was open for 0% of the time, Pallas kernels for 5%

profile of v3, /device:TPU:0, one launch (start us, length us, event | category | flops | bytes accessed | tf_op | source)
XLA Modules:
  0.0 79.7 jit_solution(17511944177658339537)
XLA Ops:
  0.6 1.6 %pack.1 = f32[32,1,1152]{2,1,0:T(1,128)} custom-call(s32[4]{0:T(128)} %bitcast.7, s32[4]{0:T(128)} %refs_1_.1, s32[4]{0:T(128)} %refs_2_.1, s32[4]{0:T(128)} %refs_3_.1, s32[4]{0:T(128)} %refs_4_.1, f32[4,16,16]{2,1,0:T(8,128)} %refs_5_.1), custom_call_target="tpu_custom_call" | custom-call | tf_op jit(solution)/shard_map/pack/pallas_call | solution.py:507
  2.3 7.3 %all-to-all-start = ((f32[32,1,1152]{2,1,0:T(1,128)}), f32[32,1,1152]{2,1,0:T(1,128)S(1)}, u32[]{:S(2)}, u32[]{:S(2)}) async-start(f32[32,1,1152]{2,1,0:T(1,128)} %pack.1), calls=%async_computation | async-start | bytes 294912 | tf_op jit(solution)/shard_map/all_to_all | solution.py:522
  9.6 4.2 %weights.1 = (bf16[1280,512]{1,0:T(8,128)(2,1)}, bf16[512,1152]{1,0:T(8,128)(2,1)}, bf16[1152,512]{1,0:T(8,128)(2,1)}, f32[2,128]{1,0:T(2,128)}, f32[64,256]{1,0:T(8,128)}) custom-call(bf16[1152,512]{1,0:T(8,128)(2,1)} %w_a.1, f32[9,512]{1,0:T(8,128)} %w_u.1, f32[1,512]{1,0:T(1,128)} %bitcast.5, f32[1,512]{1,0:T(1,128)} %bitcast.6, bf16[4608,128]{1,0:T(8,128)(2,1)} %w_b.1, ...), custom_call_target="tpu_custom_call" | custom-call | tf_op jit(solution)/shard_map/weights/pallas_call | solution.py:524
  13.8 4.2 %all-to-all-done.table_hbm.table = f32[32,1,1152]{2,1,0:T(1,128)S(1)} async-done(((f32[32,1,1152]{2,1,0:T(1,128)}), f32[32,1,1152]{2,1,0:T(1,128)S(1)}, u32[]{:S(2)}, u32[]{:S(2)}) %all-to-all-start) | async-done | bytes 147488 | tf_op jit(solution)/shard_map/all_to_all | solution.py:522
  18.0 11.0 %train.1 = (f32[16,16,2304]{2,1,0:T(8,128)S(1)}, bf16[16,16,2304]{2,1,0:T(8,128)(2,1)S(1)}, f32[32,128]{1,0:T(8,128)S(1)}) custom-call(f32[32,1,1152]{2,1,0:T(1,128)S(1)} %all-to-all-done.table_hbm.table, f32[32,1,1152]{2,1,0:T(1,128)S(1)} %all-to-all-done.table_hbm.table, bf16[64,256,128]{2,1,0:T(8,128)(2,1)} %features.1, ...), custom_call_target="tpu_custom_call" | custom-call | tf_op jit(solution)/shard_map/train/pallas_call | solution.py:557
  29.1 0.4 collective-permute-start
  29.4 2.5 %collective-permute-done.refs_0_ = bf16[16,16,2304]{2,1,0:T(8,128)(2,1)S(1)} collective-permute-done((bf16[16,16,2304]{2,1,0:T(8,128)(2,1)S(1)}, bf16[16,16,2304]{2,1,0:T(8,128)(2,1)S(1)}, u32[]{:S(2)}, u32[]{:S(2)}) %collective-permute-start) | collective-permute-done | bytes 1179680 | tf_op jit(solution)/shard_map/ppermute | solution.py:591
  32.0 0.2 halve_2.1
  32.2 0.6 collective-permute-start.1
  32.8 0.9 %collective-permute-start.2 = (bf16[2,16,2304]{2,1,0:T(8,128)(2,1)S(1)}, bf16[2,16,2304]{2,1,0:T(8,128)(2,1)S(1)}, u32[]{:S(2)}, u32[]{:S(2)}) collective-permute-start(bf16[2,16,2304]{2,1,0:T(8,128)(2,1)S(1)} %get-tuple-element.32), channel_id=1, source_target_pairs={{0,4},{1,5},{2,6},{3,7},{4,0},{5,1},{6,2},{7,3},{8,12},{9,13},{10,... | collective-permute-start | bytes 442376 | tf_op jit(solution)/shard_map/ppermute | solution.py:591
  33.8 2.0 %collective-permute-start.3 = (bf16[2,16,2304]{2,1,0:T(8,128)(2,1)S(1)}, bf16[2,16,2304]{2,1,0:T(8,128)(2,1)S(1)}, u32[]{:S(2)}, u32[]{:S(2)}) collective-permute-start(bf16[2,16,2304]{2,1,0:T(8,128)(2,1)S(1)} %get-tuple-element.33), channel_id=1, source_target_pairs={{0,6},{1,7},{2,4},{3,5},{4,2},{5,3},{6,0},{7,1},{8,14},{9,15},{10,... | collective-permute-start | bytes 442376 | tf_op jit(solution)/shard_map/ppermute | solution.py:591
  35.8 0.7 collective-permute-start.4
  36.5 1.3 %collective-permute-start.5 = (bf16[2,16,2304]{2,1,0:T(8,128)(2,1)S(1)}, bf16[2,16,2304]{2,1,0:T(8,128)(2,1)S(1)}, u32[]{:S(2)}, u32[]{:S(2)}) collective-permute-start(bf16[2,16,2304]{2,1,0:T(8,128)(2,1)S(1)} %get-tuple-element.35), channel_id=1, source_target_pairs={{0,10},{1,11},{2,8},{3,9},{4,14},{5,15},{6,12},{7,13},{8,2},{9,3},... | collective-permute-start | bytes 442376 | tf_op jit(solution)/shard_map/ppermute | solution.py:591
  37.8 0.5 collective-permute-done.1.refs_0_
  38.3 0.6 collective-permute-start.6
  39.0 0.6 collective-permute-done.2.refs_1_
  39.6 2.0 %collective-permute-start.7 = (bf16[2,16,2304]{2,1,0:T(8,128)(2,1)S(1)}, bf16[2,16,2304]{2,1,0:T(8,128)(2,1)S(1)}, u32[]{:S(2)}, u32[]{:S(2)}) collective-permute-start(bf16[2,16,2304]{2,1,0:T(8,128)(2,1)S(1)} %get-tuple-element.37), channel_id=1, source_target_pairs={{0,14},{1,15},{2,12},{3,13},{4,10},{5,11},{6,8},{7,9},{8,6},{9,7},... | collective-permute-start | bytes 442376 | tf_op jit(solution)/shard_map/ppermute | solution.py:591
  41.6 2.6 %collective-permute-done.3.refs_2_ = bf16[2,16,2304]{2,1,0:T(8,128)(2,1)S(1)} collective-permute-done((bf16[2,16,2304]{2,1,0:T(8,128)(2,1)S(1)}, bf16[2,16,2304]{2,1,0:T(8,128)(2,1)S(1)}, u32[]{:S(2)}, u32[]{:S(2)}) %collective-permute-start.3) | collective-permute-done | bytes 147488 | tf_op jit(solution)/shard_map/ppermute | solution.py:591
  44.2 0.0 collective-permute-done.4.refs_3_
  44.2 1.6 %collective-permute-done.5.refs_4_ = bf16[2,16,2304]{2,1,0:T(8,128)(2,1)S(1)} collective-permute-done((bf16[2,16,2304]{2,1,0:T(8,128)(2,1)S(1)}, bf16[2,16,2304]{2,1,0:T(8,128)(2,1)S(1)}, u32[]{:S(2)}, u32[]{:S(2)}) %collective-permute-start.5) | collective-permute-done | bytes 147488 | tf_op jit(solution)/shard_map/ppermute | solution.py:591
  45.7 3.2 %collective-permute-done.6.refs_5_ = bf16[2,16,2304]{2,1,0:T(8,128)(2,1)S(1)} collective-permute-done((bf16[2,16,2304]{2,1,0:T(8,128)(2,1)S(1)}, bf16[2,16,2304]{2,1,0:T(8,128)(2,1)S(1)}, u32[]{:S(2)}, u32[]{:S(2)}) %collective-permute-start.6) | collective-permute-done | bytes 147488 | tf_op jit(solution)/shard_map/ppermute | solution.py:591
  48.9 1.8 %collective-permute-done.7.refs_6_ = bf16[2,16,2304]{2,1,0:T(8,128)(2,1)S(1)} collective-permute-done((bf16[2,16,2304]{2,1,0:T(8,128)(2,1)S(1)}, bf16[2,16,2304]{2,1,0:T(8,128)(2,1)S(1)}, u32[]{:S(2)}, u32[]{:S(2)}) %collective-permute-start.7) | collective-permute-done | bytes 147488 | tf_op jit(solution)/shard_map/ppermute | solution.py:591
  50.7 0.1 halve_16.1
  50.8 11.6 %collective-permute-start.8 = (bf16[1,16,2304]{2,1,0:T(8,128)(2,1)S(1)}, bf16[1,16,2304]{2,1,0:T(8,128)(2,1)S(1)}, u32[]{:S(2)}, u32[]{:S(2)}) collective-permute-start(bf16[1,16,2304]{2,1,0:T(8,128)(2,1)S(1)} %get-tuple-element.40), channel_id=1, source_target_pairs={{0,16},{1,17},{2,18},{3,19},{4,20},{5,21},{6,22},{7,23},{8,24},{9,... | collective-permute-start | bytes 221192 | tf_op jit(solution)/shard_map/ppermute | solution.py:591
  62.4 2.4 %collective-permute-done.8.refs_0_ = bf16[1,16,2304]{2,1,0:T(8,128)(2,1)S(1)} collective-permute-done((bf16[1,16,2304]{2,1,0:T(8,128)(2,1)S(1)}, bf16[1,16,2304]{2,1,0:T(8,128)(2,1)S(1)}, u32[]{:S(2)}, u32[]{:S(2)}) %collective-permute-start.8) | collective-permute-done | bytes 73760 | tf_op jit(solution)/shard_map/ppermute | solution.py:591
  64.8 0.2 finish.1
  65.0 13.9 %all_to_all.10.payload = f32[32,1,128]{2,1,0:T(1,128)S(1)} all-to-all(f32[32,1,128]{2,1,0:T(1,128)S(1)} %get-tuple-element.42), channel_id=1, replica_groups=mesh['tile'=8,'dp'=4] {'tile','dp'}, dimensions={0} | all-to-all | bytes 32768 | tf_op jit(solution)/shard_map/all_to_all | solution.py:624
  78.9 0.8 scale.1
Async XLA Ops:
  2.3 15.7 %all-to-all-start = ((f32[32,1,1152]{2,1,0:T(1,128)}), f32[32,1,1152]{2,1,0:T(1,128)S(1)}, u32[]{:S(2)}, u32[]{:S(2)}) async-start(f32[32,1,1152]{2,1,0:T(1,128)} %pack.1), calls=%async_computation | async-start | bytes 294912 | tf_op jit(solution)/shard_map/all_to_all | solution.py:522
  29.1 2.9 %collective-permute-start = (bf16[16,16,2304]{2,1,0:T(8,128)(2,1)S(1)}, bf16[16,16,2304]{2,1,0:T(8,128)(2,1)S(1)}, u32[]{:S(2)}, u32[]{:S(2)}) collective-permute-start(bf16[16,16,2304]{2,1,0:T(8,128)(2,1)S(1)} %get-tuple-element.29), channel_id=1, source_target_pairs={{0,1},{1,0},{2,3},{3,2},{4,5},{5,4},{6,7},{7,6},{8,9},{9,8},{10,11... | collective-permute-start | bytes 3538952 | tf_op jit(solution)/shard_map/ppermute | solution.py:591
  32.2 6.1 %collective-permute-start.1 = (bf16[2,16,2304]{2,1,0:T(8,128)(2,1)S(1)}, bf16[2,16,2304]{2,1,0:T(8,128)(2,1)S(1)}, u32[]{:S(2)}, u32[]{:S(2)}) collective-permute-start(bf16[2,16,2304]{2,1,0:T(8,128)(2,1)S(1)} %get-tuple-element.31), channel_id=1, source_target_pairs={{0,2},{1,3},{2,0},{3,1},{4,6},{5,7},{6,4},{7,5},{8,10},{9,11},{10,... | collective-permute-start | bytes 442376 | tf_op jit(solution)/shard_map/ppermute | solution.py:591
  32.8 6.7 %collective-permute-start.2 = (bf16[2,16,2304]{2,1,0:T(8,128)(2,1)S(1)}, bf16[2,16,2304]{2,1,0:T(8,128)(2,1)S(1)}, u32[]{:S(2)}, u32[]{:S(2)}) collective-permute-start(bf16[2,16,2304]{2,1,0:T(8,128)(2,1)S(1)} %get-tuple-element.32), channel_id=1, source_target_pairs={{0,4},{1,5},{2,6},{3,7},{4,0},{5,1},{6,2},{7,3},{8,12},{9,13},{10,... | collective-permute-start | bytes 442376 | tf_op jit(solution)/shard_map/ppermute | solution.py:591
  33.8 10.4 %collective-permute-start.3 = (bf16[2,16,2304]{2,1,0:T(8,128)(2,1)S(1)}, bf16[2,16,2304]{2,1,0:T(8,128)(2,1)S(1)}, u32[]{:S(2)}, u32[]{:S(2)}) collective-permute-start(bf16[2,16,2304]{2,1,0:T(8,128)(2,1)S(1)} %get-tuple-element.33), channel_id=1, source_target_pairs={{0,6},{1,7},{2,4},{3,5},{4,2},{5,3},{6,0},{7,1},{8,14},{9,15},{10,... | collective-permute-start | bytes 442376 | tf_op jit(solution)/shard_map/ppermute | solution.py:591
  35.8 8.4 %collective-permute-start.4 = (bf16[2,16,2304]{2,1,0:T(8,128)(2,1)S(1)}, bf16[2,16,2304]{2,1,0:T(8,128)(2,1)S(1)}, u32[]{:S(2)}, u32[]{:S(2)}) collective-permute-start(bf16[2,16,2304]{2,1,0:T(8,128)(2,1)S(1)} %get-tuple-element.34), channel_id=1, source_target_pairs={{0,8},{1,9},{2,10},{3,11},{4,12},{5,13},{6,14},{7,15},{8,0},{9,1},... | collective-permute-start | bytes 442376 | tf_op jit(solution)/shard_map/ppermute | solution.py:591
  36.5 9.3 %collective-permute-start.5 = (bf16[2,16,2304]{2,1,0:T(8,128)(2,1)S(1)}, bf16[2,16,2304]{2,1,0:T(8,128)(2,1)S(1)}, u32[]{:S(2)}, u32[]{:S(2)}) collective-permute-start(bf16[2,16,2304]{2,1,0:T(8,128)(2,1)S(1)} %get-tuple-element.35), channel_id=1, source_target_pairs={{0,10},{1,11},{2,8},{3,9},{4,14},{5,15},{6,12},{7,13},{8,2},{9,3},... | collective-permute-start | bytes 442376 | tf_op jit(solution)/shard_map/ppermute | solution.py:591
  38.3 10.6 %collective-permute-start.6 = (bf16[2,16,2304]{2,1,0:T(8,128)(2,1)S(1)}, bf16[2,16,2304]{2,1,0:T(8,128)(2,1)S(1)}, u32[]{:S(2)}, u32[]{:S(2)}) collective-permute-start(bf16[2,16,2304]{2,1,0:T(8,128)(2,1)S(1)} %get-tuple-element.36), channel_id=1, source_target_pairs={{0,12},{1,13},{2,14},{3,15},{4,8},{5,9},{6,10},{7,11},{8,4},{9,5},... | collective-permute-start | bytes 442376 | tf_op jit(solution)/shard_map/ppermute | solution.py:591
  39.6 11.1 %collective-permute-start.7 = (bf16[2,16,2304]{2,1,0:T(8,128)(2,1)S(1)}, bf16[2,16,2304]{2,1,0:T(8,128)(2,1)S(1)}, u32[]{:S(2)}, u32[]{:S(2)}) collective-permute-start(bf16[2,16,2304]{2,1,0:T(8,128)(2,1)S(1)} %get-tuple-element.37), channel_id=1, source_target_pairs={{0,14},{1,15},{2,12},{3,13},{4,10},{5,11},{6,8},{7,9},{8,6},{9,7},... | collective-permute-start | bytes 442376 | tf_op jit(solution)/shard_map/ppermute | solution.py:591
  50.8 14.0 %collective-permute-start.8 = (bf16[1,16,2304]{2,1,0:T(8,128)(2,1)S(1)}, bf16[1,16,2304]{2,1,0:T(8,128)(2,1)S(1)}, u32[]{:S(2)}, u32[]{:S(2)}) collective-permute-start(bf16[1,16,2304]{2,1,0:T(8,128)(2,1)S(1)} %get-tuple-element.40), channel_id=1, source_target_pairs={{0,16},{1,17},{2,18},{3,19},{4,20},{5,21},{6,22},{7,23},{8,24},{9,... | collective-permute-start | bytes 221192 | tf_op jit(solution)/shard_map/ppermute | solution.py:591

commit v4 on v3

--- a/solution.py
+++ b/solution.py
@@ -170,6 +170,7 @@
     aim,
     grad_a,
     grad_b,
+    tails,
     int_sem,
     weight_sems,
     block_sems,
@@ -207,7 +208,6 @@
             turn = jnp.where(owned, following, turn)
         return turn, place_at
 
-    _, count = lax.fori_loop(0, devices, choose, (jnp.int32(0), jnp.int32(0)))
 
     def fields(slot):
         patch = chosen[slot]
@@ -233,12 +233,18 @@
         block_copy(slot)[0].start()
         return carry
 
-    lax.fori_loop(0, count, start_block, 0)
+    turn, count = jnp.int32(0), jnp.int32(0)
+    stops = [0, devices // 4, devices // 2, devices]
+    for begin, end in zip(stops, stops[1:]):
+        known = count
+        turn, count = lax.fori_loop(begin, end, choose, (turn, known))
+        lax.fori_loop(known, count, start_block, 0)
 
     @pl.when(count == 0)
     def _():
         grad_a[...] = jnp.zeros_like(grad_a)
         grad_b[...] = jnp.zeros_like(grad_b)
+        tails[...] = jnp.zeros_like(tails)
 
     loss_out[...] = jnp.zeros_like(loss_out)
     edge = jnp.zeros((P_SIZE, 3 * C), BF16)
@@ -257,6 +263,7 @@
     lane_tap = lax.rem(lane, taps)
     lane_row, lane_col = lax.div(lane_tap, 3), lax.rem(lane_tap, 3)
     pick_shape = (P_SIZE, P_SIZE, C)
+    tile_line = lax.broadcasted_iota(jnp.int32, (P_SIZE * SPAN // 8, 8, C), 1)
     pick_row = lax.broadcasted_iota(jnp.int32, pick_shape, 0) & 7
     pick_col = lax.broadcasted_iota(jnp.int32, pick_shape, 1)
     pick_lane = lax.broadcasted_iota(jnp.int32, pick_shape, 2)
@@ -275,9 +282,17 @@
         column = ints[device, inner * FIELDS + 2].astype(jnp.int32)
         level = ints[device, inner * FIELDS + 3]
 
-        span = blocks[slot].astype(F32).reshape(P_SIZE * SPAN, C)
-        span = pltpu.roll(span, (P_SIZE * SPAN - offset) & (P_SIZE * SPAN - 1), 0).reshape(P_SIZE, SPAN, C)
-        block = span[:, :P_SIZE, :].reshape(CELLS, C)
+        tiles = blocks[slot].astype(F32).reshape(P_SIZE * SPAN // 8, 8, C)
+        within = offset & 7
+        turned = pltpu.roll(tiles, (8 - within) & 7, 1)
+        after = jnp.concatenate([turned[1:], turned[:1]], axis=0)
+        tiles = jnp.where(tile_line + within < 8, turned, after).reshape(P_SIZE, SPAN // 8, 8, C)
+        whole_tiles = lax.shift_right_logical(offset, 3)
+        block = jnp.where(
+            whole_tiles == 0,
+            tiles[:, 0:2],
+            jnp.where(whole_tiles == 1, tiles[:, 1:3], tiles[:, 2:4]),
+        ).reshape(CELLS, C)
         for shift, value in enumerate(
             (from_previous_column(block, cell_col), block, from_next_column(block, cell_col))
         ):
@@ -412,16 +427,24 @@
         back_0 = turn_back(0, hidden_0)
         started = step > 0
         over_cells = (((0,), (0,)), ((), ()))
-        grad_b[...] = jnp.where(started, grad_b[...], 0.0) + lax.dot_general(
-            act[...], win_g[...], over_cells, preferred_element_type=F32
-        )
-        grad_pre_a = jnp.concatenate([back_0, turn_back(1, hidden_1)], axis=0)
-        grad_a[...] = jnp.where(started, grad_a[...], 0.0) + lax.dot_general(
-            grad_pre_a, win_a[:, : taps * C], over_cells, preferred_element_type=F32
-        )
+
+        def add(at, grad, rows_of, columns_of):
+            wide = columns_of[:, : 8 * C]
+            grad[:, : 8 * C] = jnp.where(started, grad[:, : 8 * C], 0.0) + lax.dot_general(
+                rows_of, wide, over_cells, preferred_element_type=F32
+            )
+            last = columns_of[:, 8 * C : 9 * C]
+            tails[at] = jnp.where(started, tails[at], 0.0) + lax.dot_general(
+                last, rows_of, over_cells, preferred_element_type=F32
+            )
+
+        add(1, grad_b, act[...], win_g)
+        add(0, grad_a, jnp.concatenate([back_0, turn_back(1, hidden_1)], axis=0), win_a)
         return carry
 
     lax.fori_loop(0, lax.div(count + GROUP - 1, GROUP), work, 0)
+    grad_a[:, 8 * C :] = tails[0].T
+    grad_b[:, 8 * C :] = tails[1].T
 
     chunk = HID // devices
     for pair in range(devices // 2):
@@ -579,6 +602,7 @@
             pltpu.VMEM((GROUP * CELLS, C), F32),
             pltpu.VMEM((HID, 9 * C), F32),
             pltpu.VMEM((HID, 9 * C), F32),
+            pltpu.VMEM((2, C, HID), F32),
             pltpu.SemaphoreType.DMA,
             pltpu.SemaphoreType.DMA((5,)),
             pltpu.SemaphoreType.DMA((slots,)),

time: 79.7 us -> 78.1 us (0.980)
  blocking collectives: 13.9 us -> 12.6 us
    all_to_all x1, blocking collectives: 13.9 us -> 12.6 us  [local(): lax.all_to_all(payload, AXES, split_axis=0, concat_axis=0, tiled=True)]
where the time goes in v4:
time: 78.1 us; the launch traced here: 77.8 us
  starting transfers between devices  27.7 us (35%)
  waiting for transfers between devices  19.1 us (24%)
  Pallas kernels  17.6 us (23%)
  blocking collectives  12.6 us (16%)
    ppermute x9, starting transfers between devices, exchange(): lax.ppermute(array, AXES, [(i, i ^ distance) for i in range(devices)])  20.4 us
    ppermute x9, waiting for transfers between devices, exchange(): lax.ppermute(array, AXES, [(i, i ^ distance) for i in range(devices)])  14.9 us
    all_to_all x1, blocking collectives, local(): lax.all_to_all(payload, AXES, split_axis=0, concat_axis=0, tiled=True)  12.6 us
    pallas_call x1, Pallas kernels, local(): pl.pallas_call(functools.partial(train_kernel, dp_count, npatch), out_sha...  10.5 us
    all_to_all x1, starting transfers between devices, local(): table = lax.all_to_all(line, AXES, split_axis=0, concat_axis=0, tiled=True)  7.3 us
    all_to_all x1, waiting for transfers between devices, local(): table = lax.all_to_all(line, AXES, split_axis=0, concat_axis=0, tiled=True)  4.24 us
    pallas_call x1, Pallas kernels, local(): pl.pallas_call(weights_kernel, out_shape=(pltpu.HBM((10 * C, HID), BF16),...  4.17 us
    pallas_call x1, Pallas kernels, local(): pl.pallas_call(pack_kernel, out_shape=jax.ShapeDtypeStruct((devices, 1, n...  1.65 us
  transfers between devices with their start and end apart: 10, of which 9 were waited for; matrix products, arithmetic and copies ran while one was open for 0% of the time, Pallas kernels for 5%

profile of v4, /device:TPU:0, one launch (start us, length us, event | category | flops | bytes accessed | tf_op | source)
XLA Modules:
  0.0 77.8 jit_solution(16555233735790911689)
XLA Ops:
  0.6 1.6 %pack.1 = f32[32,1,1152]{2,1,0:T(1,128)} custom-call(s32[4]{0:T(128)} %bitcast.7, s32[4]{0:T(128)} %refs_1_.1, s32[4]{0:T(128)} %refs_2_.1, s32[4]{0:T(128)} %refs_3_.1, s32[4]{0:T(128)} %refs_4_.1, f32[4,16,16]{2,1,0:T(8,128)} %refs_5_.1), custom_call_target="tpu_custom_call" | custom-call | tf_op jit(solution)/shard_map/pack/pallas_call | solution.py:530
  2.3 7.3 %all-to-all-start = ((f32[32,1,1152]{2,1,0:T(1,128)}), f32[32,1,1152]{2,1,0:T(1,128)S(1)}, u32[]{:S(2)}, u32[]{:S(2)}) async-start(f32[32,1,1152]{2,1,0:T(1,128)} %pack.1), calls=%async_computation | async-start | bytes 294912 | tf_op jit(solution)/shard_map/all_to_all | solution.py:545
  9.6 4.2 %weights.1 = (bf16[1280,512]{1,0:T(8,128)(2,1)}, bf16[512,1152]{1,0:T(8,128)(2,1)}, bf16[1152,512]{1,0:T(8,128)(2,1)}, f32[2,128]{1,0:T(2,128)}, f32[64,256]{1,0:T(8,128)}) custom-call(bf16[1152,512]{1,0:T(8,128)(2,1)} %w_a.1, f32[9,512]{1,0:T(8,128)} %w_u.1, f32[1,512]{1,0:T(1,128)} %bitcast.5, f32[1,512]{1,0:T(1,128)} %bitcast.6, bf16[4608,128]{1,0:T(8,128)(2,1)} %w_b.1, ...), custom_call_target="tpu_custom_call" | custom-call | tf_op jit(solution)/shard_map/weights/pallas_call | solution.py:547
  13.8 4.2 %all-to-all-done.table_hbm.table = f32[32,1,1152]{2,1,0:T(1,128)S(1)} async-done(((f32[32,1,1152]{2,1,0:T(1,128)}), f32[32,1,1152]{2,1,0:T(1,128)S(1)}, u32[]{:S(2)}, u32[]{:S(2)}) %all-to-all-start) | async-done | bytes 147488 | tf_op jit(solution)/shard_map/all_to_all | solution.py:545
  18.0 10.5 %train.1 = (f32[16,16,2304]{2,1,0:T(8,128)S(1)}, bf16[16,16,2304]{2,1,0:T(8,128)(2,1)S(1)}, f32[32,128]{1,0:T(8,128)S(1)}) custom-call(f32[32,1,1152]{2,1,0:T(1,128)S(1)} %all-to-all-done.table_hbm.table, f32[32,1,1152]{2,1,0:T(1,128)S(1)} %all-to-all-done.table_hbm.table, bf16[64,256,128]{2,1,0:T(8,128)(2,1)} %features.1, ...), custom_call_target="tpu_custom_call" | custom-call | tf_op jit(solution)/shard_map/train/pallas_call | solution.py:580
  28.5 0.3 collective-permute-start
  28.8 2.6 %collective-permute-done.refs_0_ = bf16[16,16,2304]{2,1,0:T(8,128)(2,1)S(1)} collective-permute-done((bf16[16,16,2304]{2,1,0:T(8,128)(2,1)S(1)}, bf16[16,16,2304]{2,1,0:T(8,128)(2,1)S(1)}, u32[]{:S(2)}, u32[]{:S(2)}) %collective-permute-start) | collective-permute-done | bytes 1179680 | tf_op jit(solution)/shard_map/ppermute | solution.py:615
  31.4 0.2 halve_2.1
  31.6 0.8 %collective-permute-start.1 = (bf16[2,16,2304]{2,1,0:T(8,128)(2,1)S(1)}, bf16[2,16,2304]{2,1,0:T(8,128)(2,1)S(1)}, u32[]{:S(2)}, u32[]{:S(2)}) collective-permute-start(bf16[2,16,2304]{2,1,0:T(8,128)(2,1)S(1)} %get-tuple-element.31), channel_id=1, source_target_pairs={{0,2},{1,3},{2,0},{3,1},{4,6},{5,7},{6,4},{7,5},{8,10},{9,11},{10,... | collective-permute-start | bytes 442376 | tf_op jit(solution)/shard_map/ppermute | solution.py:615
  32.5 0.7 collective-permute-start.2
  33.2 2.0 %collective-permute-start.3 = (bf16[2,16,2304]{2,1,0:T(8,128)(2,1)S(1)}, bf16[2,16,2304]{2,1,0:T(8,128)(2,1)S(1)}, u32[]{:S(2)}, u32[]{:S(2)}) collective-permute-start(bf16[2,16,2304]{2,1,0:T(8,128)(2,1)S(1)} %get-tuple-element.33), channel_id=1, source_target_pairs={{0,6},{1,7},{2,4},{3,5},{4,2},{5,3},{6,0},{7,1},{8,14},{9,15},{10,... | collective-permute-start | bytes 442376 | tf_op jit(solution)/shard_map/ppermute | solution.py:615
  35.2 0.7 collective-permute-start.4
  35.9 1.6 %collective-permute-start.5 = (bf16[2,16,2304]{2,1,0:T(8,128)(2,1)S(1)}, bf16[2,16,2304]{2,1,0:T(8,128)(2,1)S(1)}, u32[]{:S(2)}, u32[]{:S(2)}) collective-permute-start(bf16[2,16,2304]{2,1,0:T(8,128)(2,1)S(1)} %get-tuple-element.35), channel_id=1, source_target_pairs={{0,10},{1,11},{2,8},{3,9},{4,14},{5,15},{6,12},{7,13},{8,2},{9,3},... | collective-permute-start | bytes 442376 | tf_op jit(solution)/shard_map/ppermute | solution.py:615
  37.4 0.3 collective-permute-done.1.refs_0_
  37.7 0.8 %collective-permute-start.6 = (bf16[2,16,2304]{2,1,0:T(8,128)(2,1)S(1)}, bf16[2,16,2304]{2,1,0:T(8,128)(2,1)S(1)}, u32[]{:S(2)}, u32[]{:S(2)}) collective-permute-start(bf16[2,16,2304]{2,1,0:T(8,128)(2,1)S(1)} %get-tuple-element.36), channel_id=1, source_target_pairs={{0,12},{1,13},{2,14},{3,15},{4,8},{5,9},{6,10},{7,11},{8,4},{9,5},... | collective-permute-start | bytes 442376 | tf_op jit(solution)/shard_map/ppermute | solution.py:615
  38.6 0.6 collective-permute-done.2.refs_1_
  39.2 1.8 %collective-permute-start.7 = (bf16[2,16,2304]{2,1,0:T(8,128)(2,1)S(1)}, bf16[2,16,2304]{2,1,0:T(8,128)(2,1)S(1)}, u32[]{:S(2)}, u32[]{:S(2)}) collective-permute-start(bf16[2,16,2304]{2,1,0:T(8,128)(2,1)S(1)} %get-tuple-element.37), channel_id=1, source_target_pairs={{0,14},{1,15},{2,12},{3,13},{4,10},{5,11},{6,8},{7,9},{8,6},{9,7},... | collective-permute-start | bytes 442376 | tf_op jit(solution)/shard_map/ppermute | solution.py:615
  41.0 2.5 %collective-permute-done.3.refs_2_ = bf16[2,16,2304]{2,1,0:T(8,128)(2,1)S(1)} collective-permute-done((bf16[2,16,2304]{2,1,0:T(8,128)(2,1)S(1)}, bf16[2,16,2304]{2,1,0:T(8,128)(2,1)S(1)}, u32[]{:S(2)}, u32[]{:S(2)}) %collective-permute-start.3) | collective-permute-done | bytes 147488 | tf_op jit(solution)/shard_map/ppermute | solution.py:615
  43.5 0.0 collective-permute-done.4.refs_3_
  43.5 1.8 %collective-permute-done.5.refs_4_ = bf16[2,16,2304]{2,1,0:T(8,128)(2,1)S(1)} collective-permute-done((bf16[2,16,2304]{2,1,0:T(8,128)(2,1)S(1)}, bf16[2,16,2304]{2,1,0:T(8,128)(2,1)S(1)}, u32[]{:S(2)}, u32[]{:S(2)}) %collective-permute-start.5) | collective-permute-done | bytes 147488 | tf_op jit(solution)/shard_map/ppermute | solution.py:615
  45.4 2.9 %collective-permute-done.6.refs_5_ = bf16[2,16,2304]{2,1,0:T(8,128)(2,1)S(1)} collective-permute-done((bf16[2,16,2304]{2,1,0:T(8,128)(2,1)S(1)}, bf16[2,16,2304]{2,1,0:T(8,128)(2,1)S(1)}, u32[]{:S(2)}, u32[]{:S(2)}) %collective-permute-start.6) | collective-permute-done | bytes 147488 | tf_op jit(solution)/shard_map/ppermute | solution.py:615
  48.3 1.8 %collective-permute-done.7.refs_6_ = bf16[2,16,2304]{2,1,0:T(8,128)(2,1)S(1)} collective-permute-done((bf16[2,16,2304]{2,1,0:T(8,128)(2,1)S(1)}, bf16[2,16,2304]{2,1,0:T(8,128)(2,1)S(1)}, u32[]{:S(2)}, u32[]{:S(2)}) %collective-permute-start.7) | collective-permute-done | bytes 147488 | tf_op jit(solution)/shard_map/ppermute | solution.py:615
  50.1 0.1 halve_16.1
  50.2 11.6 %collective-permute-start.8 = (bf16[1,16,2304]{2,1,0:T(8,128)(2,1)S(1)}, bf16[1,16,2304]{2,1,0:T(8,128)(2,1)S(1)}, u32[]{:S(2)}, u32[]{:S(2)}) collective-permute-start(bf16[1,16,2304]{2,1,0:T(8,128)(2,1)S(1)} %get-tuple-element.40), channel_id=1, source_target_pairs={{0,16},{1,17},{2,18},{3,19},{4,20},{5,21},{6,22},{7,23},{8,24},{9,... | collective-permute-start | bytes 221192 | tf_op jit(solution)/shard_map/ppermute | solution.py:615
  61.9 2.3 %collective-permute-done.8.refs_0_ = bf16[1,16,2304]{2,1,0:T(8,128)(2,1)S(1)} collective-permute-done((bf16[1,16,2304]{2,1,0:T(8,128)(2,1)S(1)}, bf16[1,16,2304]{2,1,0:T(8,128)(2,1)S(1)}, u32[]{:S(2)}, u32[]{:S(2)}) %collective-permute-start.8) | collective-permute-done | bytes 73760 | tf_op jit(solution)/shard_map/ppermute | solution.py:615
  64.2 0.2 finish.1
  64.4 12.6 %all_to_all.10.payload = f32[32,1,128]{2,1,0:T(1,128)S(1)} all-to-all(f32[32,1,128]{2,1,0:T(1,128)S(1)} %get-tuple-element.42), channel_id=1, replica_groups=mesh['tile'=8,'dp'=4] {'tile','dp'}, dimensions={0} | all-to-all | bytes 32768 | tf_op jit(solution)/shard_map/all_to_all | solution.py:648
  77.0 0.8 %scale.1 = (f32[4]{0:T(128)}, f32[16,1152]{1,0:T(8,128)}, f32[16,1152]{1,0:T(8,128)}) custom-call(f32[16,2304]{1,0:T(8,128)S(1)} %get-tuple-element.41.grad, f32[32,1,128]{2,1,0:T(1,128)S(1)} %all_to_all.10.payload), custom_call_target="tpu_custom_call" | custom-call | tf_op jit(solution)/shard_map/scale/pallas_call | solution.py:650
Async XLA Ops:
  2.3 15.7 %all-to-all-start = ((f32[32,1,1152]{2,1,0:T(1,128)}), f32[32,1,1152]{2,1,0:T(1,128)S(1)}, u32[]{:S(2)}, u32[]{:S(2)}) async-start(f32[32,1,1152]{2,1,0:T(1,128)} %pack.1), calls=%async_computation | async-start | bytes 294912 | tf_op jit(solution)/shard_map/all_to_all | solution.py:545
  28.5 2.9 %collective-permute-start = (bf16[16,16,2304]{2,1,0:T(8,128)(2,1)S(1)}, bf16[16,16,2304]{2,1,0:T(8,128)(2,1)S(1)}, u32[]{:S(2)}, u32[]{:S(2)}) collective-permute-start(bf16[16,16,2304]{2,1,0:T(8,128)(2,1)S(1)} %get-tuple-element.29), channel_id=1, source_target_pairs={{0,1},{1,0},{2,3},{3,2},{4,5},{5,4},{6,7},{7,6},{8,9},{9,8},{10,11... | collective-permute-start | bytes 3538952 | tf_op jit(solution)/shard_map/ppermute | solution.py:615
  31.6 6.1 %collective-permute-start.1 = (bf16[2,16,2304]{2,1,0:T(8,128)(2,1)S(1)}, bf16[2,16,2304]{2,1,0:T(8,128)(2,1)S(1)}, u32[]{:S(2)}, u32[]{:S(2)}) collective-permute-start(bf16[2,16,2304]{2,1,0:T(8,128)(2,1)S(1)} %get-tuple-element.31), channel_id=1, source_target_pairs={{0,2},{1,3},{2,0},{3,1},{4,6},{5,7},{6,4},{7,5},{8,10},{9,11},{10,... | collective-permute-start | bytes 442376 | tf_op jit(solution)/shard_map/ppermute | solution.py:615
  32.5 6.7 %collective-permute-start.2 = (bf16[2,16,2304]{2,1,0:T(8,128)(2,1)S(1)}, bf16[2,16,2304]{2,1,0:T(8,128)(2,1)S(1)}, u32[]{:S(2)}, u32[]{:S(2)}) collective-permute-start(bf16[2,16,2304]{2,1,0:T(8,128)(2,1)S(1)} %get-tuple-element.32), channel_id=1, source_target_pairs={{0,4},{1,5},{2,6},{3,7},{4,0},{5,1},{6,2},{7,3},{8,12},{9,13},{10,... | collective-permute-start | bytes 442376 | tf_op jit(solution)/shard_map/ppermute | solution.py:615
  33.2 10.3 %collective-permute-start.3 = (bf16[2,16,2304]{2,1,0:T(8,128)(2,1)S(1)}, bf16[2,16,2304]{2,1,0:T(8,128)(2,1)S(1)}, u32[]{:S(2)}, u32[]{:S(2)}) collective-permute-start(bf16[2,16,2304]{2,1,0:T(8,128)(2,1)S(1)} %get-tuple-element.33), channel_id=1, source_target_pairs={{0,6},{1,7},{2,4},{3,5},{4,2},{5,3},{6,0},{7,1},{8,14},{9,15},{10,... | collective-permute-start | bytes 442376 | tf_op jit(solution)/shard_map/ppermute | solution.py:615
  35.2 8.3 %collective-permute-start.4 = (bf16[2,16,2304]{2,1,0:T(8,128)(2,1)S(1)}, bf16[2,16,2304]{2,1,0:T(8,128)(2,1)S(1)}, u32[]{:S(2)}, u32[]{:S(2)}) collective-permute-start(bf16[2,16,2304]{2,1,0:T(8,128)(2,1)S(1)} %get-tuple-element.34), channel_id=1, source_target_pairs={{0,8},{1,9},{2,10},{3,11},{4,12},{5,13},{6,14},{7,15},{8,0},{9,1},... | collective-permute-start | bytes 442376 | tf_op jit(solution)/shard_map/ppermute | solution.py:615
  35.9 9.5 %collective-permute-start.5 = (bf16[2,16,2304]{2,1,0:T(8,128)(2,1)S(1)}, bf16[2,16,2304]{2,1,0:T(8,128)(2,1)S(1)}, u32[]{:S(2)}, u32[]{:S(2)}) collective-permute-start(bf16[2,16,2304]{2,1,0:T(8,128)(2,1)S(1)} %get-tuple-element.35), channel_id=1, source_target_pairs={{0,10},{1,11},{2,8},{3,9},{4,14},{5,15},{6,12},{7,13},{8,2},{9,3},... | collective-permute-start | bytes 442376 | tf_op jit(solution)/shard_map/ppermute | solution.py:615
  37.7 10.6 %collective-permute-start.6 = (bf16[2,16,2304]{2,1,0:T(8,128)(2,1)S(1)}, bf16[2,16,2304]{2,1,0:T(8,128)(2,1)S(1)}, u32[]{:S(2)}, u32[]{:S(2)}) collective-permute-start(bf16[2,16,2304]{2,1,0:T(8,128)(2,1)S(1)} %get-tuple-element.36), channel_id=1, source_target_pairs={{0,12},{1,13},{2,14},{3,15},{4,8},{5,9},{6,10},{7,11},{8,4},{9,5},... | collective-permute-start | bytes 442376 | tf_op jit(solution)/shard_map/ppermute | solution.py:615
  39.2 10.9 %collective-permute-start.7 = (bf16[2,16,2304]{2,1,0:T(8,128)(2,1)S(1)}, bf16[2,16,2304]{2,1,0:T(8,128)(2,1)S(1)}, u32[]{:S(2)}, u32[]{:S(2)}) collective-permute-start(bf16[2,16,2304]{2,1,0:T(8,128)(2,1)S(1)} %get-tuple-element.37), channel_id=1, source_target_pairs={{0,14},{1,15},{2,12},{3,13},{4,10},{5,11},{6,8},{7,9},{8,6},{9,7},... | collective-permute-start | bytes 442376 | tf_op jit(solution)/shard_map/ppermute | solution.py:615
  50.2 14.0 %collective-permute-start.8 = (bf16[1,16,2304]{2,1,0:T(8,128)(2,1)S(1)}, bf16[1,16,2304]{2,1,0:T(8,128)(2,1)S(1)}, u32[]{:S(2)}, u32[]{:S(2)}) collective-permute-start(bf16[1,16,2304]{2,1,0:T(8,128)(2,1)S(1)} %get-tuple-element.40), channel_id=1, source_target_pairs={{0,16},{1,17},{2,18},{3,19},{4,20},{5,21},{6,22},{7,23},{8,24},{9,... | collective-permute-start | bytes 221192 | tf_op jit(solution)/shard_map/ppermute | solution.py:615

commit v5 on v4

--- a/solution.py
+++ b/solution.py
@@ -152,7 +152,8 @@
     weight_b_hbm,
     weight_back_hbm,
     ends_hbm,
-    keep_out,
+    grad_a,
+    grad_b,
     send_out,
     loss_out,
     ints,
@@ -168,8 +169,6 @@
     win_g,
     slope,
     aim,
-    grad_a,
-    grad_b,
     tails,
     int_sem,
     weight_sems,
@@ -449,26 +448,27 @@
     chunk = HID // devices
     for pair in range(devices // 2):
         for at, grad in ((0, grad_a), (taps * C, grad_b)):
-            lanes = pl.ds(at, taps * C)
             even = grad[2 * pair * chunk : (2 * pair + 1) * chunk]
             odd = grad[(2 * pair + 1) * chunk : (2 * pair + 2) * chunk]
-            first = my_core == 0
-            keep_out[pair, :, lanes] = jnp.where(first, even, odd)
-            send_out[pair, :, lanes] = jnp.where(first, odd, even).astype(BF16)
-
-
-def halve_kernel(fan, count, step, keep, *refs):
-    received, outs = refs[:count], refs[count:]
+            send_out[pair, :, pl.ds(at, taps * C)] = jnp.where(my_core == 0, odd, even).astype(BF16)
+
+
+def halve_kernel(fan, kept, count, step, *refs):
+    keeps, received, outs = refs[:kept], refs[kept : kept + count], refs[kept + count :]
     index = lax.axis_index("tile") * lax.axis_size("dp") + lax.axis_index("dp")
     mine = lax.rem(lax.div(index, step), fan)
+    rows = outs[0].shape[0]
+    width = outs[0].shape[2] // kept
     for peer in range(fan):
         low = jnp.bitwise_xor(mine, peer)
-        for high_part in range(keep.shape[0] // fan):
+        for high_part in range(rows):
             at = high_part * fan + low
-            total = keep[at]
-            for other in received:
-                total = total + other[at].astype(F32)
-            outs[peer][high_part] = total.astype(outs[peer].dtype)
+            for side, keep in enumerate(keeps):
+                lanes = slice(side * width, (side + 1) * width)
+                total = keep[2 * at + lax.rem(index, 2)] if kept > 1 else keep[at]
+                for other in received:
+                    total = total + other[at, :, lanes].astype(F32)
+                outs[peer][high_part, :, lanes] = total.astype(outs[peer].dtype)
 
 
 def finish_kernel(npatch, keep, losses, *refs):
@@ -577,15 +577,16 @@
     )
     weight_a, weight_b, weight_back, ends, target32 = weights
 
-    keep, send, losses = pl.pallas_call(
+    grad_a, grad_b, send, losses = pl.pallas_call(
         functools.partial(train_kernel, dp_count, npatch),
         out_shape=(
-            pltpu.VMEM((devices // 2, chunk, width), F32),
+            pltpu.VMEM((HID, 9 * C), F32),
+            pltpu.VMEM((HID, 9 * C), F32),
             pltpu.VMEM((devices // 2, chunk, width), BF16),
             pltpu.VMEM((devices, C), F32),
         ),
         in_specs=[in_hbm, in_vmem] + [in_hbm] * 6,
-        out_specs=(in_vmem, in_vmem, in_vmem),
+        out_specs=(in_vmem,) * 4,
         scratch_shapes=[
             pltpu.SMEM((devices, C), F32),
             pltpu.SMEM((slots + 1,), jnp.int32),
@@ -600,8 +601,6 @@
             pltpu.VMEM((GROUP * CELLS, 9 * C), BF16),
             pltpu.VMEM((GROUP * CELLS, HID), F32),
             pltpu.VMEM((GROUP * CELLS, C), F32),
-            pltpu.VMEM((HID, 9 * C), F32),
-            pltpu.VMEM((HID, 9 * C), F32),
             pltpu.VMEM((2, C, HID), F32),
             pltpu.SemaphoreType.DMA,
             pltpu.SemaphoreType.DMA((5,)),
@@ -615,23 +614,27 @@
         return lax.ppermute(array, AXES, [(i, i ^ distance) for i in range(devices)])
 
     received = [exchange(send, 1)]
+    keeps = [grad.reshape(devices, chunk, 9 * C) for grad in (grad_a, grad_b)]
+    rows = devices // 2
     step = 2
     while step < devices:
         fan = min(8, devices // step)
-        part = (keep.shape[0] // fan, chunk, width)
+        rows //= fan
+        part = (rows, chunk, width)
         outs = pl.pallas_call(
-            functools.partial(halve_kernel, fan, len(received), step),
+            functools.partial(halve_kernel, fan, len(keeps), len(received), step),
             out_shape=(
                 pltpu.VMEM(part, F32),
                 *[pltpu.VMEM(part, BF16) for _ in range(fan - 1)],
             ),
-            in_specs=[in_vmem] * (1 + len(received)),
+            in_specs=[in_vmem] * (len(keeps) + len(received)),
             out_specs=(in_vmem,) * fan,
-            compiler_params=room(8),
+            compiler_params=room(16),
             name=f"halve_{step}",
-        )(keep, *received)
-        keep = outs[0]
-        received = [exchange(outs[peer], peer * step) for peer in range(1, fan)]
+        )(*keeps, *received)
+        keeps = outs[:1]
+        order = sorted(range(1, fan), key=lambda peer: ((0, 0, 2, 1)[peer.bit_count()], peer))
+        received = [exchange(outs[peer], peer * step) for peer in order]
         step *= fan
 
     grad, payload = pl.pallas_call(
@@ -644,7 +647,7 @@
         out_specs=(in_vmem, in_vmem),
         compiler_params=room(4),
         name="finish",
-    )(keep, losses, *received)
+    )(*keeps, losses, *received)
     payload = lax.all_to_all(payload, AXES, split_axis=0, concat_axis=0, tiled=True)
     out = jax.ShapeDtypeStruct((chunk, width // 2), F32)
     sums, upd_a, upd_b = pl.pallas_call(

time: 78.1 us -> 76.6 us (0.981)
  blocking collectives: 12.6 us -> 10.1 us
  waiting for transfers between devices: 19.1 us -> 20.5 us
    all_to_all x1, blocking collectives: 12.6 us -> 10.1 us  [local(): lax.all_to_all(payload, AXES, split_axis=0, concat_axis=0, tiled=True)]
    ppermute x9, waiting for transfers between devices: 14.9 us -> 16.3 us  [exchange(): lax.ppermute(array, AXES, [(i, i ^ distance) for i in range(devices)])]
  transfers between devices with their start and end apart: 10 -> 10, of which waited for: 9 -> 7; matrix products, arithmetic and copies ran while one was open for 0% -> 0% of each run, Pallas kernels for 5% -> 5%
where the time goes in v5:
time: 76.6 us; the launch traced here: 76.3 us
  starting transfers between devices  27.4 us (36%)
  waiting for transfers between devices  20.5 us (27%)
  Pallas kernels  17.5 us (23%)
  blocking collectives  10.1 us (13%)
    ppermute x9, starting transfers between devices, exchange(): lax.ppermute(array, AXES, [(i, i ^ distance) for i in range(devices)])  20.1 us
    ppermute x9, waiting for transfers between devices, exchange(): lax.ppermute(array, AXES, [(i, i ^ distance) for i in range(devices)])  16.3 us
    pallas_call x1, Pallas kernels, local(): pl.pallas_call(functools.partial(train_kernel, dp_count, npatch), out_sha...  10.4 us
    all_to_all x1, blocking collectives, local(): lax.all_to_all(payload, AXES, split_axis=0, concat_axis=0, tiled=True)  10.1 us
    all_to_all x1, starting transfers between devices, local(): table = lax.all_to_all(line, AXES, split_axis=0, concat_axis=0, tiled=True)  7.3 us
    all_to_all x1, waiting for transfers between devices, local(): table = lax.all_to_all(line, AXES, split_axis=0, concat_axis=0, tiled=True)  4.24 us
    pallas_call x1, Pallas kernels, local(): pl.pallas_call(weights_kernel, out_shape=(pltpu.HBM((10 * C, HID), BF16),...  4.17 us
    pallas_call x1, Pallas kernels, local(): pl.pallas_call(pack_kernel, out_shape=jax.ShapeDtypeStruct((devices, 1, n...  1.65 us
  transfers between devices with their start and end apart: 10, of which 7 were waited for; matrix products, arithmetic and copies ran while one was open for 0% of the time, Pallas kernels for 5%

profile of v5, /device:TPU:0, one launch (start us, length us, event | category | flops | bytes accessed | tf_op | source)
XLA Modules:
  0.0 76.3 jit_solution(9405697368984524667)
XLA Ops:
  0.6 1.6 %pack.1 = f32[32,1,1152]{2,1,0:T(1,128)} custom-call(s32[4]{0:T(128)} %bitcast.11, s32[4]{0:T(128)} %refs_1_.1, s32[4]{0:T(128)} %refs_2_.1, s32[4]{0:T(128)} %refs_3_.1, s32[4]{0:T(128)} %refs_4_.1, f32[4,16,16]{2,1,0:T(8,128)} %refs_5_.1), custom_call_target="tpu_custom_call" | custom-call | tf_op jit(solution)/shard_map/pack/pallas_call | solution.py:530
  2.3 7.3 %all-to-all-start = ((f32[32,1,1152]{2,1,0:T(1,128)}), f32[32,1,1152]{2,1,0:T(1,128)S(1)}, u32[]{:S(2)}, u32[]{:S(2)}) async-start(f32[32,1,1152]{2,1,0:T(1,128)} %pack.1), calls=%async_computation | async-start | bytes 294912 | tf_op jit(solution)/shard_map/all_to_all | solution.py:545
  9.6 4.2 %weights.1 = (bf16[1280,512]{1,0:T(8,128)(2,1)}, bf16[512,1152]{1,0:T(8,128)(2,1)}, bf16[1152,512]{1,0:T(8,128)(2,1)}, f32[2,128]{1,0:T(2,128)}, f32[64,256]{1,0:T(8,128)}) custom-call(bf16[1152,512]{1,0:T(8,128)(2,1)} %w_a.1, f32[9,512]{1,0:T(8,128)} %w_u.1, f32[1,512]{1,0:T(1,128)} %bitcast.9, f32[1,512]{1,0:T(1,128)} %bitcast.10, bf16[4608,128]{1,0:T(8,128)(2,1)} %w_b.1, ...), custom_call_target="tpu_custom_call" | custom-call | tf_op jit(solution)/shard_map/weights/pallas_call | solution.py:547
  13.8 4.2 %all-to-all-done.table_hbm.table = f32[32,1,1152]{2,1,0:T(1,128)S(1)} async-done(((f32[32,1,1152]{2,1,0:T(1,128)}), f32[32,1,1152]{2,1,0:T(1,128)S(1)}, u32[]{:S(2)}, u32[]{:S(2)}) %all-to-all-start) | async-done | bytes 147488 | tf_op jit(solution)/shard_map/all_to_all | solution.py:545
  18.0 10.4 %train.1 = (f32[512,1152]{1,0:T(8,128)S(1)}, f32[512,1152]{1,0:T(8,128)S(1)}, bf16[16,16,2304]{2,1,0:T(8,128)(2,1)S(1)}, f32[32,128]{1,0:T(8,128)S(1)}) custom-call(f32[32,1,1152]{2,1,0:T(1,128)S(1)} %all-to-all-done.table_hbm.table, f32[32,1,1152]{2,1,0:T(1,128)S(1)} %all-to-all-done.table_hbm.table, bf16[64,256,128]{2,1,0:T(8,128)(2,1)} %features.1, ...), custom_call_target="tpu_custom_call" | custom-call | tf_op jit(solution)/shard_map/train/pallas_call | solution.py:580
  28.4 0.3 collective-permute-start
  28.8 2.6 %collective-permute-done.refs_2_ = bf16[16,16,2304]{2,1,0:T(8,128)(2,1)S(1)} collective-permute-done((bf16[16,16,2304]{2,1,0:T(8,128)(2,1)S(1)}, bf16[16,16,2304]{2,1,0:T(8,128)(2,1)S(1)}, u32[]{:S(2)}, u32[]{:S(2)}) %collective-permute-start) | collective-permute-done | bytes 1179680 | tf_op jit(solution)/shard_map/ppermute | solution.py:614
  31.4 0.2 halve_2.1
  31.6 0.6 collective-permute-start.1
  32.2 12.3 %collective-permute-start.2 = (bf16[2,16,2304]{2,1,0:T(8,128)(2,1)S(1)}, bf16[2,16,2304]{2,1,0:T(8,128)(2,1)S(1)}, u32[]{:S(2)}, u32[]{:S(2)}) collective-permute-start(bf16[2,16,2304]{2,1,0:T(8,128)(2,1)S(1)} %get-tuple-element.34), channel_id=1, source_target_pairs={{0,4},{1,5},{2,6},{3,7},{4,0},{5,1},{6,2},{7,3},{8,12},{9,13},{10,... | collective-permute-start | bytes 442376 | tf_op jit(solution)/shard_map/ppermute | solution.py:614
  44.5 0.0 collective-permute-start.3
  44.5 2.2 %collective-permute-start.4 = (bf16[2,16,2304]{2,1,0:T(8,128)(2,1)S(1)}, bf16[2,16,2304]{2,1,0:T(8,128)(2,1)S(1)}, u32[]{:S(2)}, u32[]{:S(2)}) collective-permute-start(bf16[2,16,2304]{2,1,0:T(8,128)(2,1)S(1)} %get-tuple-element.36), channel_id=1, source_target_pairs={{0,14},{1,15},{2,12},{3,13},{4,10},{5,11},{6,8},{7,9},{8,6},{9,7},... | collective-permute-start | bytes 442376 | tf_op jit(solution)/shard_map/ppermute | solution.py:614
  46.7 2.2 %collective-permute-start.5 = (bf16[2,16,2304]{2,1,0:T(8,128)(2,1)S(1)}, bf16[2,16,2304]{2,1,0:T(8,128)(2,1)S(1)}, u32[]{:S(2)}, u32[]{:S(2)}) collective-permute-start(bf16[2,16,2304]{2,1,0:T(8,128)(2,1)S(1)} %get-tuple-element.37), channel_id=1, source_target_pairs={{0,6},{1,7},{2,4},{3,5},{4,2},{5,3},{6,0},{7,1},{8,14},{9,15},{10,... | collective-permute-start | bytes 442376 | tf_op jit(solution)/shard_map/ppermute | solution.py:614
  48.9 0.0 collective-permute-done.1.refs_1_
  48.9 0.7 collective-permute-start.6
  49.6 0.0 collective-permute-done.2.refs_2_
  49.6 1.7 %collective-permute-start.7 = (bf16[2,16,2304]{2,1,0:T(8,128)(2,1)S(1)}, bf16[2,16,2304]{2,1,0:T(8,128)(2,1)S(1)}, u32[]{:S(2)}, u32[]{:S(2)}) collective-permute-start(bf16[2,16,2304]{2,1,0:T(8,128)(2,1)S(1)} %get-tuple-element.39), channel_id=1, source_target_pairs={{0,12},{1,13},{2,14},{3,15},{4,8},{5,9},{6,10},{7,11},{8,4},{9,5},... | collective-permute-start | bytes 442376 | tf_op jit(solution)/shard_map/ppermute | solution.py:614
  51.3 0.0 collective-permute-done.3.refs_3_
  51.3 4.0 %collective-permute-done.4.refs_4_ = bf16[2,16,2304]{2,1,0:T(8,128)(2,1)S(1)} collective-permute-done((bf16[2,16,2304]{2,1,0:T(8,128)(2,1)S(1)}, bf16[2,16,2304]{2,1,0:T(8,128)(2,1)S(1)}, u32[]{:S(2)}, u32[]{:S(2)}) %collective-permute-start.4) | collective-permute-done | bytes 147488 | tf_op jit(solution)/shard_map/ppermute | solution.py:614
  55.3 2.9 %collective-permute-done.5.refs_5_ = bf16[2,16,2304]{2,1,0:T(8,128)(2,1)S(1)} collective-permute-done((bf16[2,16,2304]{2,1,0:T(8,128)(2,1)S(1)}, bf16[2,16,2304]{2,1,0:T(8,128)(2,1)S(1)}, u32[]{:S(2)}, u32[]{:S(2)}) %collective-permute-start.5) | collective-permute-done | bytes 147488 | tf_op jit(solution)/shard_map/ppermute | solution.py:614
  58.2 0.5 collective-permute-done.6.refs_6_
  58.8 0.9 %collective-permute-done.7.refs_7_ = bf16[2,16,2304]{2,1,0:T(8,128)(2,1)S(1)} collective-permute-done((bf16[2,16,2304]{2,1,0:T(8,128)(2,1)S(1)}, bf16[2,16,2304]{2,1,0:T(8,128)(2,1)S(1)}, u32[]{:S(2)}, u32[]{:S(2)}) %collective-permute-start.7) | collective-permute-done | bytes 147488 | tf_op jit(solution)/shard_map/ppermute | solution.py:614
  59.7 0.1 halve_16.1
  59.8 0.1 collective-permute-start.8
  59.9 5.3 %collective-permute-done.8.refs_0_ = bf16[1,16,2304]{2,1,0:T(8,128)(2,1)S(1)} collective-permute-done((bf16[1,16,2304]{2,1,0:T(8,128)(2,1)S(1)}, bf16[1,16,2304]{2,1,0:T(8,128)(2,1)S(1)}, u32[]{:S(2)}, u32[]{:S(2)}) %collective-permute-start.8) | collective-permute-done | bytes 73760 | tf_op jit(solution)/shard_map/ppermute | solution.py:614
  65.2 0.2 finish.1
  65.4 10.1 %all_to_all.10.payload = f32[32,1,128]{2,1,0:T(1,128)S(1)} all-to-all(f32[32,1,128]{2,1,0:T(1,128)S(1)} %get-tuple-element.44), channel_id=1, replica_groups=mesh['tile'=8,'dp'=4] {'tile','dp'}, dimensions={0} | all-to-all | bytes 32768 | tf_op jit(solution)/shard_map/all_to_all | solution.py:651
  75.5 0.8 %scale.1 = (f32[4]{0:T(128)}, f32[16,1152]{1,0:T(8,128)}, f32[16,1152]{1,0:T(8,128)}) custom-call(f32[16,2304]{1,0:T(8,128)S(1)} %get-tuple-element.43.grad, f32[32,1,128]{2,1,0:T(1,128)S(1)} %all_to_all.10.payload), custom_call_target="tpu_custom_call" | custom-call | tf_op jit(solution)/shard_map/scale/pallas_call | solution.py:653
Async XLA Ops:
  2.3 15.7 %all-to-all-start = ((f32[32,1,1152]{2,1,0:T(1,128)}), f32[32,1,1152]{2,1,0:T(1,128)S(1)}, u32[]{:S(2)}, u32[]{:S(2)}) async-start(f32[32,1,1152]{2,1,0:T(1,128)} %pack.1), calls=%async_computation | async-start | bytes 294912 | tf_op jit(solution)/shard_map/all_to_all | solution.py:545
  28.4 2.9 %collective-permute-start = (bf16[16,16,2304]{2,1,0:T(8,128)(2,1)S(1)}, bf16[16,16,2304]{2,1,0:T(8,128)(2,1)S(1)}, u32[]{:S(2)}, u32[]{:S(2)}) collective-permute-start(bf16[16,16,2304]{2,1,0:T(8,128)(2,1)S(1)} %get-tuple-element.31), channel_id=1, source_target_pairs={{0,1},{1,0},{2,3},{3,2},{4,5},{5,4},{6,7},{7,6},{8,9},{9,8},{10,11... | collective-permute-start | bytes 3538952 | tf_op jit(solution)/shard_map/ppermute | solution.py:614
  31.6 17.3 %collective-permute-start.1 = (bf16[2,16,2304]{2,1,0:T(8,128)(2,1)S(1)}, bf16[2,16,2304]{2,1,0:T(8,128)(2,1)S(1)}, u32[]{:S(2)}, u32[]{:S(2)}) collective-permute-start(bf16[2,16,2304]{2,1,0:T(8,128)(2,1)S(1)} %get-tuple-element.33), channel_id=1, source_target_pairs={{0,2},{1,3},{2,0},{3,1},{4,6},{5,7},{6,4},{7,5},{8,10},{9,11},{10,... | collective-permute-start | bytes 442376 | tf_op jit(solution)/shard_map/ppermute | solution.py:614
  32.2 17.4 %collective-permute-start.2 = (bf16[2,16,2304]{2,1,0:T(8,128)(2,1)S(1)}, bf16[2,16,2304]{2,1,0:T(8,128)(2,1)S(1)}, u32[]{:S(2)}, u32[]{:S(2)}) collective-permute-start(bf16[2,16,2304]{2,1,0:T(8,128)(2,1)S(1)} %get-tuple-element.34), channel_id=1, source_target_pairs={{0,4},{1,5},{2,6},{3,7},{4,0},{5,1},{6,2},{7,3},{8,12},{9,13},{10,... | collective-permute-start | bytes 442376 | tf_op jit(solution)/shard_map/ppermute | solution.py:614
  44.5 6.8 %collective-permute-start.3 = (bf16[2,16,2304]{2,1,0:T(8,128)(2,1)S(1)}, bf16[2,16,2304]{2,1,0:T(8,128)(2,1)S(1)}, u32[]{:S(2)}, u32[]{:S(2)}) collective-permute-start(bf16[2,16,2304]{2,1,0:T(8,128)(2,1)S(1)} %get-tuple-element.35), channel_id=1, source_target_pairs={{0,8},{1,9},{2,10},{3,11},{4,12},{5,13},{6,14},{7,15},{8,0},{9,1},... | collective-permute-start | bytes 442376 | tf_op jit(solution)/shard_map/ppermute | solution.py:614
  44.5 10.8 %collective-permute-start.4 = (bf16[2,16,2304]{2,1,0:T(8,128)(2,1)S(1)}, bf16[2,16,2304]{2,1,0:T(8,128)(2,1)S(1)}, u32[]{:S(2)}, u32[]{:S(2)}) collective-permute-start(bf16[2,16,2304]{2,1,0:T(8,128)(2,1)S(1)} %get-tuple-element.36), channel_id=1, source_target_pairs={{0,14},{1,15},{2,12},{3,13},{4,10},{5,11},{6,8},{7,9},{8,6},{9,7},... | collective-permute-start | bytes 442376 | tf_op jit(solution)/shard_map/ppermute | solution.py:614
  46.7 11.6 %collective-permute-start.5 = (bf16[2,16,2304]{2,1,0:T(8,128)(2,1)S(1)}, bf16[2,16,2304]{2,1,0:T(8,128)(2,1)S(1)}, u32[]{:S(2)}, u32[]{:S(2)}) collective-permute-start(bf16[2,16,2304]{2,1,0:T(8,128)(2,1)S(1)} %get-tuple-element.37), channel_id=1, source_target_pairs={{0,6},{1,7},{2,4},{3,5},{4,2},{5,3},{6,0},{7,1},{8,14},{9,15},{10,... | collective-permute-start | bytes 442376 | tf_op jit(solution)/shard_map/ppermute | solution.py:614
  48.9 9.9 %collective-permute-start.6 = (bf16[2,16,2304]{2,1,0:T(8,128)(2,1)S(1)}, bf16[2,16,2304]{2,1,0:T(8,128)(2,1)S(1)}, u32[]{:S(2)}, u32[]{:S(2)}) collective-permute-start(bf16[2,16,2304]{2,1,0:T(8,128)(2,1)S(1)} %get-tuple-element.38), channel_id=1, source_target_pairs={{0,10},{1,11},{2,8},{3,9},{4,14},{5,15},{6,12},{7,13},{8,2},{9,3},... | collective-permute-start | bytes 442376 | tf_op jit(solution)/shard_map/ppermute | solution.py:614
  49.6 10.1 %collective-permute-start.7 = (bf16[2,16,2304]{2,1,0:T(8,128)(2,1)S(1)}, bf16[2,16,2304]{2,1,0:T(8,128)(2,1)S(1)}, u32[]{:S(2)}, u32[]{:S(2)}) collective-permute-start(bf16[2,16,2304]{2,1,0:T(8,128)(2,1)S(1)} %get-tuple-element.39), channel_id=1, source_target_pairs={{0,12},{1,13},{2,14},{3,15},{4,8},{5,9},{6,10},{7,11},{8,4},{9,5},... | collective-permute-start | bytes 442376 | tf_op jit(solution)/shard_map/ppermute | solution.py:614
  59.8 5.4 %collective-permute-start.8 = (bf16[1,16,2304]{2,1,0:T(8,128)(2,1)S(1)}, bf16[1,16,2304]{2,1,0:T(8,128)(2,1)S(1)}, u32[]{:S(2)}, u32[]{:S(2)}) collective-permute-start(bf16[1,16,2304]{2,1,0:T(8,128)(2,1)S(1)} %get-tuple-element.42), channel_id=1, source_target_pairs={{0,16},{1,17},{2,18},{3,19},{4,20},{5,21},{6,22},{7,23},{8,24},{9,... | collective-permute-start | bytes 221192 | tf_op jit(solution)/shard_map/ppermute | solution.py:614

commit v6 on v5

--- a/solution.py
+++ b/solution.py
@@ -364,12 +364,17 @@
             slope[rows[part]] = gate * (1.0 + pre_a * (1.0 - gate))
 
         def second_layer(part):
-            return jnp.dot(act[rows[part]], weight_b[...], preferred_element_type=F32)
+            mine = act[rows[part]]
+            wide = jnp.dot(mine, weight_b[:, : 8 * C], preferred_element_type=F32)
+            last = lax.dot_general(
+                weight_back[8 * C :], mine, (((1,), (1,)), ((), ())), preferred_element_type=F32
+            )
+            return [wide[:, tap * C : (tap + 1) * C] for tap in range(8)] + [last.T]
 
         def finish(part, product):
             columns = []
             for shift in range(3):
-                tap = [product[:, (3 * r + shift) * C : (3 * r + shift + 1) * C] for r in range(3)]
+                tap = [product[3 * r + shift] for r in range(3)]
                 columns.append(from_previous_row(tap[0]) + tap[1] + from_next_row(tap[2]))
             pre_b = (
                 ends[0:1]

time: 76.6 us -> 76.1 us (level)
  waiting for transfers between devices: 20.5 us -> 17 us
  blocking collectives: 10.1 us -> 12.6 us
  starting transfers between devices: 27.4 us -> 28.6 us
    ppermute x9, waiting for transfers between devices: 16.3 us -> 12.8 us  [exchange(): lax.ppermute(array, AXES, [(i, i ^ distance) for i in range(devices)])]
    all_to_all x1, blocking collectives: 10.1 us -> 12.6 us  [local(): lax.all_to_all(payload, AXES, split_axis=0, concat_axis=0, tiled=True)]
    ppermute x9, starting transfers between devices: 20.1 us -> 21.3 us  [exchange(): lax.ppermute(array, AXES, [(i, i ^ distance) for i in range(devices)])]
  transfers between devices with their start and end apart: 10 -> 10, of which waited for: 7 -> 6; matrix products, arithmetic and copies ran while one was open for 0% -> 0% of each run, Pallas kernels for 5% -> 5%
where the time goes in v6:
time: 76.1 us; the launch traced here: 76.3 us
  starting transfers between devices  28.6 us (38%)
  Pallas kernels  17.4 us (23%)
  waiting for transfers between devices  17 us (22%)
  blocking collectives  12.6 us (17%)
    ppermute x9, starting transfers between devices, exchange(): lax.ppermute(array, AXES, [(i, i ^ distance) for i in range(devices)])  21.3 us
    ppermute x9, waiting for transfers between devices, exchange(): lax.ppermute(array, AXES, [(i, i ^ distance) for i in range(devices)])  12.8 us
    all_to_all x1, blocking collectives, local(): lax.all_to_all(payload, AXES, split_axis=0, concat_axis=0, tiled=True)  12.6 us
    pallas_call x1, Pallas kernels, local(): pl.pallas_call(functools.partial(train_kernel, dp_count, npatch), out_sha...  10.3 us
    all_to_all x1, starting transfers between devices, local(): table = lax.all_to_all(line, AXES, split_axis=0, concat_axis=0, tiled=True)  7.3 us
    all_to_all x1, waiting for transfers between devices, local(): table = lax.all_to_all(line, AXES, split_axis=0, concat_axis=0, tiled=True)  4.24 us
    pallas_call x1, Pallas kernels, local(): pl.pallas_call(weights_kernel, out_shape=(pltpu.HBM((10 * C, HID), BF16),...  4.17 us
    pallas_call x1, Pallas kernels, local(): pl.pallas_call(pack_kernel, out_shape=jax.ShapeDtypeStruct((devices, 1, n...  1.65 us
  transfers between devices with their start and end apart: 10, of which 6 were waited for; matrix products, arithmetic and copies ran while one was open for 0% of the time, Pallas kernels for 5%

profile of v6, /device:TPU:0, one launch (start us, length us, event | category | flops | bytes accessed | tf_op | source)
XLA Modules:
  0.0 76.3 jit_solution(15423390348156997406)
XLA Ops:
  0.6 1.6 %pack.1 = f32[32,1,1152]{2,1,0:T(1,128)} custom-call(s32[4]{0:T(128)} %bitcast.11, s32[4]{0:T(128)} %refs_1_.1, s32[4]{0:T(128)} %refs_2_.1, s32[4]{0:T(128)} %refs_3_.1, s32[4]{0:T(128)} %refs_4_.1, f32[4,16,16]{2,1,0:T(8,128)} %refs_5_.1), custom_call_target="tpu_custom_call" | custom-call | tf_op jit(solution)/shard_map/pack/pallas_call | solution.py:535
  2.3 7.3 %all-to-all-start = ((f32[32,1,1152]{2,1,0:T(1,128)}), f32[32,1,1152]{2,1,0:T(1,128)S(1)}, u32[]{:S(2)}, u32[]{:S(2)}) async-start(f32[32,1,1152]{2,1,0:T(1,128)} %pack.1), calls=%async_computation | async-start | bytes 294912 | tf_op jit(solution)/shard_map/all_to_all | solution.py:550
  9.6 4.2 %weights.1 = (bf16[1280,512]{1,0:T(8,128)(2,1)}, bf16[512,1152]{1,0:T(8,128)(2,1)}, bf16[1152,512]{1,0:T(8,128)(2,1)}, f32[2,128]{1,0:T(2,128)}, f32[64,256]{1,0:T(8,128)}) custom-call(bf16[1152,512]{1,0:T(8,128)(2,1)} %w_a.1, f32[9,512]{1,0:T(8,128)} %w_u.1, f32[1,512]{1,0:T(1,128)} %bitcast.9, f32[1,512]{1,0:T(1,128)} %bitcast.10, bf16[4608,128]{1,0:T(8,128)(2,1)} %w_b.1, ...), custom_call_target="tpu_custom_call" | custom-call | tf_op jit(solution)/shard_map/weights/pallas_call | solution.py:552
  13.8 4.2 %all-to-all-done.table_hbm.table = f32[32,1,1152]{2,1,0:T(1,128)S(1)} async-done(((f32[32,1,1152]{2,1,0:T(1,128)}), f32[32,1,1152]{2,1,0:T(1,128)S(1)}, u32[]{:S(2)}, u32[]{:S(2)}) %all-to-all-start) | async-done | bytes 147488 | tf_op jit(solution)/shard_map/all_to_all | solution.py:550
  18.0 10.3 %train.1 = (f32[512,1152]{1,0:T(8,128)S(1)}, f32[512,1152]{1,0:T(8,128)S(1)}, bf16[16,16,2304]{2,1,0:T(8,128)(2,1)S(1)}, f32[32,128]{1,0:T(8,128)S(1)}) custom-call(f32[32,1,1152]{2,1,0:T(1,128)S(1)} %all-to-all-done.table_hbm.table, f32[32,1,1152]{2,1,0:T(1,128)S(1)} %all-to-all-done.table_hbm.table, bf16[64,256,128]{2,1,0:T(8,128)(2,1)} %features.1, ...), custom_call_target="tpu_custom_call" | custom-call | tf_op jit(solution)/shard_map/train/pallas_call | solution.py:585
  28.3 0.6 collective-permute-start
  28.9 2.5 %collective-permute-done.refs_2_ = bf16[16,16,2304]{2,1,0:T(8,128)(2,1)S(1)} collective-permute-done((bf16[16,16,2304]{2,1,0:T(8,128)(2,1)S(1)}, bf16[16,16,2304]{2,1,0:T(8,128)(2,1)S(1)}, u32[]{:S(2)}, u32[]{:S(2)}) %collective-permute-start) | collective-permute-done | bytes 1179680 | tf_op jit(solution)/shard_map/ppermute | solution.py:619
  31.4 0.2 halve_2.1
  31.6 0.7 collective-permute-start.1
  32.3 1.0 %collective-permute-start.2 = (bf16[2,16,2304]{2,1,0:T(8,128)(2,1)S(1)}, bf16[2,16,2304]{2,1,0:T(8,128)(2,1)S(1)}, u32[]{:S(2)}, u32[]{:S(2)}) collective-permute-start(bf16[2,16,2304]{2,1,0:T(8,128)(2,1)S(1)} %get-tuple-element.34), channel_id=1, source_target_pairs={{0,4},{1,5},{2,6},{3,7},{4,0},{5,1},{6,2},{7,3},{8,12},{9,13},{10,... | collective-permute-start | bytes 442376 | tf_op jit(solution)/shard_map/ppermute | solution.py:619
  33.3 0.4 collective-permute-start.3
  33.7 3.0 %collective-permute-start.4 = (bf16[2,16,2304]{2,1,0:T(8,128)(2,1)S(1)}, bf16[2,16,2304]{2,1,0:T(8,128)(2,1)S(1)}, u32[]{:S(2)}, u32[]{:S(2)}) collective-permute-start(bf16[2,16,2304]{2,1,0:T(8,128)(2,1)S(1)} %get-tuple-element.36), channel_id=1, source_target_pairs={{0,14},{1,15},{2,12},{3,13},{4,10},{5,11},{6,8},{7,9},{8,6},{9,7},... | collective-permute-start | bytes 442376 | tf_op jit(solution)/shard_map/ppermute | solution.py:619
  36.7 1.0 %collective-permute-start.5 = (bf16[2,16,2304]{2,1,0:T(8,128)(2,1)S(1)}, bf16[2,16,2304]{2,1,0:T(8,128)(2,1)S(1)}, u32[]{:S(2)}, u32[]{:S(2)}) collective-permute-start(bf16[2,16,2304]{2,1,0:T(8,128)(2,1)S(1)} %get-tuple-element.37), channel_id=1, source_target_pairs={{0,6},{1,7},{2,4},{3,5},{4,2},{5,3},{6,0},{7,1},{8,14},{9,15},{10,... | collective-permute-start | bytes 442376 | tf_op jit(solution)/shard_map/ppermute | solution.py:619
  37.7 0.2 collective-permute-done.1.refs_1_
  37.8 0.9 %collective-permute-start.6 = (bf16[2,16,2304]{2,1,0:T(8,128)(2,1)S(1)}, bf16[2,16,2304]{2,1,0:T(8,128)(2,1)S(1)}, u32[]{:S(2)}, u32[]{:S(2)}) collective-permute-start(bf16[2,16,2304]{2,1,0:T(8,128)(2,1)S(1)} %get-tuple-element.38), channel_id=1, source_target_pairs={{0,10},{1,11},{2,8},{3,9},{4,14},{5,15},{6,12},{7,13},{8,2},{9,3},... | collective-permute-start | bytes 442376 | tf_op jit(solution)/shard_map/ppermute | solution.py:619
  38.7 0.0 collective-permute-done.2.refs_2_
  38.7 2.3 %collective-permute-start.7 = (bf16[2,16,2304]{2,1,0:T(8,128)(2,1)S(1)}, bf16[2,16,2304]{2,1,0:T(8,128)(2,1)S(1)}, u32[]{:S(2)}, u32[]{:S(2)}) collective-permute-start(bf16[2,16,2304]{2,1,0:T(8,128)(2,1)S(1)} %get-tuple-element.39), channel_id=1, source_target_pairs={{0,12},{1,13},{2,14},{3,15},{4,8},{5,9},{6,10},{7,11},{8,4},{9,5},... | collective-permute-start | bytes 442376 | tf_op jit(solution)/shard_map/ppermute | solution.py:619
  41.1 0.0 collective-permute-done.3.refs_3_
  41.1 4.5 %collective-permute-done.4.refs_4_ = bf16[2,16,2304]{2,1,0:T(8,128)(2,1)S(1)} collective-permute-done((bf16[2,16,2304]{2,1,0:T(8,128)(2,1)S(1)}, bf16[2,16,2304]{2,1,0:T(8,128)(2,1)S(1)}, u32[]{:S(2)}, u32[]{:S(2)}) %collective-permute-start.4) | collective-permute-done | bytes 147488 | tf_op jit(solution)/shard_map/ppermute | solution.py:619
  45.6 3.1 %collective-permute-done.5.refs_5_ = bf16[2,16,2304]{2,1,0:T(8,128)(2,1)S(1)} collective-permute-done((bf16[2,16,2304]{2,1,0:T(8,128)(2,1)S(1)}, bf16[2,16,2304]{2,1,0:T(8,128)(2,1)S(1)}, u32[]{:S(2)}, u32[]{:S(2)}) %collective-permute-start.5) | collective-permute-done | bytes 147488 | tf_op jit(solution)/shard_map/ppermute | solution.py:619
  48.7 0.0 collective-permute-done.6.refs_6_
  48.7 0.0 collective-permute-done.7.refs_7_
  48.7 0.1 halve_16.1
  48.8 11.4 %collective-permute-start.8 = (bf16[1,16,2304]{2,1,0:T(8,128)(2,1)S(1)}, bf16[1,16,2304]{2,1,0:T(8,128)(2,1)S(1)}, u32[]{:S(2)}, u32[]{:S(2)}) collective-permute-start(bf16[1,16,2304]{2,1,0:T(8,128)(2,1)S(1)} %get-tuple-element.42), channel_id=1, source_target_pairs={{0,16},{1,17},{2,18},{3,19},{4,20},{5,21},{6,22},{7,23},{8,24},{9,... | collective-permute-start | bytes 221192 | tf_op jit(solution)/shard_map/ppermute | solution.py:619
  60.2 2.5 %collective-permute-done.8.refs_0_ = bf16[1,16,2304]{2,1,0:T(8,128)(2,1)S(1)} collective-permute-done((bf16[1,16,2304]{2,1,0:T(8,128)(2,1)S(1)}, bf16[1,16,2304]{2,1,0:T(8,128)(2,1)S(1)}, u32[]{:S(2)}, u32[]{:S(2)}) %collective-permute-start.8) | collective-permute-done | bytes 73760 | tf_op jit(solution)/shard_map/ppermute | solution.py:619
  62.7 0.2 finish.1
  62.9 12.6 %all_to_all.10.payload = f32[32,1,128]{2,1,0:T(1,128)S(1)} all-to-all(f32[32,1,128]{2,1,0:T(1,128)S(1)} %get-tuple-element.44), channel_id=1, replica_groups=mesh['tile'=8,'dp'=4] {'tile','dp'}, dimensions={0} | all-to-all | bytes 32768 | tf_op jit(solution)/shard_map/all_to_all | solution.py:656
  75.5 0.8 %scale.1 = (f32[4]{0:T(128)}, f32[16,1152]{1,0:T(8,128)}, f32[16,1152]{1,0:T(8,128)}) custom-call(f32[16,2304]{1,0:T(8,128)S(1)} %get-tuple-element.43.grad, f32[32,1,128]{2,1,0:T(1,128)S(1)} %all_to_all.10.payload), custom_call_target="tpu_custom_call" | custom-call | tf_op jit(solution)/shard_map/scale/pallas_call | solution.py:658
Async XLA Ops:
  2.3 15.7 %all-to-all-start = ((f32[32,1,1152]{2,1,0:T(1,128)}), f32[32,1,1152]{2,1,0:T(1,128)S(1)}, u32[]{:S(2)}, u32[]{:S(2)}) async-start(f32[32,1,1152]{2,1,0:T(1,128)} %pack.1), calls=%async_computation | async-start | bytes 294912 | tf_op jit(solution)/shard_map/all_to_all | solution.py:550
  28.3 3.1 %collective-permute-start = (bf16[16,16,2304]{2,1,0:T(8,128)(2,1)S(1)}, bf16[16,16,2304]{2,1,0:T(8,128)(2,1)S(1)}, u32[]{:S(2)}, u32[]{:S(2)}) collective-permute-start(bf16[16,16,2304]{2,1,0:T(8,128)(2,1)S(1)} %get-tuple-element.31), channel_id=1, source_target_pairs={{0,1},{1,0},{2,3},{3,2},{4,5},{5,4},{6,7},{7,6},{8,9},{9,8},{10,11... | collective-permute-start | bytes 3538952 | tf_op jit(solution)/shard_map/ppermute | solution.py:619
  31.6 6.2 %collective-permute-start.1 = (bf16[2,16,2304]{2,1,0:T(8,128)(2,1)S(1)}, bf16[2,16,2304]{2,1,0:T(8,128)(2,1)S(1)}, u32[]{:S(2)}, u32[]{:S(2)}) collective-permute-start(bf16[2,16,2304]{2,1,0:T(8,128)(2,1)S(1)} %get-tuple-element.33), channel_id=1, source_target_pairs={{0,2},{1,3},{2,0},{3,1},{4,6},{5,7},{6,4},{7,5},{8,10},{9,11},{10,... | collective-permute-start | bytes 442376 | tf_op jit(solution)/shard_map/ppermute | solution.py:619
  32.3 6.5 %collective-permute-start.2 = (bf16[2,16,2304]{2,1,0:T(8,128)(2,1)S(1)}, bf16[2,16,2304]{2,1,0:T(8,128)(2,1)S(1)}, u32[]{:S(2)}, u32[]{:S(2)}) collective-permute-start(bf16[2,16,2304]{2,1,0:T(8,128)(2,1)S(1)} %get-tuple-element.34), channel_id=1, source_target_pairs={{0,4},{1,5},{2,6},{3,7},{4,0},{5,1},{6,2},{7,3},{8,12},{9,13},{10,... | collective-permute-start | bytes 442376 | tf_op jit(solution)/shard_map/ppermute | solution.py:619
  33.3 7.8 %collective-permute-start.3 = (bf16[2,16,2304]{2,1,0:T(8,128)(2,1)S(1)}, bf16[2,16,2304]{2,1,0:T(8,128)(2,1)S(1)}, u32[]{:S(2)}, u32[]{:S(2)}) collective-permute-start(bf16[2,16,2304]{2,1,0:T(8,128)(2,1)S(1)} %get-tuple-element.35), channel_id=1, source_target_pairs={{0,8},{1,9},{2,10},{3,11},{4,12},{5,13},{6,14},{7,15},{8,0},{9,1},... | collective-permute-start | bytes 442376 | tf_op jit(solution)/shard_map/ppermute | solution.py:619
  33.7 11.9 %collective-permute-start.4 = (bf16[2,16,2304]{2,1,0:T(8,128)(2,1)S(1)}, bf16[2,16,2304]{2,1,0:T(8,128)(2,1)S(1)}, u32[]{:S(2)}, u32[]{:S(2)}) collective-permute-start(bf16[2,16,2304]{2,1,0:T(8,128)(2,1)S(1)} %get-tuple-element.36), channel_id=1, source_target_pairs={{0,14},{1,15},{2,12},{3,13},{4,10},{5,11},{6,8},{7,9},{8,6},{9,7},... | collective-permute-start | bytes 442376 | tf_op jit(solution)/shard_map/ppermute | solution.py:619
  36.7 12.0 %collective-permute-start.5 = (bf16[2,16,2304]{2,1,0:T(8,128)(2,1)S(1)}, bf16[2,16,2304]{2,1,0:T(8,128)(2,1)S(1)}, u32[]{:S(2)}, u32[]{:S(2)}) collective-permute-start(bf16[2,16,2304]{2,1,0:T(8,128)(2,1)S(1)} %get-tuple-element.37), channel_id=1, source_target_pairs={{0,6},{1,7},{2,4},{3,5},{4,2},{5,3},{6,0},{7,1},{8,14},{9,15},{10,... | collective-permute-start | bytes 442376 | tf_op jit(solution)/shard_map/ppermute | solution.py:619
  37.8 10.9 %collective-permute-start.6 = (bf16[2,16,2304]{2,1,0:T(8,128)(2,1)S(1)}, bf16[2,16,2304]{2,1,0:T(8,128)(2,1)S(1)}, u32[]{:S(2)}, u32[]{:S(2)}) collective-permute-start(bf16[2,16,2304]{2,1,0:T(8,128)(2,1)S(1)} %get-tuple-element.38), channel_id=1, source_target_pairs={{0,10},{1,11},{2,8},{3,9},{4,14},{5,15},{6,12},{7,13},{8,2},{9,3},... | collective-permute-start | bytes 442376 | tf_op jit(solution)/shard_map/ppermute | solution.py:619
  38.7 9.9 %collective-permute-start.7 = (bf16[2,16,2304]{2,1,0:T(8,128)(2,1)S(1)}, bf16[2,16,2304]{2,1,0:T(8,128)(2,1)S(1)}, u32[]{:S(2)}, u32[]{:S(2)}) collective-permute-start(bf16[2,16,2304]{2,1,0:T(8,128)(2,1)S(1)} %get-tuple-element.39), channel_id=1, source_target_pairs={{0,12},{1,13},{2,14},{3,15},{4,8},{5,9},{6,10},{7,11},{8,4},{9,5},... | collective-permute-start | bytes 442376 | tf_op jit(solution)/shard_map/ppermute | solution.py:619
  48.8 13.9 %collective-permute-start.8 = (bf16[1,16,2304]{2,1,0:T(8,128)(2,1)S(1)}, bf16[1,16,2304]{2,1,0:T(8,128)(2,1)S(1)}, u32[]{:S(2)}, u32[]{:S(2)}) collective-permute-start(bf16[1,16,2304]{2,1,0:T(8,128)(2,1)S(1)} %get-tuple-element.42), channel_id=1, source_target_pairs={{0,16},{1,17},{2,18},{3,19},{4,20},{5,21},{6,22},{7,23},{8,24},{9,... | collective-permute-start | bytes 221192 | tf_op jit(solution)/shard_map/ppermute | solution.py:619

commit v7 on v6

--- a/solution.py
+++ b/solution.py
@@ -233,7 +233,7 @@
         return carry
 
     turn, count = jnp.int32(0), jnp.int32(0)
-    stops = [0, devices // 4, devices // 2, devices]
+    stops = [0, devices // 8, devices // 4, devices // 2, devices]
     for begin, end in zip(stops, stops[1:]):
         known = count
         turn, count = lax.fori_loop(begin, end, choose, (turn, known))

time: 76.1 us -> 76.1 us (level)
  blocking collectives: 12.6 us -> 10.9 us
  waiting for transfers between devices: 17 us -> 18.6 us
    all_to_all x1, blocking collectives: 12.6 us -> 10.9 us  [local(): lax.all_to_all(payload, AXES, split_axis=0, concat_axis=0, tiled=True)]
    ppermute x9, waiting for transfers between devices: 12.8 us -> 14.3 us  [exchange(): lax.ppermute(array, AXES, [(i, i ^ distance) for i in range(devices)])]
where the time goes in v7:
time: 76.1 us
  starting transfers between devices  28.6 us (38%)
  waiting for transfers between devices  18.6 us (24%)
  Pallas kernels  17.4 us (23%)
  blocking collectives  10.9 us (14%)
    ppermute x9, starting transfers between devices, exchange(): lax.ppermute(array, AXES, [(i, i ^ distance) for i in range(devices)])  21.3 us
    ppermute x9, waiting for transfers between devices, exchange(): lax.ppermute(array, AXES, [(i, i ^ distance) for i in range(devices)])  14.3 us
    all_to_all x1, blocking collectives, local(): lax.all_to_all(payload, AXES, split_axis=0, concat_axis=0, tiled=True)  10.9 us
    pallas_call x1, Pallas kernels, local(): pl.pallas_call(functools.partial(train_kernel, dp_count, npatch), out_sha...  10.3 us
    all_to_all x1, starting transfers between devices, local(): table = lax.all_to_all(line, AXES, split_axis=0, concat_axis=0, tiled=True)  7.3 us
    all_to_all x1, waiting for transfers between devices, local(): table = lax.all_to_all(line, AXES, split_axis=0, concat_axis=0, tiled=True)  4.24 us
    pallas_call x1, Pallas kernels, local(): pl.pallas_call(weights_kernel, out_shape=(pltpu.HBM((10 * C, HID), BF16),...  4.17 us
    pallas_call x1, Pallas kernels, local(): pl.pallas_call(pack_kernel, out_shape=jax.ShapeDtypeStruct((devices, 1, n...  1.65 us
  transfers between devices with their start and end apart: 10, of which 6 were waited for; matrix products, arithmetic and copies ran while one was open for 0% of the time, Pallas kernels for 5%

profile of v7, /device:TPU:0, one launch (start us, length us, event | category | flops | bytes accessed | tf_op | source)
XLA Modules:
  0.0 76.1 jit_solution(7187449345276843701)
XLA Ops:
  0.6 1.6 %pack.1 = f32[32,1,1152]{2,1,0:T(1,128)} custom-call(s32[4]{0:T(128)} %bitcast.11, s32[4]{0:T(128)} %refs_1_.1, s32[4]{0:T(128)} %refs_2_.1, s32[4]{0:T(128)} %refs_3_.1, s32[4]{0:T(128)} %refs_4_.1, f32[4,16,16]{2,1,0:T(8,128)} %refs_5_.1), custom_call_target="tpu_custom_call" | custom-call | tf_op jit(solution)/shard_map/pack/pallas_call | solution.py:535
  2.3 7.3 %all-to-all-start = ((f32[32,1,1152]{2,1,0:T(1,128)}), f32[32,1,1152]{2,1,0:T(1,128)S(1)}, u32[]{:S(2)}, u32[]{:S(2)}) async-start(f32[32,1,1152]{2,1,0:T(1,128)} %pack.1), calls=%async_computation | async-start | bytes 294912 | tf_op jit(solution)/shard_map/all_to_all | solution.py:550
  9.6 4.2 %weights.1 = (bf16[1280,512]{1,0:T(8,128)(2,1)}, bf16[512,1152]{1,0:T(8,128)(2,1)}, bf16[1152,512]{1,0:T(8,128)(2,1)}, f32[2,128]{1,0:T(2,128)}, f32[64,256]{1,0:T(8,128)}) custom-call(bf16[1152,512]{1,0:T(8,128)(2,1)} %w_a.1, f32[9,512]{1,0:T(8,128)} %w_u.1, f32[1,512]{1,0:T(1,128)} %bitcast.9, f32[1,512]{1,0:T(1,128)} %bitcast.10, bf16[4608,128]{1,0:T(8,128)(2,1)} %w_b.1, ...), custom_call_target="tpu_custom_call" | custom-call | tf_op jit(solution)/shard_map/weights/pallas_call | solution.py:552
  13.8 4.2 %all-to-all-done.table_hbm.table = f32[32,1,1152]{2,1,0:T(1,128)S(1)} async-done(((f32[32,1,1152]{2,1,0:T(1,128)}), f32[32,1,1152]{2,1,0:T(1,128)S(1)}, u32[]{:S(2)}, u32[]{:S(2)}) %all-to-all-start) | async-done | bytes 147488 | tf_op jit(solution)/shard_map/all_to_all | solution.py:550
  18.0 10.3 %train.1 = (f32[512,1152]{1,0:T(8,128)S(1)}, f32[512,1152]{1,0:T(8,128)S(1)}, bf16[16,16,2304]{2,1,0:T(8,128)(2,1)S(1)}, f32[32,128]{1,0:T(8,128)S(1)}) custom-call(f32[32,1,1152]{2,1,0:T(1,128)S(1)} %all-to-all-done.table_hbm.table, f32[32,1,1152]{2,1,0:T(1,128)S(1)} %all-to-all-done.table_hbm.table, bf16[64,256,128]{2,1,0:T(8,128)(2,1)} %features.1, ...), custom_call_target="tpu_custom_call" | custom-call | tf_op jit(solution)/shard_map/train/pallas_call | solution.py:585
  28.3 0.3 collective-permute-start
  28.6 2.6 %collective-permute-done.refs_2_ = bf16[16,16,2304]{2,1,0:T(8,128)(2,1)S(1)} collective-permute-done((bf16[16,16,2304]{2,1,0:T(8,128)(2,1)S(1)}, bf16[16,16,2304]{2,1,0:T(8,128)(2,1)S(1)}, u32[]{:S(2)}, u32[]{:S(2)}) %collective-permute-start) | collective-permute-done | bytes 1179680 | tf_op jit(solution)/shard_map/ppermute | solution.py:619
  31.2 0.2 halve_2.1
  31.4 0.6 collective-permute-start.1
  32.0 1.0 %collective-permute-start.2 = (bf16[2,16,2304]{2,1,0:T(8,128)(2,1)S(1)}, bf16[2,16,2304]{2,1,0:T(8,128)(2,1)S(1)}, u32[]{:S(2)}, u32[]{:S(2)}) collective-permute-start(bf16[2,16,2304]{2,1,0:T(8,128)(2,1)S(1)} %get-tuple-element.34), channel_id=1, source_target_pairs={{0,4},{1,5},{2,6},{3,7},{4,0},{5,1},{6,2},{7,3},{8,12},{9,13},{10,... | collective-permute-start | bytes 442376 | tf_op jit(solution)/shard_map/ppermute | solution.py:619
  33.0 1.0 %collective-permute-start.3 = (bf16[2,16,2304]{2,1,0:T(8,128)(2,1)S(1)}, bf16[2,16,2304]{2,1,0:T(8,128)(2,1)S(1)}, u32[]{:S(2)}, u32[]{:S(2)}) collective-permute-start(bf16[2,16,2304]{2,1,0:T(8,128)(2,1)S(1)} %get-tuple-element.35), channel_id=1, source_target_pairs={{0,8},{1,9},{2,10},{3,11},{4,12},{5,13},{6,14},{7,15},{8,0},{9,1},... | collective-permute-start | bytes 442376 | tf_op jit(solution)/shard_map/ppermute | solution.py:619
  34.0 2.5 %collective-permute-start.4 = (bf16[2,16,2304]{2,1,0:T(8,128)(2,1)S(1)}, bf16[2,16,2304]{2,1,0:T(8,128)(2,1)S(1)}, u32[]{:S(2)}, u32[]{:S(2)}) collective-permute-start(bf16[2,16,2304]{2,1,0:T(8,128)(2,1)S(1)} %get-tuple-element.36), channel_id=1, source_target_pairs={{0,14},{1,15},{2,12},{3,13},{4,10},{5,11},{6,8},{7,9},{8,6},{9,7},... | collective-permute-start | bytes 442376 | tf_op jit(solution)/shard_map/ppermute | solution.py:619
  36.5 0.9 %collective-permute-start.5 = (bf16[2,16,2304]{2,1,0:T(8,128)(2,1)S(1)}, bf16[2,16,2304]{2,1,0:T(8,128)(2,1)S(1)}, u32[]{:S(2)}, u32[]{:S(2)}) collective-permute-start(bf16[2,16,2304]{2,1,0:T(8,128)(2,1)S(1)} %get-tuple-element.37), channel_id=1, source_target_pairs={{0,6},{1,7},{2,4},{3,5},{4,2},{5,3},{6,0},{7,1},{8,14},{9,15},{10,... | collective-permute-start | bytes 442376 | tf_op jit(solution)/shard_map/ppermute | solution.py:619
  37.4 0.1 collective-permute-done.1.refs_1_
  37.5 1.2 %collective-permute-start.6 = (bf16[2,16,2304]{2,1,0:T(8,128)(2,1)S(1)}, bf16[2,16,2304]{2,1,0:T(8,128)(2,1)S(1)}, u32[]{:S(2)}, u32[]{:S(2)}) collective-permute-start(bf16[2,16,2304]{2,1,0:T(8,128)(2,1)S(1)} %get-tuple-element.38), channel_id=1, source_target_pairs={{0,10},{1,11},{2,8},{3,9},{4,14},{5,15},{6,12},{7,13},{8,2},{9,3},... | collective-permute-start | bytes 442376 | tf_op jit(solution)/shard_map/ppermute | solution.py:619
  38.8 0.0 collective-permute-done.2.refs_2_
  38.8 2.1 %collective-permute-start.7 = (bf16[2,16,2304]{2,1,0:T(8,128)(2,1)S(1)}, bf16[2,16,2304]{2,1,0:T(8,128)(2,1)S(1)}, u32[]{:S(2)}, u32[]{:S(2)}) collective-permute-start(bf16[2,16,2304]{2,1,0:T(8,128)(2,1)S(1)} %get-tuple-element.39), channel_id=1, source_target_pairs={{0,12},{1,13},{2,14},{3,15},{4,8},{5,9},{6,10},{7,11},{8,4},{9,5},... | collective-permute-start | bytes 442376 | tf_op jit(solution)/shard_map/ppermute | solution.py:619
  40.9 0.0 collective-permute-done.3.refs_3_
  40.9 4.5 %collective-permute-done.4.refs_4_ = bf16[2,16,2304]{2,1,0:T(8,128)(2,1)S(1)} collective-permute-done((bf16[2,16,2304]{2,1,0:T(8,128)(2,1)S(1)}, bf16[2,16,2304]{2,1,0:T(8,128)(2,1)S(1)}, u32[]{:S(2)}, u32[]{:S(2)}) %collective-permute-start.4) | collective-permute-done | bytes 147488 | tf_op jit(solution)/shard_map/ppermute | solution.py:619
  45.3 4.4 %collective-permute-done.5.refs_5_ = bf16[2,16,2304]{2,1,0:T(8,128)(2,1)S(1)} collective-permute-done((bf16[2,16,2304]{2,1,0:T(8,128)(2,1)S(1)}, bf16[2,16,2304]{2,1,0:T(8,128)(2,1)S(1)}, u32[]{:S(2)}, u32[]{:S(2)}) %collective-permute-start.5) | collective-permute-done | bytes 147488 | tf_op jit(solution)/shard_map/ppermute | solution.py:619
  49.8 0.0 collective-permute-done.6.refs_6_
  49.8 0.0 collective-permute-done.7.refs_7_
  49.8 0.1 halve_16.1
  49.9 11.6 %collective-permute-start.8 = (bf16[1,16,2304]{2,1,0:T(8,128)(2,1)S(1)}, bf16[1,16,2304]{2,1,0:T(8,128)(2,1)S(1)}, u32[]{:S(2)}, u32[]{:S(2)}) collective-permute-start(bf16[1,16,2304]{2,1,0:T(8,128)(2,1)S(1)} %get-tuple-element.42), channel_id=1, source_target_pairs={{0,16},{1,17},{2,18},{3,19},{4,20},{5,21},{6,22},{7,23},{8,24},{9,... | collective-permute-start | bytes 221192 | tf_op jit(solution)/shard_map/ppermute | solution.py:619
  61.6 2.7 %collective-permute-done.8.refs_0_ = bf16[1,16,2304]{2,1,0:T(8,128)(2,1)S(1)} collective-permute-done((bf16[1,16,2304]{2,1,0:T(8,128)(2,1)S(1)}, bf16[1,16,2304]{2,1,0:T(8,128)(2,1)S(1)}, u32[]{:S(2)}, u32[]{:S(2)}) %collective-permute-start.8) | collective-permute-done | bytes 73760 | tf_op jit(solution)/shard_map/ppermute | solution.py:619
  64.3 0.2 finish.1
  64.4 10.9 %all_to_all.10.payload = f32[32,1,128]{2,1,0:T(1,128)S(1)} all-to-all(f32[32,1,128]{2,1,0:T(1,128)S(1)} %get-tuple-element.44), channel_id=1, replica_groups=mesh['tile'=8,'dp'=4] {'tile','dp'}, dimensions={0} | all-to-all | bytes 32768 | tf_op jit(solution)/shard_map/all_to_all | solution.py:656
  75.3 0.8 %scale.1 = (f32[4]{0:T(128)}, f32[16,1152]{1,0:T(8,128)}, f32[16,1152]{1,0:T(8,128)}) custom-call(f32[16,2304]{1,0:T(8,128)S(1)} %get-tuple-element.43.grad, f32[32,1,128]{2,1,0:T(1,128)S(1)} %all_to_all.10.payload), custom_call_target="tpu_custom_call" | custom-call | tf_op jit(solution)/shard_map/scale/pallas_call | solution.py:658
Async XLA Ops:
  2.3 15.7 %all-to-all-start = ((f32[32,1,1152]{2,1,0:T(1,128)}), f32[32,1,1152]{2,1,0:T(1,128)S(1)}, u32[]{:S(2)}, u32[]{:S(2)}) async-start(f32[32,1,1152]{2,1,0:T(1,128)} %pack.1), calls=%async_computation | async-start | bytes 294912 | tf_op jit(solution)/shard_map/all_to_all | solution.py:550
  28.3 2.9 %collective-permute-start = (bf16[16,16,2304]{2,1,0:T(8,128)(2,1)S(1)}, bf16[16,16,2304]{2,1,0:T(8,128)(2,1)S(1)}, u32[]{:S(2)}, u32[]{:S(2)}) collective-permute-start(bf16[16,16,2304]{2,1,0:T(8,128)(2,1)S(1)} %get-tuple-element.31), channel_id=1, source_target_pairs={{0,1},{1,0},{2,3},{3,2},{4,5},{5,4},{6,7},{7,6},{8,9},{9,8},{10,11... | collective-permute-start | bytes 3538952 | tf_op jit(solution)/shard_map/ppermute | solution.py:619
  31.4 6.1 %collective-permute-start.1 = (bf16[2,16,2304]{2,1,0:T(8,128)(2,1)S(1)}, bf16[2,16,2304]{2,1,0:T(8,128)(2,1)S(1)}, u32[]{:S(2)}, u32[]{:S(2)}) collective-permute-start(bf16[2,16,2304]{2,1,0:T(8,128)(2,1)S(1)} %get-tuple-element.33), channel_id=1, source_target_pairs={{0,2},{1,3},{2,0},{3,1},{4,6},{5,7},{6,4},{7,5},{8,10},{9,11},{10,... | collective-permute-start | bytes 442376 | tf_op jit(solution)/shard_map/ppermute | solution.py:619
  32.0 6.8 %collective-permute-start.2 = (bf16[2,16,2304]{2,1,0:T(8,128)(2,1)S(1)}, bf16[2,16,2304]{2,1,0:T(8,128)(2,1)S(1)}, u32[]{:S(2)}, u32[]{:S(2)}) collective-permute-start(bf16[2,16,2304]{2,1,0:T(8,128)(2,1)S(1)} %get-tuple-element.34), channel_id=1, source_target_pairs={{0,4},{1,5},{2,6},{3,7},{4,0},{5,1},{6,2},{7,3},{8,12},{9,13},{10,... | collective-permute-start | bytes 442376 | tf_op jit(solution)/shard_map/ppermute | solution.py:619
  33.0 7.8 %collective-permute-start.3 = (bf16[2,16,2304]{2,1,0:T(8,128)(2,1)S(1)}, bf16[2,16,2304]{2,1,0:T(8,128)(2,1)S(1)}, u32[]{:S(2)}, u32[]{:S(2)}) collective-permute-start(bf16[2,16,2304]{2,1,0:T(8,128)(2,1)S(1)} %get-tuple-element.35), channel_id=1, source_target_pairs={{0,8},{1,9},{2,10},{3,11},{4,12},{5,13},{6,14},{7,15},{8,0},{9,1},... | collective-permute-start | bytes 442376 | tf_op jit(solution)/shard_map/ppermute | solution.py:619
  34.0 11.4 %collective-permute-start.4 = (bf16[2,16,2304]{2,1,0:T(8,128)(2,1)S(1)}, bf16[2,16,2304]{2,1,0:T(8,128)(2,1)S(1)}, u32[]{:S(2)}, u32[]{:S(2)}) collective-permute-start(bf16[2,16,2304]{2,1,0:T(8,128)(2,1)S(1)} %get-tuple-element.36), channel_id=1, source_target_pairs={{0,14},{1,15},{2,12},{3,13},{4,10},{5,11},{6,8},{7,9},{8,6},{9,7},... | collective-permute-start | bytes 442376 | tf_op jit(solution)/shard_map/ppermute | solution.py:619
  36.5 13.3 %collective-permute-start.5 = (bf16[2,16,2304]{2,1,0:T(8,128)(2,1)S(1)}, bf16[2,16,2304]{2,1,0:T(8,128)(2,1)S(1)}, u32[]{:S(2)}, u32[]{:S(2)}) collective-permute-start(bf16[2,16,2304]{2,1,0:T(8,128)(2,1)S(1)} %get-tuple-element.37), channel_id=1, source_target_pairs={{0,6},{1,7},{2,4},{3,5},{4,2},{5,3},{6,0},{7,1},{8,14},{9,15},{10,... | collective-permute-start | bytes 442376 | tf_op jit(solution)/shard_map/ppermute | solution.py:619
  37.5 12.2 %collective-permute-start.6 = (bf16[2,16,2304]{2,1,0:T(8,128)(2,1)S(1)}, bf16[2,16,2304]{2,1,0:T(8,128)(2,1)S(1)}, u32[]{:S(2)}, u32[]{:S(2)}) collective-permute-start(bf16[2,16,2304]{2,1,0:T(8,128)(2,1)S(1)} %get-tuple-element.38), channel_id=1, source_target_pairs={{0,10},{1,11},{2,8},{3,9},{4,14},{5,15},{6,12},{7,13},{8,2},{9,3},... | collective-permute-start | bytes 442376 | tf_op jit(solution)/shard_map/ppermute | solution.py:619
  38.8 11.0 %collective-permute-start.7 = (bf16[2,16,2304]{2,1,0:T(8,128)(2,1)S(1)}, bf16[2,16,2304]{2,1,0:T(8,128)(2,1)S(1)}, u32[]{:S(2)}, u32[]{:S(2)}) collective-permute-start(bf16[2,16,2304]{2,1,0:T(8,128)(2,1)S(1)} %get-tuple-element.39), channel_id=1, source_target_pairs={{0,12},{1,13},{2,14},{3,15},{4,8},{5,9},{6,10},{7,11},{8,4},{9,5},... | collective-permute-start | bytes 442376 | tf_op jit(solution)/shard_map/ppermute | solution.py:619
  49.9 14.3 %collective-permute-start.8 = (bf16[1,16,2304]{2,1,0:T(8,128)(2,1)S(1)}, bf16[1,16,2304]{2,1,0:T(8,128)(2,1)S(1)}, u32[]{:S(2)}, u32[]{:S(2)}) collective-permute-start(bf16[1,16,2304]{2,1,0:T(8,128)(2,1)S(1)} %get-tuple-element.42), channel_id=1, source_target_pairs={{0,16},{1,17},{2,18},{3,19},{4,20},{5,21},{6,22},{7,23},{8,24},{9,... | collective-permute-start | bytes 221192 | tf_op jit(solution)/shard_map/ppermute | solution.py:619
